TPU v7x, 128 devices: a whole 4x4x4 slice. The times are simulated.
128 devices in a mesh: gx: 16 (over z_lo, x, core), gy: 8 (over z_hi, y).
Axes of the slice: x: 4, y: 4, z: 4 (z_hi: 2, z_lo: 2; z = z_hi * 2 + z_lo), core: 2. Of those that a mesh axis runs over, the one named last changes fastest.
Arguments:
- u_now: float32 [3, 12, 128, 1024], P(None, None, 'gx', 'gy'), may hold values from -6 to 6
- u_prev: float32 [3, 12, 128, 1024], P(None, None, 'gx', 'gy'), may hold values from -6 to 6
- adjoint_next: float32 [3, 12, 128, 1024], P(None, None, 'gx', 'gy'), may hold values from -6 to 6
- adjoint_later: float32 [3, 12, 128, 1024], P(None, None, 'gx', 'gy'), may hold values from -6 to 6
- density: float32 [11, 128, 1024], P(None, 'gx', 'gy'), may hold values from 0.05 to 1
- step_factor: float32 [12, 128, 1024], P(None, 'gx', 'gy'), may hold values from 0.003 to 0.01
- fixed_nodes: int32 [12, 128, 1024], P(None, 'gx', 'gy'), may hold values 0 or 1
- load_top: float32 [128, 1024], P('gx', 'gy'), may hold values from -6 to 6
- load_depth: int32 [128, 1024], P('gx', 'gy'), may hold values from 0 to 11
- brick_stiffness: float32 [24, 24], replicated, as said below
Outputs:
- adjoint_first: float32 [3, 12, 128, 1024], P(None, None, 'gx', 'gy')
- adjoint_second: float32 [3, 12, 128, 1024], P(None, None, 'gx', 'gy')
- sensitivity: float32 [11, 128, 1024], P(None, 'gx', 'gy')
Inputs may be any that keep to these rules, and one draw needn't show every extreme that they name: `fixed_nodes`: 1 marks a fixed node. `load_depth`: a node layer index. brick_stiffness is symmetric.
All inputs are finite; a program needn't handle non-finite values. No bound on the sum of `fixed_nodes` on one device may be relied on, other than what follows from the above.
Results may differ from a plain program's by a relative error of at most 0.00015.
Values sent between devices are 32-bit elements; how exact they have to be, the bound alone decides.
A program may use at most 64 MiB of HBM per device.

v0:
```python
import jax
import jax.numpy as jnp
from jax import lax
from jax.sharding import PartitionSpec as P

EMIN = 0.001
precise = lax.Precision.HIGHEST
OFFSETS = tuple(
    ((lift_z, lift_x, lift_y) for lift_z in (0, 1) for lift_x in (0, 1) for lift_y in (0, 1))
)


def from_behind(x, axis, by):
    devices = lax.axis_size(axis)
    pairs = [(i, i + by) for i in range(devices) if 0 <= i + by < devices]
    return lax.ppermute(x, axis, pairs)


def nodal_load(load_top, load_depth, layer_count):
    layers = lax.broadcasted_iota(jnp.int32, (layer_count,) + load_top.shape, 0)
    vertical = jnp.where(layers == load_depth[None], load_top[None], jnp.zeros_like(load_top)[None])
    zeros = jnp.zeros_like(vertical)
    return jnp.stack([zeros, zeros, vertical])


def corner_stack(extended):
    depth = extended.shape[1] - 1
    rows = extended.shape[2] - 1
    cols = extended.shape[3] - 1
    parts = [
        extended[
            :,
            offset[0] : offset[0] + depth,
            offset[1] : offset[1] + rows,
            offset[2] : offset[2] + cols,
        ]
        for offset in OFFSETS
    ]
    return jnp.stack(parts, axis=1).reshape(24, depth * rows * cols)


def spread(forces, factor, extended):
    depth = extended.shape[1] - 1
    rows = extended.shape[2] - 1
    cols = extended.shape[3] - 1
    scaled = forces.reshape(3, 8, depth, rows, cols) * factor[None, None]
    total = jnp.zeros(extended.shape, jnp.float32)
    for place, offset in enumerate(OFFSETS):
        total = total + jnp.pad(
            scaled[:, place],
            (
                (0, 0),
                (offset[0], 1 - offset[0]),
                (offset[1], 1 - offset[1]),
                (offset[2], 1 - offset[2]),
            ),
        )
    return total


def extend_rims(field):
    top_plane = from_behind(field[:, :, :1, :], "gx", -1)
    longer = jnp.concatenate([field, top_plane], 2)
    side_plane = from_behind(longer[:, :, :, :1], "gy", -1)
    return jnp.concatenate([longer, side_plane], 3)


def fold_rims(total):
    edge_plane = from_behind(total[:, :, :, -1:], "gy", 1)
    total = jnp.concatenate([total[:, :, :, :1] + edge_plane, total[:, :, :, 1:-1]], 3)
    row_plane = from_behind(total[:, :, -1:, :], "gx", 1)
    return jnp.concatenate([total[:, :, :1] + row_plane, total[:, :, 1:-1]], 2)


def local(
    u_now,
    u_prev,
    adjoint_next,
    adjoint_later,
    density,
    step_factor,
    fixed_nodes,
    load_top,
    load_depth,
    brick_stiffness,
):
    free = 1.0 - fixed_nodes.astype(jnp.float32)
    load = nodal_load(load_top, load_depth, u_now.shape[1])
    factor = EMIN + (1.0 - EMIN) * density**3
    fields = [u_prev, u_now]
    wides = []
    for step in range(2):
        wide = extend_rims(fields[-1])
        wides.append(wide)
        forces = jnp.dot(brick_stiffness, corner_stack(wide), precision=precise)
        pushed = fold_rims(spread(forces, factor, wide))
        fields.append(free * (2.0 * fields[-1] - fields[-2] + step_factor * (load - pushed)))
    weighted = free * step_factor * adjoint_next
    paired = extend_rims(jnp.concatenate([fields[3], weighted], 0))
    wides.append(paired[:3])
    wide_weighted = paired[3:]
    later = adjoint_later
    current = adjoint_next
    total = jnp.zeros(density.shape, jnp.float32)
    results = []
    for level in (2, 1, 0):
        if level < 2:
            wide_weighted = extend_rims(free * step_factor * current)
        forces = jnp.dot(brick_stiffness, corner_stack(wide_weighted), precision=precise)
        wide_state = wides[level]
        depth = wide_state.shape[1] - 1
        rows = wide_state.shape[2] - 1
        cols = wide_state.shape[3] - 1
        product = (forces * corner_stack(wide_state)).reshape(24, depth, rows, cols)
        total = total + jnp.sum(product, axis=0)
        pushed = fold_rims(spread(forces, factor, wide_weighted))
        newest = 2.0 * current - later + load - pushed
        later = current
        current = newest
        results.append(newest)
    sensitivity = -3.0 * (1.0 - EMIN) * density**2 * total
    return (results[2], results[1], sensitivity)


def solution(mesh):
    in_specs = (
        P(None, None, "gx", "gy"),
        P(None, None, "gx", "gy"),
        P(None, None, "gx", "gy"),
        P(None, None, "gx", "gy"),
        P(None, "gx", "gy"),
        P(None, "gx", "gy"),
        P(None, "gx", "gy"),
        P("gx", "gy"),
        P("gx", "gy"),
        P(),
    )
    out_specs = (P(None, None, "gx", "gy"), P(None, None, "gx", "gy"), P(None, "gx", "gy"))
    return jax.shard_map(local, mesh=mesh, in_specs=in_specs, out_specs=out_specs, check_vma=False)
```

profile of v0, /device:TPU:56, one launch (start us, length us, event | category | flops | bytes accessed | tf_op | source)
XLA Modules:
  0.0 211.3 jit_solution(5552144048970788760)
XLA Ops:
  1.6 3.7 %collective-permute-start = (f32[3,12,1,128]{3,2,1,0:T(1,128)S(1)}, f32[3,12,1,128]{3,2,1,0:T(1,128)S(1)}, u32[]{:S(2)}, u32[]{:S(2)}) collective-permute-start(f32[3,12,1,128]{3,2,1,0:T(1,128)S(1)} %slice.436), channel_id=1, source_target_pairs={{8,0},{16,8},{24,16},{32,24},{40,32},{48,40},{56,48},{64,56},{72,6... | collective-permute-start | bytes 55304 | tf_op jit(solution)/shard_map/ppermute | solution.py:16
  9.1 2.7 %collective-permute-start.1 = (f32[3,12,9,1]{3,2,1,0:T(8,128)S(1)}, f32[3,12,9,1]{3,2,1,0:T(8,128)S(1)}, u32[]{:S(2)}, u32[]{:S(2)}) collective-permute-start(f32[3,12,9,1]{3,2,1,0:T(8,128)S(1)} %bitcast.282), channel_id=1, source_target_pairs={{1,0},{2,1},{3,2},{4,3},{5,4},{6,5},{7,6},{9,8},{10,9},{11,10},{12... | collective-permute-start | bytes 3896 | tf_op jit(solution)/shard_map/ppermute | solution.py:16
  11.8 10.5 %collective-permute-done.1 = f32[3,12,9,1]{3,2,1,0:T(8,128)S(1)} collective-permute-done((f32[3,12,9,1]{3,2,1,0:T(8,128)S(1)}, f32[3,12,9,1]{3,2,1,0:T(8,128)S(1)}, u32[]{:S(2)}, u32[]{:S(2)}) %collective-permute-start.1) | collective-permute-done | bytes 1328 | tf_op jit(solution)/shard_map/ppermute | solution.py:16
  25.6 1.9 collective-permute-start.2
  27.7 5.7 %collective-permute-done.2 = f32[3,12,9,1]{3,1,2,0:T(8,128)S(1)} collective-permute-done((f32[3,12,9,1]{3,1,2,0:T(8,128)S(1)}, f32[3,12,9,1]{3,1,2,0:T(8,128)S(1)}, u32[]{:S(2)}, u32[]{:S(2)}) %collective-permute-start.2) | collective-permute-done | bytes 1328 | tf_op jit(solution)/shard_map/ppermute | solution.py:16
  35.6 5.2 %collective-permute-done.3 = f32[3,12,1,128]{3,1,2,0:T(8,128)S(1)} collective-permute-done((f32[3,12,1,128]{3,1,2,0:T(8,128)S(1)}, f32[3,12,1,128]{3,1,2,0:T(8,128)S(1)}, u32[]{:S(2)}, u32[]{:S(2)}) %collective-permute-start.3) | collective-permute-done | bytes 18464 | tf_op jit(solution)/shard_map/ppermute | solution.py:16
  41.0 1.9 collective-permute-start.4
  46.3 11.5 %collective-permute-done.5 = f32[3,12,9,1]{3,1,2,0:T(8,128)S(1)} collective-permute-done((f32[3,12,9,1]{3,1,2,0:T(8,128)S(1)}, f32[3,12,9,1]{3,1,2,0:T(8,128)S(1)}, u32[]{:S(2)}, u32[]{:S(2)}) %collective-permute-start.5) | collective-permute-done | bytes 1328 | tf_op jit(solution)/shard_map/ppermute | solution.py:16
  61.2 2.2 %collective-permute-start.6 = (f32[3,12,9,1]{3,1,2,0:T(8,128)S(1)}, f32[3,12,9,1]{3,1,2,0:T(8,128)S(1)}, u32[]{:S(2)}, u32[]{:S(2)}) collective-permute-start(f32[3,12,9,1]{3,1,2,0:T(8,128)S(1)} %slice.598), channel_id=1, source_target_pairs={{0,1},{1,2},{2,3},{3,4},{4,5},{5,6},{6,7},{8,9},{9,10},{10,11},{11... | collective-permute-start | bytes 3896 | tf_op jit(solution)/shard_map/ppermute | solution.py:16
  64.2 6.0 %collective-permute-done.6 = f32[3,12,9,1]{3,1,2,0:T(8,128)S(1)} collective-permute-done((f32[3,12,9,1]{3,1,2,0:T(8,128)S(1)}, f32[3,12,9,1]{3,1,2,0:T(8,128)S(1)}, u32[]{:S(2)}, u32[]{:S(2)}) %collective-permute-start.6) | collective-permute-done | bytes 1328 | tf_op jit(solution)/shard_map/ppermute | solution.py:16
  72.4 5.2 %collective-permute-done.7 = f32[3,12,1,128]{3,1,2,0:T(8,128)S(1)} collective-permute-done((f32[3,12,1,128]{3,1,2,0:T(8,128)S(1)}, f32[3,12,1,128]{3,1,2,0:T(8,128)S(1)}, u32[]{:S(2)}, u32[]{:S(2)}) %collective-permute-start.7) | collective-permute-done | bytes 18464 | tf_op jit(solution)/shard_map/ppermute | solution.py:16
  80.4 1.9 collective-permute-start.8
  83.0 4.6 %collective-permute-done.8 = f32[6,12,1,128]{1,3,2,0:T(8,128)S(1)} collective-permute-done((f32[6,12,1,128]{1,3,2,0:T(8,128)S(1)}, f32[6,12,1,128]{1,3,2,0:T(8,128)S(1)}, u32[]{:S(2)}, u32[]{:S(2)}) %collective-permute-start.8) | collective-permute-done | bytes 36896 | tf_op jit(solution)/shard_map/ppermute | solution.py:16
  87.7 2.1 collective-permute-start.9
  89.8 3.7 %fusion.7 = (f32[3,1,11,8,128]{2,4,3,0,1:T(8,128)}, f32[3,1,11,8,128]{2,4,3,0,1:T(8,128)}, f32[3,1,11,8,128]{2,4,3,0,1:T(8,128)}, f32[3,1,11,8,128]{2,4,3,0,1:T(8,128)}) fusion(f32[6,12,8,128]{1,3,2,0:T(8,128)S(1)} %copy.144, f32[6,12,1,128]{1,3,2,0:T(8,128)S(1)} %collective-permute-done.8), kind=kLoop, calls=%fused_computation.32 | loop fusion | flops 135168 | bytes 872448 | tf_op jit(solution)/shard_map/stack | solution.py:39
  93.5 2.2 %pad_maximum_fusion = f32[6,12,9,128]{1,3,2,0:T(8,128)} fusion(f32[6,12,1,128]{1,3,2,0:T(8,128)S(1)} %collective-permute-done.8, f32[6,12,8,128]{1,3,2,0:T(8,128)S(1)} %copy.144), kind=kLoop, calls=%fused_computation.5 | loop fusion | flops 82944 | bytes 663552 | tf_op jit(solution)/shard_map/concatenate | solution.py:63
  95.7 3.4 %copy.145 = f32[6,12,9,128]{3,1,2,0:T(8,128)} copy(f32[6,12,9,128]{1,3,2,0:T(8,128)} %pad_maximum_fusion) | data formatting | bytes 663552 | tf_op jit(solution)/shard_map/concatenate | solution.py:63
  111.6 7.5 %collective-permute-start.10 = (f32[3,12,9,1]{3,1,2,0:T(8,128)S(1)}, f32[3,12,9,1]{3,1,2,0:T(8,128)S(1)}, u32[]{:S(2)}, u32[]{:S(2)}) collective-permute-start(f32[3,12,9,1]{3,1,2,0:T(8,128)S(1)} %slice.625), channel_id=1, source_target_pairs={{0,1},{1,2},{2,3},{3,4},{4,5},{5,6},{6,7},{8,9},{9,10},{10,11},{11... | collective-permute-start | bytes 3896 | tf_op jit(solution)/shard_map/ppermute | solution.py:16
  120.5 2.3 %collective-permute-done.10 = f32[3,12,9,1]{3,1,2,0:T(8,128)S(1)} collective-permute-done((f32[3,12,9,1]{3,1,2,0:T(8,128)S(1)}, f32[3,12,9,1]{3,1,2,0:T(8,128)S(1)}, u32[]{:S(2)}, u32[]{:S(2)}) %collective-permute-start.10) | collective-permute-done | bytes 1328 | tf_op jit(solution)/shard_map/ppermute | solution.py:16
  122.9 2.0 collective-permute-start.11
  125.1 5.2 %collective-permute-done.11 = f32[3,12,1,128]{3,1,2,0:T(8,128)S(1)} collective-permute-done((f32[3,12,1,128]{3,1,2,0:T(8,128)S(1)}, f32[3,12,1,128]{3,1,2,0:T(8,128)S(1)}, u32[]{:S(2)}, u32[]{:S(2)}) %collective-permute-start.11) | collective-permute-done | bytes 18464 | tf_op jit(solution)/shard_map/ppermute | solution.py:16
  130.5 1.9 collective-permute-start.12
  136.4 10.9 %collective-permute-done.13 = f32[3,12,9,1]{3,1,2,0:T(8,128)S(1)} collective-permute-done((f32[3,12,9,1]{3,1,2,0:T(8,128)S(1)}, f32[3,12,9,1]{3,1,2,0:T(8,128)S(1)}, u32[]{:S(2)}, u32[]{:S(2)}) %collective-permute-start.13) | collective-permute-done | bytes 1328 | tf_op jit(solution)/shard_map/ppermute | solution.py:16
  157.4 3.6 %collective-permute-start.14 = (f32[3,12,9,1]{3,1,2,0:T(8,128)S(1)}, f32[3,12,9,1]{3,1,2,0:T(8,128)S(1)}, u32[]{:S(2)}, u32[]{:S(2)}) collective-permute-start(f32[3,12,9,1]{3,1,2,0:T(8,128)S(1)} %slice.648), channel_id=1, source_target_pairs={{0,1},{1,2},{2,3},{3,4},{4,5},{5,6},{6,7},{8,9},{9,10},{10,11},{11... | collective-permute-start | bytes 3896 | tf_op jit(solution)/shard_map/ppermute | solution.py:16
  162.0 4.0 %collective-permute-done.14 = f32[3,12,9,1]{3,1,2,0:T(8,128)S(1)} collective-permute-done((f32[3,12,9,1]{3,1,2,0:T(8,128)S(1)}, f32[3,12,9,1]{3,1,2,0:T(8,128)S(1)}, u32[]{:S(2)}, u32[]{:S(2)}) %collective-permute-start.14) | collective-permute-done | bytes 1328 | tf_op jit(solution)/shard_map/ppermute | solution.py:16
  166.1 2.1 %collective-permute-start.15 = (f32[3,12,1,128]{3,1,2,0:T(8,128)S(1)}, f32[3,12,1,128]{3,1,2,0:T(8,128)S(1)}, u32[]{:S(2)}, u32[]{:S(2)}) collective-permute-start(f32[3,12,1,128]{3,1,2,0:T(8,128)S(1)} %pad_maximum_fusion.13), channel_id=1, source_target_pairs={{0,8},{8,16},{16,24},{24,32},{32,40},{40,48},{48,56},{56,64},{64,7... | collective-permute-start | bytes 55304 | tf_op jit(solution)/shard_map/ppermute | solution.py:16
  168.4 4.9 %collective-permute-done.15 = f32[3,12,1,128]{3,1,2,0:T(8,128)S(1)} collective-permute-done((f32[3,12,1,128]{3,1,2,0:T(8,128)S(1)}, f32[3,12,1,128]{3,1,2,0:T(8,128)S(1)}, u32[]{:S(2)}, u32[]{:S(2)}) %collective-permute-start.15) | collective-permute-done | bytes 18464 | tf_op jit(solution)/shard_map/ppermute | solution.py:16
  174.2 1.9 collective-permute-start.16
  179.5 10.8 %collective-permute-done.17 = f32[3,12,9,1]{3,1,2,0:T(8,128)S(1)} collective-permute-done((f32[3,12,9,1]{3,1,2,0:T(8,128)S(1)}, f32[3,12,9,1]{3,1,2,0:T(8,128)S(1)}, u32[]{:S(2)}, u32[]{:S(2)}) %collective-permute-start.17) | collective-permute-done | bytes 1328 | tf_op jit(solution)/shard_map/ppermute | solution.py:16
  194.8 3.3 %collective-permute-start.18 = (f32[3,12,9,1]{3,1,2,0:T(8,128)S(1)}, f32[3,12,9,1]{3,1,2,0:T(8,128)S(1)}, u32[]{:S(2)}, u32[]{:S(2)}) collective-permute-start(f32[3,12,9,1]{3,1,2,0:T(8,128)S(1)} %slice.671), channel_id=1, source_target_pairs={{0,1},{1,2},{2,3},{3,4},{4,5},{5,6},{6,7},{8,9},{9,10},{10,11},{11... | collective-permute-start | bytes 3896 | tf_op jit(solution)/shard_map/ppermute | solution.py:16
  198.9 4.1 %collective-permute-done.18 = f32[3,12,9,1]{3,1,2,0:T(8,128)S(1)} collective-permute-done((f32[3,12,9,1]{3,1,2,0:T(8,128)S(1)}, f32[3,12,9,1]{3,1,2,0:T(8,128)S(1)}, u32[]{:S(2)}, u32[]{:S(2)}) %collective-permute-start.18) | collective-permute-done | bytes 1328 | tf_op jit(solution)/shard_map/ppermute | solution.py:16
  205.3 5.2 %collective-permute-done.19 = f32[3,12,1,128]{3,1,2,0:T(8,128)S(1)} collective-permute-done((f32[3,12,1,128]{3,1,2,0:T(8,128)S(1)}, f32[3,12,1,128]{3,1,2,0:T(8,128)S(1)}, u32[]{:S(2)}, u32[]{:S(2)}) %collective-permute-start.19) | collective-permute-done | bytes 18464 | tf_op jit(solution)/shard_map/ppermute | solution.py:16
  (235 shorter events, 65.2 us)
Async XLA Ops:
  0.6 22.5 %copy-start = (f32[24,24]{1,0:T(8,128)S(1)}, f32[24,24]{1,0:T(8,128)}, u32[]{:S(2)}) copy-start(f32[24,24]{1,0:T(8,128)} %param.19) | copy-start | bytes 6916
  0.6 11.1 %copy-start.29 = (f32[11,8,128]{2,1,0:T(8,128)S(1)}, f32[11,8,128]{2,1,0:T(8,128)}, u32[]{:S(2)}) copy-start(f32[11,8,128]{2,1,0:T(8,128)} %param.14) | copy-start | bytes 135172
  1.6 7.4 %collective-permute-start = (f32[3,12,1,128]{3,2,1,0:T(1,128)S(1)}, f32[3,12,1,128]{3,2,1,0:T(1,128)S(1)}, u32[]{:S(2)}, u32[]{:S(2)}) collective-permute-start(f32[3,12,1,128]{3,2,1,0:T(1,128)S(1)} %slice.436), channel_id=1, source_target_pairs={{8,0},{16,8},{24,16},{32,24},{40,32},{48,40},{56,48},{64,56},{72,6... | collective-permute-start | bytes 55304 | tf_op jit(solution)/shard_map/ppermute | solution.py:16
  8.0 14.6 %copy-start.10 = (f32[3,12,8,128]{3,2,1,0:T(8,128)S(1)}, f32[3,12,8,128]{3,2,1,0:T(8,128)}, u32[]{:S(2)}) copy-start(f32[3,12,8,128]{3,2,1,0:T(8,128)} %param.10) | copy-start | bytes 442372
  9.1 13.2 %collective-permute-start.1 = (f32[3,12,9,1]{3,2,1,0:T(8,128)S(1)}, f32[3,12,9,1]{3,2,1,0:T(8,128)S(1)}, u32[]{:S(2)}, u32[]{:S(2)}) collective-permute-start(f32[3,12,9,1]{3,2,1,0:T(8,128)S(1)} %bitcast.282), channel_id=1, source_target_pairs={{1,0},{2,1},{3,2},{4,3},{5,4},{6,5},{7,6},{9,8},{10,9},{11,10},{12... | collective-permute-start | bytes 3896 | tf_op jit(solution)/shard_map/ppermute | solution.py:16
  25.6 7.8 %collective-permute-start.2 = (f32[3,12,9,1]{3,1,2,0:T(8,128)S(1)}, f32[3,12,9,1]{3,1,2,0:T(8,128)S(1)}, u32[]{:S(2)}, u32[]{:S(2)}) collective-permute-start(f32[3,12,9,1]{3,1,2,0:T(8,128)S(1)} %slice.575), channel_id=1, source_target_pairs={{0,1},{1,2},{2,3},{3,4},{4,5},{5,6},{6,7},{8,9},{9,10},{10,11},{11... | collective-permute-start | bytes 3896 | tf_op jit(solution)/shard_map/ppermute | solution.py:16
  27.5 50.1 %copy-start.12 = (f32[1,12,8,128]{3,2,1,0:T(8,128)}, f32[1,12,8,128]{3,2,1,0:T(8,128)S(1)}, u32[]{:S(2)}) copy-start(f32[1,12,8,128]{3,2,1,0:T(8,128)S(1)} %fusion.73) | copy-start | bytes 147460
  33.4 7.5 %copy-start.28 = (f32[12,8,128]{2,1,0:T(8,128)S(1)}, f32[12,8,128]{2,1,0:T(8,128)}, u32[]{:S(2)}) copy-start(f32[12,8,128]{2,1,0:T(8,128)} %param.15) | copy-start | bytes 147460
  33.4 7.5 %copy-start.33 = (f32[3,12,8,128]{3,2,1,0:T(8,128)S(1)}, f32[3,12,8,128]{3,2,1,0:T(8,128)}, u32[]{:S(2)}) copy-start(f32[3,12,8,128]{3,2,1,0:T(8,128)} %param.11) | copy-start | bytes 442372
  33.5 7.2 %collective-permute-start.3 = (f32[3,12,1,128]{3,1,2,0:T(8,128)S(1)}, f32[3,12,1,128]{3,1,2,0:T(8,128)S(1)}, u32[]{:S(2)}, u32[]{:S(2)}) collective-permute-start(f32[3,12,1,128]{3,1,2,0:T(8,128)S(1)} %pad_maximum_fusion.16), channel_id=1, source_target_pairs={{0,8},{8,16},{16,24},{24,32},{32,40},{40,48},{48,56},{56,64},{64,7... | collective-permute-start | bytes 55304 | tf_op jit(solution)/shard_map/ppermute | solution.py:16
  41.0 3.4 %collective-permute-start.4 = (f32[3,12,1,128]{3,2,1,0:T(1,128)S(1)}, f32[3,12,1,128]{3,2,1,0:T(1,128)S(1)}, u32[]{:S(2)}, u32[]{:S(2)}) collective-permute-start(f32[3,12,1,128]{3,2,1,0:T(1,128)S(1)} %slice.578), channel_id=1, source_target_pairs={{8,0},{16,8},{24,16},{32,24},{40,32},{48,40},{56,48},{64,56},{72,6... | collective-permute-start | bytes 55304 | tf_op jit(solution)/shard_map/ppermute | solution.py:16
  44.4 13.4 %collective-permute-start.5 = (f32[3,12,9,1]{3,1,2,0:T(8,128)S(1)}, f32[3,12,9,1]{3,1,2,0:T(8,128)S(1)}, u32[]{:S(2)}, u32[]{:S(2)}) collective-permute-start(f32[3,12,9,1]{3,1,2,0:T(8,128)S(1)} %bitcast.287), channel_id=1, source_target_pairs={{1,0},{2,1},{3,2},{4,3},{5,4},{6,5},{7,6},{9,8},{10,9},{11,10},{12... | collective-permute-start | bytes 3896 | tf_op jit(solution)/shard_map/ppermute | solution.py:16
  61.2 9.0 %collective-permute-start.6 = (f32[3,12,9,1]{3,1,2,0:T(8,128)S(1)}, f32[3,12,9,1]{3,1,2,0:T(8,128)S(1)}, u32[]{:S(2)}, u32[]{:S(2)}) collective-permute-start(f32[3,12,9,1]{3,1,2,0:T(8,128)S(1)} %slice.598), channel_id=1, source_target_pairs={{0,1},{1,2},{2,3},{3,4},{4,5},{5,6},{6,7},{8,9},{9,10},{10,11},{11... | collective-permute-start | bytes 3896 | tf_op jit(solution)/shard_map/ppermute | solution.py:16
  70.3 7.2 %collective-permute-start.7 = (f32[3,12,1,128]{3,1,2,0:T(8,128)S(1)}, f32[3,12,1,128]{3,1,2,0:T(8,128)S(1)}, u32[]{:S(2)}, u32[]{:S(2)}) collective-permute-start(f32[3,12,1,128]{3,1,2,0:T(8,128)S(1)} %pad_maximum_fusion.15), channel_id=1, source_target_pairs={{0,8},{8,16},{16,24},{24,32},{32,40},{40,48},{48,56},{56,64},{64,7... | collective-permute-start | bytes 55304 | tf_op jit(solution)/shard_map/ppermute | solution.py:16
  80.4 7.2 %collective-permute-start.8 = (f32[6,12,1,128]{1,3,2,0:T(8,128)S(1)}, f32[6,12,1,128]{1,3,2,0:T(8,128)S(1)}, u32[]{:S(2)}, u32[]{:S(2)}) collective-permute-start(f32[6,12,1,128]{1,3,2,0:T(8,128)S(1)} %slice.600), channel_id=1, source_target_pairs={{8,0},{16,8},{24,16},{32,24},{40,32},{48,40},{56,48},{64,56},{72,6... | collective-permute-start | bytes 110600 | tf_op jit(solution)/shard_map/ppermute | solution.py:16
  87.7 16.5 %collective-permute-start.9 = (f32[6,12,9,1]{1,3,2,0:T(1,128)S(1)}, f32[6,12,9,1]{1,3,2,0:T(1,128)}, u32[]{:S(2)}, u32[]{:S(2)}) collective-permute-start(f32[6,12,9,1]{1,3,2,0:T(1,128)S(1)} %fusion.77), channel_id=1, source_target_pairs={{1,0},{2,1},{3,2},{4,3},{5,4},{6,5},{7,6},{9,8},{10,9},{11,10},{12... | collective-permute-start | bytes 7784 | tf_op jit(solution)/shard_map/ppermute | solution.py:16
  111.1 8.2 %copy-start.17 = (f32[3,8,11,8,128]{4,3,2,1,0:T(8,128)S(1)}, f32[3,8,11,8,128]{4,3,2,1,0:T(8,128)}, u32[]{:S(2)}) copy-start(f32[3,8,11,8,128]{4,3,2,1,0:T(8,128)} %copy-done.16) | copy-start | bytes 3244036
  111.6 11.1 %collective-permute-start.10 = (f32[3,12,9,1]{3,1,2,0:T(8,128)S(1)}, f32[3,12,9,1]{3,1,2,0:T(8,128)S(1)}, u32[]{:S(2)}, u32[]{:S(2)}) collective-permute-start(f32[3,12,9,1]{3,1,2,0:T(8,128)S(1)} %slice.625), channel_id=1, source_target_pairs={{0,1},{1,2},{2,3},{3,4},{4,5},{5,6},{6,7},{8,9},{9,10},{10,11},{11... | collective-permute-start | bytes 3896 | tf_op jit(solution)/shard_map/ppermute | solution.py:16
  122.8 7.6 %copy-start.13 = (f32[1,12,8,128]{3,2,1,0:T(8,128)S(1)}, f32[1,12,8,128]{3,2,1,0:T(8,128)}, u32[]{:S(2)}) copy-start(f32[1,12,8,128]{3,2,1,0:T(8,128)} %copy-done.12) | copy-start | bytes 147460
  122.8 7.6 %copy-start.18 = (f32[3,12,8,128]{3,2,1,0:T(8,128)S(1)}, f32[3,12,8,128]{3,2,1,0:T(8,128)}, u32[]{:S(2)}) copy-start(f32[3,12,8,128]{3,2,1,0:T(8,128)} %param.12) | copy-start | bytes 442372
  122.8 7.6 %copy-start.21 = (f32[12,8,128]{2,1,0:T(8,128)S(1)}, f32[12,8,128]{2,1,0:T(8,128)}, u32[]{:S(2)}) copy-start(f32[12,8,128]{2,1,0:T(8,128)} %copy-done.20) | copy-start | bytes 147460
  122.8 7.6 %copy-start.34 = (f32[3,12,8,128]{3,2,1,0:T(8,128)S(1)}, f32[3,12,8,128]{3,2,1,0:T(8,128)}, u32[]{:S(2)}) copy-start(f32[3,12,8,128]{3,2,1,0:T(8,128)} %param.13) | copy-start | bytes 442372
  122.9 7.4 %collective-permute-start.11 = (f32[3,12,1,128]{3,1,2,0:T(8,128)S(1)}, f32[3,12,1,128]{3,1,2,0:T(8,128)S(1)}, u32[]{:S(2)}, u32[]{:S(2)}) collective-permute-start(f32[3,12,1,128]{3,1,2,0:T(8,128)S(1)} %pad_maximum_fusion.14), channel_id=1, source_target_pairs={{0,8},{8,16},{16,24},{24,32},{32,40},{40,48},{48,56},{56,64},{64,7... | collective-permute-start | bytes 55304 | tf_op jit(solution)/shard_map/ppermute | solution.py:16
  130.5 3.4 %collective-permute-start.12 = (f32[3,12,1,128]{3,2,1,0:T(1,128)S(1)}, f32[3,12,1,128]{3,2,1,0:T(1,128)S(1)}, u32[]{:S(2)}, u32[]{:S(2)}) collective-permute-start(f32[3,12,1,128]{3,2,1,0:T(1,128)S(1)} %slice.628), channel_id=1, source_target_pairs={{8,0},{16,8},{24,16},{32,24},{40,32},{48,40},{56,48},{64,56},{72,6... | collective-permute-start | bytes 55304 | tf_op jit(solution)/shard_map/ppermute | solution.py:16
  133.9 13.5 %collective-permute-start.13 = (f32[3,12,9,1]{3,1,2,0:T(8,128)S(1)}, f32[3,12,9,1]{3,1,2,0:T(8,128)S(1)}, u32[]{:S(2)}, u32[]{:S(2)}) collective-permute-start(f32[3,12,9,1]{3,1,2,0:T(8,128)S(1)} %bitcast.288), channel_id=1, source_target_pairs={{1,0},{2,1},{3,2},{4,3},{5,4},{6,5},{7,6},{9,8},{10,9},{11,10},{12... | collective-permute-start | bytes 3896 | tf_op jit(solution)/shard_map/ppermute | solution.py:16
  157.4 8.6 %collective-permute-start.14 = (f32[3,12,9,1]{3,1,2,0:T(8,128)S(1)}, f32[3,12,9,1]{3,1,2,0:T(8,128)S(1)}, u32[]{:S(2)}, u32[]{:S(2)}) collective-permute-start(f32[3,12,9,1]{3,1,2,0:T(8,128)S(1)} %slice.648), channel_id=1, source_target_pairs={{0,1},{1,2},{2,3},{3,4},{4,5},{5,6},{6,7},{8,9},{9,10},{10,11},{11... | collective-permute-start | bytes 3896 | tf_op jit(solution)/shard_map/ppermute | solution.py:16
  166.0 7.5 %copy-start.19 = (f32[3,12,8,128]{3,2,1,0:T(8,128)S(1)}, f32[3,12,8,128]{3,2,1,0:T(8,128)}, u32[]{:S(2)}) copy-start(f32[3,12,8,128]{3,2,1,0:T(8,128)} %param.12) | copy-start | bytes 442372
  166.1 7.2 %collective-permute-start.15 = (f32[3,12,1,128]{3,1,2,0:T(8,128)S(1)}, f32[3,12,1,128]{3,1,2,0:T(8,128)S(1)}, u32[]{:S(2)}, u32[]{:S(2)}) collective-permute-start(f32[3,12,1,128]{3,1,2,0:T(8,128)S(1)} %pad_maximum_fusion.13), channel_id=1, source_target_pairs={{0,8},{8,16},{16,24},{24,32},{32,40},{40,48},{48,56},{56,64},{64,7... | collective-permute-start | bytes 55304 | tf_op jit(solution)/shard_map/ppermute | solution.py:16
  174.2 3.4 %collective-permute-start.16 = (f32[3,12,1,128]{3,2,1,0:T(1,128)S(1)}, f32[3,12,1,128]{3,2,1,0:T(1,128)S(1)}, u32[]{:S(2)}, u32[]{:S(2)}) collective-permute-start(f32[3,12,1,128]{3,2,1,0:T(1,128)S(1)} %slice.651), channel_id=1, source_target_pairs={{8,0},{16,8},{24,16},{32,24},{40,32},{48,40},{56,48},{64,56},{72,6... | collective-permute-start | bytes 55304 | tf_op jit(solution)/shard_map/ppermute | solution.py:16
  177.5 12.7 %collective-permute-start.17 = (f32[3,12,9,1]{3,1,2,0:T(8,128)S(1)}, f32[3,12,9,1]{3,1,2,0:T(8,128)S(1)}, u32[]{:S(2)}, u32[]{:S(2)}) collective-permute-start(f32[3,12,9,1]{3,1,2,0:T(8,128)S(1)} %bitcast.289), channel_id=1, source_target_pairs={{1,0},{2,1},{3,2},{4,3},{5,4},{6,5},{7,6},{9,8},{10,9},{11,10},{12... | collective-permute-start | bytes 3896 | tf_op jit(solution)/shard_map/ppermute | solution.py:16
  194.8 8.2 %collective-permute-start.18 = (f32[3,12,9,1]{3,1,2,0:T(8,128)S(1)}, f32[3,12,9,1]{3,1,2,0:T(8,128)S(1)}, u32[]{:S(2)}, u32[]{:S(2)}) collective-permute-start(f32[3,12,9,1]{3,1,2,0:T(8,128)S(1)} %slice.671), channel_id=1, source_target_pairs={{0,1},{1,2},{2,3},{3,4},{4,5},{5,6},{6,7},{8,9},{9,10},{10,11},{11... | collective-permute-start | bytes 3896 | tf_op jit(solution)/shard_map/ppermute | solution.py:16
  203.2 7.2 %collective-permute-start.19 = (f32[3,12,1,128]{3,1,2,0:T(8,128)S(1)}, f32[3,12,1,128]{3,1,2,0:T(8,128)S(1)}, u32[]{:S(2)}, u32[]{:S(2)}) collective-permute-start(f32[3,12,1,128]{3,1,2,0:T(8,128)S(1)} %pad_maximum_fusion.12), channel_id=1, source_target_pairs={{0,8},{8,16},{16,24},{24,32},{32,40},{40,48},{48,56},{56,64},{64,7... | collective-permute-start | bytes 55304 | tf_op jit(solution)/shard_map/ppermute | solution.py:16
  (25 other events, 63.8 us)
where the time goes:
time: 215 us; the launch traced here: 211 us
  waiting for transfers between devices  100 us (47%)
  starting transfers between devices  50.3 us (23%)
  local copies, waits for them, and re-layouts  31.1 us (14%)
  other arithmetic  21.6 us (10%)
  matrix products  6.04 us (3%)
    ppermute x20, waiting for transfers between devices, from_behind(): return lax.ppermute(x, axis, pairs)  100 us
    ppermute x20, starting transfers between devices, from_behind(): return lax.ppermute(x, axis, pairs)  50.3 us
    unnamed x117, local copies, waits for them, and re-layouts  13.1 us
    another operation x6, other arithmetic, corner_stack(): return jnp.stack(parts, axis=1).reshape(24, depth * rows * cols)  6.17 us
    another operation x9, local copies, waits for them, and re-layouts, corner_stack(): return jnp.stack(parts, axis=1).reshape(24, depth * rows * cols)  5.6 us
  transfers between devices with their start and end apart: 20, of which 18 were waited for; matrix products, arithmetic and copies ran while one was open for 11% of the time, Pallas kernels for 0%

commit v1 on v0

v1 whole, which is shorter than its diff:
```python
import jax
import jax.numpy as jnp
import numpy as np
from jax import lax
from jax.experimental import pallas as pl
from jax.experimental.pallas import tpu as pltpu
from jax.sharding import PartitionSpec as P

EMIN = 0.001
MESH = pl.DeviceIdType.MESH
F32 = jnp.float32
BF16 = jnp.bfloat16

ROWS = 8
TILES = 16
LEFT, RIGHT = 14, 15
U, S, A, D, B, LOAD, Q, PLANES = 0, 36, 48, 84, 96, 132, 136, 176
DEEP = 96
GROUP = 40
SLOT = 48
OUT = 8 * GROUP
DEPTH = 4 * SLOT


def band_tables():
    m = np.arange(OUT)
    group, r = m // GROUP, m % GROUP
    place, dz = group // 2, group % 2
    comp, layer = r // 12, r % 12
    element = layer - dz
    real = (r < 36) & (element >= 0) & (element <= 10)
    pick = np.zeros((OUT, 24), np.float32)
    pick[m[real], (comp * 8 + 4 * dz + place)[real]] = 1
    q = np.arange(DEPTH)
    place_in, s = q // SLOT, q % SLOT
    comp_in, layer_in = s // 12, s % 12
    spread = np.zeros((2, 24, DEPTH), np.float32)
    band = np.zeros((2, OUT, DEPTH), np.float32)
    for up in (0, 1):
        ok = s < 36
        spread[up, (comp_in * 8 + 4 * up + place_in)[ok], q[ok]] = 1
        band[up] = layer_in[None, :] == (element + up)[:, None]
    return pick, spread, band


def exchange_kernel(u, b, a, q, den, step, fix, top, depth, stiff, pick, spread, band, e, w, packed, from_left, from_right, send_sem, recv_sem):
    gx, gy = lax.axis_index("gx"), lax.axis_index("gy")
    nx, ny = lax.axis_size("gx"), lax.axis_size("gy")
    has = {"down": gx > 0, "up": gx < nx - 1, "left": gy > 0, "right": gy < ny - 1}
    where = {"down": (gx - 1, gy), "up": (gx + 1, gy), "left": (gx, gy - 1), "right": (gx, gy + 1)}
    barrier = pltpu.get_barrier_semaphore()
    for side in where:
        @pl.when(has[side])
        def _(side=side):
            pl.semaphore_signal(barrier, inc=1, device_id=where[side], device_id_type=MESH)

    e[LEFT] = jnp.zeros((PLANES, 128), F32)
    e[RIGHT] = jnp.zeros((PLANES, 128), F32)
    for r in range(ROWS):
        t = r + 3
        free = 1.0 - fix[pl.ds(r, 12, stride=8), :].astype(F32)
        e[t, U:U + 36] = u[pl.ds(r, 36, stride=8), :]
        e[t, S:S + 12] = free * step[pl.ds(r, 12, stride=8), :]
        e[t, A:A + 36] = a[pl.ds(r, 36, stride=8), :]
        e[t, D:D + 11] = den[pl.ds(r, 11, stride=8), :]
        e[t, D + 11:D + 12] = jnp.zeros((1, 128), F32)
        e[t, B:B + 36] = b[pl.ds(r, 36, stride=8), :]
        e[t, LOAD:LOAD + 1] = top[r:r + 1, :]
        e[t, LOAD + 1:LOAD + 2] = depth[r:r + 1, :].astype(F32)
        e[t, LOAD + 2:LOAD + 4] = jnp.zeros((2, 128), F32)
        e[t, Q:Q + 36] = q[pl.ds(r, 36, stride=8), :]
        e[t, Q + 36:Q + 40] = jnp.zeros((4, 128), F32)
    for t in (0, 13):
        e[t, DEEP:PLANES] = jnp.zeros((PLANES - DEEP, 128), F32)

    @pl.when(gx == 0)
    def _():
        for t in (0, 1, 2):
            e[t] = jnp.zeros((PLANES, 128), F32)

    @pl.when(gx == nx - 1)
    def _():
        for t in (11, 12, 13):
            e[t] = jnp.zeros((PLANES, 128), F32)

    count = sum(has[side].astype(jnp.int32) for side in where)
    pl.semaphore_wait(barrier, count)

    def remote(src, dst, k, side):
        return pltpu.make_async_remote_copy(
            src_ref=src, dst_ref=dst, send_sem=send_sem.at[k], recv_sem=recv_sem.at[k],
            device_id=where[side], device_id_type=MESH,
        )

    down = [
        remote(e.at[3:6, 0:DEEP], e.at[11:14, 0:DEEP], 0, "down"),
        remote(e.at[3:5, DEEP:PLANES], e.at[11:13, DEEP:PLANES], 1, "down"),
    ]
    up = [
        remote(e.at[8:11, 0:DEEP], e.at[0:3, 0:DEEP], 2, "up"),
        remote(e.at[9:11, DEEP:PLANES], e.at[1:3, DEEP:PLANES], 3, "up"),
    ]

    @pl.when(has["down"])
    def _():
        for c in down:
            c.start()

    @pl.when(has["up"])
    def _():
        for c in up:
            c.start()

    lane = lax.broadcasted_iota(jnp.int32, (PLANES, 128), 1)
    row_of = ((lane + 1) & 127) >> 3
    column = ((lane + 1) & 7) - 1

    def pack(tiles):
        total = packed[...]
        for t in tiles:
            total = jnp.where(row_of == t, pltpu.roll(e[t], 8 * t + 3, 1), total)
        packed[...] = total

    packed[...] = jnp.zeros((PLANES, 128), F32)
    pack(range(3, 11))

    low = stiff[...] - stiff[...].astype(BF16).astype(F32)
    for part, value in enumerate((stiff[...].astype(BF16), low.astype(BF16))):
        rows = jnp.dot(pick[...], value, preferred_element_type=F32).astype(BF16)
        full = jnp.zeros((OUT, DEPTH), F32)
        for dz in (0, 1):
            full = full + band[dz].astype(F32) * jnp.dot(rows, spread[dz], preferred_element_type=F32)
        w[part] = full.astype(BF16)

    @pl.when(has["down"])
    def _():
        for c in up:
            c.wait_recv()

    @pl.when(has["up"])
    def _():
        for c in down:
            c.wait_recv()

    pack((0, 1, 2, 11, 12, 13))
    to_left = remote(packed, from_right, 4, "left")
    to_right = remote(packed, from_left, 5, "right")

    @pl.when(has["left"])
    def _():
        to_left.start()

    @pl.when(has["right"])
    def _():
        to_right.start()

    e[LEFT] = jnp.where(column >= 3, packed[...], 0.0)
    e[RIGHT] = jnp.where(column <= 2, packed[...], 0.0)

    @pl.when(has["left"])
    def _():
        to_right.wait_recv()
        e[LEFT] = jnp.where(column <= 2, from_left[...], e[LEFT])

    @pl.when(has["right"])
    def _():
        to_left.wait_recv()
        e[RIGHT] = jnp.where(column >= 3, from_right[...], e[RIGHT])

    @pl.when(has["down"])
    def _():
        for c in down:
            c.wait_send()

    @pl.when(has["up"])
    def _():
        for c in up:
            c.wait_send()

    @pl.when(has["left"])
    def _():
        to_left.wait_send()

    @pl.when(has["right"])
    def _():
        to_right.wait_send()


def plate_kernel(e, w, first, second, sens, fac, fup, srep, load, u1, u2, a2, a1, z, xh, xl, xsh, xsl, acc0, acc1):
    lane = lax.broadcasted_iota(jnp.int32, (GROUP, 128), 1)
    layer = lax.broadcasted_iota(jnp.int32, (12, 128), 0).astype(F32)
    edge = (lane == 0) | (lane == 127)
    from_left = ((lane + 1) & 7) >= 4
    wl = jnp.zeros((8, 128), F32)

    def halves(v):
        v = jnp.concatenate([v, wl], 0)
        high = v.astype(BF16)
        return high, (v - high.astype(F32)).astype(BF16)

    def put(t, v):
        high, low = halves(v)
        xh[t, 0:SLOT] = high
        xl[t, 0:SLOT] = low
        high, low = halves(pltpu.roll(v, 127, 1))
        xh[t, SLOT:2 * SLOT] = high
        xl[t, SLOT:2 * SLOT] = low

    def put_seam(side, v):
        cols = slice(128 * side, 128 * side + 128)
        for k, by in enumerate((0, 127, 120, 119)):
            high, low = halves(pltpu.roll(v, by, 1) if by else v)
            xsh[SLOT * k:SLOT * (k + 1), cols] = high
            xsl[SLOT * k:SLOT * (k + 1), cols] = low

    def field(t, at):
        rows = lax.broadcasted_iota(jnp.int32, (GROUP, 128), 0)
        return jnp.where(rows < 36, e[t, at:at + GROUP], 0.0)

    zeros = jnp.zeros((GROUP, 128), F32)

    def prepare(t, _):
        d = e[t, D:D + 12]
        f = jnp.where(d > 0.0, EMIN + (1.0 - EMIN) * (d * d * d), 0.0)
        s = e[t, S:S + 12]
        fac[t] = zeros
        fup[t] = zeros
        srep[t] = zeros
        load[t] = zeros
        for c in (0, 12, 24):
            fac[t, c:c + 12] = f
            fup[t, c + 1:c + 12] = f[0:11]
            srep[t, c:c + 12] = s
        load[t, 24:36] = jnp.where(e[t, LOAD + 1:LOAD + 2] == layer, e[t, LOAD:LOAD + 1], 0.0)
        acc0[t] = zeros
        acc1[t] = zeros
        put(t, field(t, U))
        return 0

    lax.fori_loop(0, TILES, prepare, 0)
    for side in (0, 1):
        put_seam(side, field(LEFT + side, U))

    def forces(high, low):
        return (
            jnp.dot(w[0], high, preferred_element_type=F32)
            + jnp.dot(w[1], high, preferred_element_type=F32)
            + jnp.dot(w[0], low, preferred_element_type=F32)
        )

    def weigh(t, f):
        return [
            fac[t] * f[(2 * k) * GROUP:(2 * k + 1) * GROUP] + fup[t] * f[(2 * k + 1) * GROUP:(2 * k + 2) * GROUP]
            for k in range(4)
        ]

    def collect(t, f, corners):
        for dz, acc in ((0, acc0), (1, acc1)):
            total = acc[t]
            for k in range(4):
                total = total + f[(2 * k + dz) * GROUP:(2 * k + dz + 1) * GROUP] * corners[k]
            acc[t] = total

    def stiffness_map(start, pairs, finish, seam_finish, state=None):
        f = forces(xsh[...], xsl[...])
        seams = []
        for side in (0, 1):
            t = LEFT + side
            part = f[:, 128 * side:128 * side + 128]
            if state is not None and side == 1:
                v = state(t)
                collect(t, part, [pltpu.roll(v, by, 1) if by else v for by in (0, 127, 120, 119)])
            g = weigh(t, part)
            seams.append(g[0] + pltpu.roll(g[1], 1, 1) + pltpu.roll(g[2], 8, 1) + pltpu.roll(g[3], 9, 1))
        both = jnp.where(from_left, seams[0], seams[1])

        def step(i, carry):
            t0 = start + 2 * i
            tiles = [xh[t0 + k] for k in range(3)]
            lows = [xl[t0 + k] for k in range(3)]
            high = jnp.concatenate([jnp.concatenate(tiles[0:2], 0), jnp.concatenate(tiles[1:3], 0)], 1)
            low = jnp.concatenate([jnp.concatenate(lows[0:2], 0), jnp.concatenate(lows[1:3], 0)], 1)
            f = forces(high, low)
            if state is not None:
                @pl.when((t0 >= 2) & (t0 <= 10))
                def _():
                    for k in (0, 1):
                        here, there = state(t0 + k), state(t0 + k + 1)
                        collect(t0 + k, f[:, 128 * k:128 * k + 128], [here, pltpu.roll(here, 127, 1), there, pltpu.roll(there, 127, 1)])
            below, below_rolled = carry
            for k in (0, 1):
                t = t0 + k
                g = weigh(t, f[:, 128 * k:128 * k + 128])
                out = g[0] + below + pltpu.roll(g[1] + below_rolled, 1, 1)
                out = jnp.where(edge, pltpu.roll(both, 125 - 8 * t, 1), out)
                finish(t, out)
                below, below_rolled = g[2], g[3]
            return below, below_rolled

        lax.fori_loop(0, pairs, step, (zeros, zeros))
        for side in (0, 1):
            seam_finish(side, seams[side])

    def displacement(now, before, target, follow):
        def value(t, out):
            s = srep[t]
            return jnp.where(s > 0.0, 2.0 * now(t) - before(t) + s * (load[t] - out), 0.0)

        def finish(t, out):
            v = value(t, out)
            target[t] = v
            if follow:
                put(t, v)

        def seam_finish(side, out):
            v = value(LEFT + side, out)
            target[LEFT + side] = v
            if follow:
                put_seam(side, v)

        return finish, seam_finish

    def adjoint(now, before, target, result):
        def value(t, out):
            return 2.0 * now(t) - before(t) + load[t] - out

        def finish(t, out):
            v = value(t, out)
            if target is not None:
                target[t] = v
                put(t, srep[t] * v)
            if result is not None:
                @pl.when((t >= 3) & (t <= 10))
                def _():
                    result[pl.ds(t - 3, 36, stride=8), :] = v[0:36]

        def seam_finish(side, out):
            if target is not None:
                v = value(LEFT + side, out)
                target[LEFT + side] = v
                put_seam(side, srep[LEFT + side] * v)

        return finish, seam_finish

    u_now = lambda t: field(t, U)
    u_before = lambda t: field(t, B)
    adj_next = lambda t: field(t, A)
    adj_later = lambda t: field(t, Q)
    of = lambda ref: (lambda t: ref[t])

    stiffness_map(1, 6, *displacement(u_now, u_before, u1, True))
    stiffness_map(2, 5, *displacement(of(u1), u_now, u2, False))

    def weighted(t, _):
        put(t, srep[t] * adj_next(t))
        return 0

    lax.fori_loop(0, TILES, weighted, 0)
    for side in (0, 1):
        put_seam(side, srep[LEFT + side] * adj_next(LEFT + side))

    stiffness_map(0, 7, *adjoint(adj_next, adj_later, a2, None), of(u2))
    stiffness_map(1, 6, *adjoint(of(a2), adj_next, a1, second), of(u1))
    stiffness_map(2, 5, *adjoint(of(a1), of(a2), None, first), u_now)

    def total(t):
        p, r = acc0[t], acc1[t]
        return p[0:11] + p[12:23] + p[24:35] + r[1:12] + r[13:24] + r[25:36]

    seam = total(RIGHT)
    last = lax.broadcasted_iota(jnp.int32, (11, 128), 1) == 127
    for r in range(ROWS):
        t = r + 3
        d = e[t, D:D + 11]
        both = jnp.where(last, pltpu.roll(seam, 125 - 8 * t, 1), total(t))
        sens[pl.ds(r, 11, stride=8), :] = (-3.0 * (1.0 - EMIN)) * (d * d) * both


def local(u_now, u_prev, adjoint_next, adjoint_later, density, step_factor, fixed_nodes, load_top, load_depth, brick_stiffness):
    pick, spread, band = (jnp.asarray(x, BF16) for x in band_tables())
    vmem = pl.BlockSpec(memory_space=pltpu.VMEM)
    flat = lambda x: x.reshape(-1, 128)
    e, w = pl.pallas_call(
        exchange_kernel,
        out_shape=(
            jax.ShapeDtypeStruct((TILES, PLANES, 128), F32),
            jax.ShapeDtypeStruct((2, OUT, DEPTH), BF16),
        ),
        in_specs=[vmem] * 13,
        out_specs=(vmem, vmem),
        scratch_shapes=[
            pltpu.VMEM((PLANES, 128), F32),
            pltpu.VMEM((PLANES, 128), F32),
            pltpu.VMEM((PLANES, 128), F32),
            pltpu.SemaphoreType.DMA((6,)),
            pltpu.SemaphoreType.DMA((6,)),
        ],
        compiler_params=pltpu.CompilerParams(collective_id=0, has_side_effects=True, vmem_limit_bytes=24 * 2**20),
        name="exchange",
    )(
        flat(u_now), flat(u_prev), flat(adjoint_next), flat(adjoint_later), flat(density), flat(step_factor),
        flat(fixed_nodes), load_top, load_depth, brick_stiffness, pick, spread, band,
    )
    tile = pltpu.VMEM((TILES, GROUP, 128), F32)
    first, second, sens = pl.pallas_call(
        plate_kernel,
        out_shape=(
            jax.ShapeDtypeStruct((36 * ROWS, 128), F32),
            jax.ShapeDtypeStruct((36 * ROWS, 128), F32),
            jax.ShapeDtypeStruct((11 * ROWS, 128), F32),
        ),
        in_specs=[vmem] * 2,
        out_specs=(vmem,) * 3,
        scratch_shapes=[tile] * 9 + [
            pltpu.VMEM((TILES, 2 * SLOT, 128), BF16),
            pltpu.VMEM((TILES, 2 * SLOT, 128), BF16),
            pltpu.VMEM((DEPTH, 256), BF16),
            pltpu.VMEM((DEPTH, 256), BF16),
            tile, tile,
        ],
        compiler_params=pltpu.CompilerParams(vmem_limit_bytes=40 * 2**20),
        name="plate",
    )(e, w)
    return (
        first.reshape(u_now.shape),
        second.reshape(u_now.shape),
        sens.reshape(density.shape),
    )


def solution(mesh):
    in_specs = (
        P(None, None, "gx", "gy"),
        P(None, None, "gx", "gy"),
        P(None, None, "gx", "gy"),
        P(None, None, "gx", "gy"),
        P(None, "gx", "gy"),
        P(None, "gx", "gy"),
        P(None, "gx", "gy"),
        P("gx", "gy"),
        P("gx", "gy"),
        P(),
    )
    out_specs = (P(None, None, "gx", "gy"), P(None, None, "gx", "gy"), P(None, "gx", "gy"))
    return jax.shard_map(local, mesh=mesh, in_specs=in_specs, out_specs=out_specs, check_vma=False)
```

time: 215 us -> 46.7 us (0.22)
  the two profiles are of different devices: /device:TPU:56 before, /device:TPU:96 now
where the time goes in v1:
time: 46.7 us; the launch traced here: 46.1 us
  Pallas kernels  34.7 us (74%)
  local copies, waits for them, and re-layouts  10.7 us (23%)
  between operations  0.66 us (1%)
    pallas_call x1, Pallas kernels, local(): pl.pallas_call(plate_kernel, out_shape=(jax.ShapeDtypeStruct((36 * ROWS,...  20.2 us
    pallas_call x1, Pallas kernels, local(): pl.pallas_call(exchange_kernel, out_shape=(jax.ShapeDtypeStruct((TILES, P...  14.6 us
    unnamed x26, local copies, waits for them, and re-layouts  10.7 us

profile of v1, /device:TPU:96, one launch (start us, length us, event | category | flops | bytes accessed | tf_op | source)
XLA Modules:
  0.0 46.1 jit_solution(14335179432664108409)
XLA Ops:
  0.6 0.0 copy-start
  0.6 1.0 %copy-done = bf16[2,320,192]{2,1,0:T(8,128)(2,1)S(1)} copy-done((bf16[2,320,192]{2,1,0:T(8,128)(2,1)S(1)}, bf16[2,320,192]{2,1,0:T(8,128)(2,1)}, u32[]{:S(2)}) %copy-start) | copy-done | bytes 245784
  1.6 0.0 copy-start.1
  1.6 0.9 %copy-done.1 = f32[3,12,8,128]{3,2,1,0:T(8,128)S(1)} copy-done((f32[3,12,8,128]{3,2,1,0:T(8,128)S(1)}, f32[3,12,8,128]{3,2,1,0:T(8,128)}, u32[]{:S(2)}) %copy-start.1) | copy-done | bytes 147480
  2.5 0.0 copy-start.2
  2.5 0.9 %copy-done.2 = f32[3,12,8,128]{3,2,1,0:T(8,128)S(1)} copy-done((f32[3,12,8,128]{3,2,1,0:T(8,128)S(1)}, f32[3,12,8,128]{3,2,1,0:T(8,128)}, u32[]{:S(2)}) %copy-start.2) | copy-done | bytes 147480
  3.4 0.0 copy-start.3
  3.4 0.9 %copy-done.3 = f32[3,12,8,128]{3,2,1,0:T(8,128)S(1)} copy-done((f32[3,12,8,128]{3,2,1,0:T(8,128)S(1)}, f32[3,12,8,128]{3,2,1,0:T(8,128)}, u32[]{:S(2)}) %copy-start.3) | copy-done | bytes 147480
  4.3 0.0 copy-start.4
  4.3 0.9 %copy-done.4 = f32[3,12,8,128]{3,2,1,0:T(8,128)S(1)} copy-done((f32[3,12,8,128]{3,2,1,0:T(8,128)S(1)}, f32[3,12,8,128]{3,2,1,0:T(8,128)}, u32[]{:S(2)}) %copy-start.4) | copy-done | bytes 147480
  5.3 0.0 copy-start.5
  5.3 0.9 %copy-done.5 = bf16[320,24]{1,0:T(8,128)(2,1)S(1)} copy-done((bf16[320,24]{1,0:T(8,128)(2,1)S(1)}, bf16[320,24]{1,0:T(8,128)(2,1)}, u32[]{:S(2)}) %copy-start.5) | copy-done | bytes 15384
  6.1 0.0 copy-start.6
  6.1 0.8 %copy-done.6 = f32[12,8,128]{2,1,0:T(8,128)S(1)} copy-done((f32[12,8,128]{2,1,0:T(8,128)S(1)}, f32[12,8,128]{2,1,0:T(8,128)}, u32[]{:S(2)}) %copy-start.6) | copy-done | bytes 49176
  6.9 0.0 copy-start.7
  6.9 0.8 %copy-done.7 = s32[12,8,128]{2,1,0:T(8,128)S(1)} copy-done((s32[12,8,128]{2,1,0:T(8,128)S(1)}, s32[12,8,128]{2,1,0:T(8,128)}, u32[]{:S(2)}) %copy-start.7) | copy-done | bytes 49176
  7.7 0.0 copy-start.8
  7.7 0.8 %copy-done.8 = f32[11,8,128]{2,1,0:T(8,128)S(1)} copy-done((f32[11,8,128]{2,1,0:T(8,128)S(1)}, f32[11,8,128]{2,1,0:T(8,128)}, u32[]{:S(2)}) %copy-start.8) | copy-done | bytes 45080
  8.5 0.0 copy-start.9
  8.5 0.7 %copy-done.9 = bf16[2,24,192]{2,1,0:T(8,128)(2,1)S(1)} copy-done((bf16[2,24,192]{2,1,0:T(8,128)(2,1)S(1)}, bf16[2,24,192]{2,1,0:T(8,128)(2,1)}, u32[]{:S(2)}) %copy-start.9) | copy-done | bytes 18456
  9.3 0.0 copy-start.10
  9.3 0.7 %copy-done.10 = f32[24,24]{1,0:T(8,128)S(1)} copy-done((f32[24,24]{1,0:T(8,128)S(1)}, f32[24,24]{1,0:T(8,128)}, u32[]{:S(2)}) %copy-start.10) | copy-done | bytes 2328
  10.0 0.0 copy-start.11
  10.0 0.7 %copy-done.11 = f32[8,128]{1,0:T(8,128)S(1)} copy-done((f32[8,128]{1,0:T(8,128)S(1)}, f32[8,128]{1,0:T(8,128)}, u32[]{:S(2)}) %copy-start.11) | copy-done | bytes 4120
  10.7 0.0 copy-start.12
  10.7 0.7 %copy-done.12 = s32[8,128]{1,0:T(8,128)S(1)} copy-done((s32[8,128]{1,0:T(8,128)S(1)}, s32[8,128]{1,0:T(8,128)}, u32[]{:S(2)}) %copy-start.12) | copy-done | bytes 4120
  11.3 14.6 %exchange.1 = (f32[16,176,128]{2,1,0:T(8,128)S(1)}, bf16[2,320,192]{2,1,0:T(8,128)(2,1)S(1)}) custom-call(f32[288,128]{1,0:T(8,128)S(1)} %bitcast.10, f32[288,128]{1,0:T(8,128)S(1)} %bitcast.11, f32[288,128]{1,0:T(8,128)S(1)} %bitcast.12, f32[288,128]{1,0:T(8,128)S(1)} %bitcast.13, f32[88,128]{1,0:T(8,128)S(1)} %bitcast.16, f32[96,128]{1,0:T(8,128)S(1)} %bitcast.14, ...), custom_call_target="tpu_custom_call" | custom-call | tf_op jit(solution)/shard_map/exchange/pallas_call | solution.py:383
  25.9 20.2 %plate.1 = (f32[288,128]{1,0:T(8,128)}, f32[288,128]{1,0:T(8,128)}, f32[88,128]{1,0:T(8,128)}) custom-call(f32[16,176,128]{2,1,0:T(8,128)S(1)} %get-tuple-element.8.e, bf16[2,320,192]{2,1,0:T(8,128)(2,1)S(1)} %get-tuple-element.9.w), custom_call_target="tpu_custom_call" | custom-call | tf_op jit(solution)/shard_map/plate/pallas_call | solution.py:405
Async XLA Ops:
  0.6 1.0 %copy-start = (bf16[2,320,192]{2,1,0:T(8,128)(2,1)S(1)}, bf16[2,320,192]{2,1,0:T(8,128)(2,1)}, u32[]{:S(2)}) copy-start(bf16[2,320,192]{2,1,0:T(8,128)(2,1)} %constant.8.clone.band) | copy-start | bytes 737284
  1.6 0.9 %copy-start.1 = (f32[3,12,8,128]{3,2,1,0:T(8,128)S(1)}, f32[3,12,8,128]{3,2,1,0:T(8,128)}, u32[]{:S(2)}) copy-start(f32[3,12,8,128]{3,2,1,0:T(8,128)} %param.13) | copy-start | bytes 442372
  2.5 0.9 %copy-start.2 = (f32[3,12,8,128]{3,2,1,0:T(8,128)S(1)}, f32[3,12,8,128]{3,2,1,0:T(8,128)}, u32[]{:S(2)}) copy-start(f32[3,12,8,128]{3,2,1,0:T(8,128)} %param.14) | copy-start | bytes 442372
  3.4 0.9 %copy-start.3 = (f32[3,12,8,128]{3,2,1,0:T(8,128)S(1)}, f32[3,12,8,128]{3,2,1,0:T(8,128)}, u32[]{:S(2)}) copy-start(f32[3,12,8,128]{3,2,1,0:T(8,128)} %param.15) | copy-start | bytes 442372
  4.3 0.9 %copy-start.4 = (f32[3,12,8,128]{3,2,1,0:T(8,128)S(1)}, f32[3,12,8,128]{3,2,1,0:T(8,128)}, u32[]{:S(2)}) copy-start(f32[3,12,8,128]{3,2,1,0:T(8,128)} %param.16) | copy-start | bytes 442372
  5.3 0.9 %copy-start.5 = (bf16[320,24]{1,0:T(8,128)(2,1)S(1)}, bf16[320,24]{1,0:T(8,128)(2,1)}, u32[]{:S(2)}) copy-start(bf16[320,24]{1,0:T(8,128)(2,1)} %constant.6.clone.pick) | copy-start | bytes 46084
  6.1 0.8 %copy-start.6 = (f32[12,8,128]{2,1,0:T(8,128)S(1)}, f32[12,8,128]{2,1,0:T(8,128)}, u32[]{:S(2)}) copy-start(f32[12,8,128]{2,1,0:T(8,128)} %param.18) | copy-start | bytes 147460
  6.9 0.8 %copy-start.7 = (s32[12,8,128]{2,1,0:T(8,128)S(1)}, s32[12,8,128]{2,1,0:T(8,128)}, u32[]{:S(2)}) copy-start(s32[12,8,128]{2,1,0:T(8,128)} %param.19) | copy-start | bytes 147460
  7.7 0.8 %copy-start.8 = (f32[11,8,128]{2,1,0:T(8,128)S(1)}, f32[11,8,128]{2,1,0:T(8,128)}, u32[]{:S(2)}) copy-start(f32[11,8,128]{2,1,0:T(8,128)} %param.17) | copy-start | bytes 135172
  8.5 0.7 %copy-start.9 = (bf16[2,24,192]{2,1,0:T(8,128)(2,1)S(1)}, bf16[2,24,192]{2,1,0:T(8,128)(2,1)}, u32[]{:S(2)}) copy-start(bf16[2,24,192]{2,1,0:T(8,128)(2,1)} %constant.7.clone.spread) | copy-start | bytes 55300
  9.3 0.7 %copy-start.10 = (f32[24,24]{1,0:T(8,128)S(1)}, f32[24,24]{1,0:T(8,128)}, u32[]{:S(2)}) copy-start(f32[24,24]{1,0:T(8,128)} %stiff.1) | copy-start | bytes 6916
  10.0 0.7 %copy-start.11 = (f32[8,128]{1,0:T(8,128)S(1)}, f32[8,128]{1,0:T(8,128)}, u32[]{:S(2)}) copy-start(f32[8,128]{1,0:T(8,128)} %top.1) | copy-start | bytes 12292
  10.7 0.7 %copy-start.12 = (s32[8,128]{1,0:T(8,128)S(1)}, s32[8,128]{1,0:T(8,128)}, u32[]{:S(2)}) copy-start(s32[8,128]{1,0:T(8,128)} %depth.1) | copy-start | bytes 12292

commit v2 on v1

--- a/solution.py
+++ b/solution.py
@@ -1,6 +1,5 @@
 import jax
 import jax.numpy as jnp
-import numpy as np
 from jax import lax
 from jax.experimental import pallas as pl
 from jax.experimental.pallas import tpu as pltpu
@@ -22,28 +21,47 @@
 DEPTH = 4 * SLOT
 
 
-def band_tables():
-    m = np.arange(OUT)
-    group, r = m // GROUP, m % GROUP
-    place, dz = group // 2, group % 2
-    comp, layer = r // 12, r % 12
+def banded_weights(stiff, w):
+    def split(place):
+        comp = (place >= 12).astype(jnp.int32) + (place >= 24).astype(jnp.int32)
+        return comp, place - 12 * comp
+
+    iota = lambda shape, d: lax.broadcasted_iota(jnp.int32, shape, d)
+    group, r = iota((8, GROUP, 24), 0), iota((8, GROUP, 24), 1)
+    dz = group & 1
+    comp, layer = split(r)
     element = layer - dz
     real = (r < 36) & (element >= 0) & (element <= 10)
-    pick = np.zeros((OUT, 24), np.float32)
-    pick[m[real], (comp * 8 + 4 * dz + place)[real]] = 1
-    q = np.arange(DEPTH)
-    place_in, s = q // SLOT, q % SLOT
-    comp_in, layer_in = s // 12, s % 12
-    spread = np.zeros((2, 24, DEPTH), np.float32)
-    band = np.zeros((2, OUT, DEPTH), np.float32)
-    for up in (0, 1):
-        ok = s < 36
-        spread[up, (comp_in * 8 + 4 * up + place_in)[ok], q[ok]] = 1
-        band[up] = layer_in[None, :] == (element + up)[:, None]
-    return pick, spread, band
-
-
-def exchange_kernel(u, b, a, q, den, step, fix, top, depth, stiff, pick, spread, band, e, w, packed, from_left, from_right, send_sem, recv_sem):
+    pick = jnp.where(real & (iota((8, GROUP, 24), 2) == comp * 8 + 4 * dz + (group >> 1)), 1.0, 0.0)
+    pick = pick.reshape(OUT, 24).astype(BF16)
+
+    def columns(shape):
+        q = iota(shape, len(shape) - 1)
+        place = sum((q >= SLOT * k).astype(jnp.int32) for k in (1, 2, 3))
+        s = q - SLOT * place
+        return (place, s) + split(s)
+
+    place, s, comp, _ = columns((24, DEPTH))
+    spread = [
+        jnp.where((s < 36) & (iota((24, DEPTH), 0) == comp * 8 + 4 * up + place), 1.0, 0.0).astype(BF16)
+        for up in (0, 1)
+    ]
+    group, r = iota((8, GROUP, DEPTH), 0), iota((8, GROUP, DEPTH), 1)
+    offset = columns((8, GROUP, DEPTH))[3] - split(r)[1] + (group & 1)
+    offset = offset.reshape(OUT, DEPTH)
+    low = stiff - stiff.astype(BF16).astype(F32)
+    for part, value in enumerate((stiff.astype(BF16), low.astype(BF16))):
+        rows = jnp.dot(pick, value, preferred_element_type=F32).astype(BF16)
+        full = jnp.zeros((OUT, DEPTH), F32)
+        for up in (0, 1):
+            full = jnp.where(offset == up, jnp.dot(rows, spread[up], preferred_element_type=F32), full)
+        w[part] = full.astype(BF16)
+
+
+def exchange_kernel(*refs):
+    sources, (e, w), held, rest = refs[:10], refs[10:12], refs[12:22], refs[22:]
+    u, b, a, q, den, step, fix, top, depth, stiff = held
+    packed, from_left, from_right, load_sem, send_sem, recv_sem = rest
     gx, gy = lax.axis_index("gx"), lax.axis_index("gy")
     nx, ny = lax.axis_size("gx"), lax.axis_size("gy")
     has = {"down": gx > 0, "up": gx < nx - 1, "left": gy > 0, "right": gy < ny - 1}
@@ -54,8 +72,11 @@
         def _(side=side):
             pl.semaphore_signal(barrier, inc=1, device_id=where[side], device_id_type=MESH)
 
-    e[LEFT] = jnp.zeros((PLANES, 128), F32)
-    e[RIGHT] = jnp.zeros((PLANES, 128), F32)
+    loads = [pltpu.make_async_copy(src, dst, load_sem.at[k]) for k, (src, dst) in enumerate(zip(sources, held))]
+    for c in loads:
+        c.start()
+    for c in loads:
+        c.wait()
     for r in range(ROWS):
         t = r + 3
         free = 1.0 - fix[pl.ds(r, 12, stride=8), :].astype(F32)
@@ -124,13 +145,7 @@
     packed[...] = jnp.zeros((PLANES, 128), F32)
     pack(range(3, 11))
 
-    low = stiff[...] - stiff[...].astype(BF16).astype(F32)
-    for part, value in enumerate((stiff[...].astype(BF16), low.astype(BF16))):
-        rows = jnp.dot(pick[...], value, preferred_element_type=F32).astype(BF16)
-        full = jnp.zeros((OUT, DEPTH), F32)
-        for dz in (0, 1):
-            full = full + band[dz].astype(F32) * jnp.dot(rows, spread[dz], preferred_element_type=F32)
-        w[part] = full.astype(BF16)
+    banded_weights(stiff[...], w)
 
     @pl.when(has["down"])
     def _():
@@ -377,30 +392,31 @@
 
 
 def local(u_now, u_prev, adjoint_next, adjoint_later, density, step_factor, fixed_nodes, load_top, load_depth, brick_stiffness):
-    pick, spread, band = (jnp.asarray(x, BF16) for x in band_tables())
     vmem = pl.BlockSpec(memory_space=pltpu.VMEM)
     flat = lambda x: x.reshape(-1, 128)
+    sources = (
+        flat(u_now), flat(u_prev), flat(adjoint_next), flat(adjoint_later), flat(density), flat(step_factor),
+        flat(fixed_nodes), load_top, load_depth, brick_stiffness,
+    )
     e, w = pl.pallas_call(
         exchange_kernel,
         out_shape=(
             jax.ShapeDtypeStruct((TILES, PLANES, 128), F32),
             jax.ShapeDtypeStruct((2, OUT, DEPTH), BF16),
         ),
-        in_specs=[vmem] * 13,
+        in_specs=[pl.BlockSpec(memory_space=pltpu.HBM)] * 10,
         out_specs=(vmem, vmem),
-        scratch_shapes=[
+        scratch_shapes=[pltpu.VMEM(x.shape, x.dtype) for x in sources] + [
             pltpu.VMEM((PLANES, 128), F32),
             pltpu.VMEM((PLANES, 128), F32),
             pltpu.VMEM((PLANES, 128), F32),
+            pltpu.SemaphoreType.DMA((10,)),
             pltpu.SemaphoreType.DMA((6,)),
             pltpu.SemaphoreType.DMA((6,)),
         ],
-        compiler_params=pltpu.CompilerParams(collective_id=0, has_side_effects=True, vmem_limit_bytes=24 * 2**20),
+        compiler_params=pltpu.CompilerParams(collective_id=0, has_side_effects=True, vmem_limit_bytes=48 * 2**20),
         name="exchange",
-    )(
-        flat(u_now), flat(u_prev), flat(adjoint_next), flat(adjoint_later), flat(density), flat(step_factor),
-        flat(fixed_nodes), load_top, load_depth, brick_stiffness, pick, spread, band,
-    )
+    )(*(pltpu.with_memory_space_constraint(x, pltpu.HBM) for x in sources))
     tile = pltpu.VMEM((TILES, GROUP, 128), F32)
     first, second, sens = pl.pallas_call(
         plate_kernel,

time: 46.7 us -> 35.7 us (0.76); the launches traced: 46.1 us -> 35.6 us
  local copies, waits for them, and re-layouts: 10.7 us -> 0 us
    unnamed x26 -> x0, local copies, waits for them, and re-layouts: 10.7 us -> none
where the time goes in v2:
time: 35.7 us; the launch traced here: 35.6 us
  Pallas kernels  34.9 us (98%)
  between operations  0.64 us (2%)
    pallas_call x1, Pallas kernels, local(): pl.pallas_call(plate_kernel, out_shape=(jax.ShapeDtypeStruct((36 * ROWS,...  20.2 us
    pallas_call x1, Pallas kernels, local(): pl.pallas_call(exchange_kernel, out_shape=(jax.ShapeDtypeStruct((TILES, P...  14.8 us

profile of v2, /device:TPU:96, one launch (start us, length us, event | category | flops | bytes accessed | tf_op | source)
XLA Modules:
  0.0 35.6 jit_solution(10526323747050254523)
XLA Ops:
  0.6 14.8 %exchange.1 = (f32[16,176,128]{2,1,0:T(8,128)S(1)}, bf16[2,320,192]{2,1,0:T(8,128)(2,1)S(1)}) custom-call(f32[288,128]{1,0:T(8,128)} %bitcast.10, f32[288,128]{1,0:T(8,128)} %bitcast.11, f32[288,128]{1,0:T(8,128)} %bitcast.12, f32[288,128]{1,0:T(8,128)} %bitcast.13, f32[88,128]{1,0:T(8,128)} %bitcast.16, f32[96,128]{1,0:T(8,128)} %bitcast.14, ...), custom_call_target="tpu_custom_call" | custom-call | tf_op jit(solution)/shard_map/exchange/pallas_call | solution.py:401
  15.4 20.2 %plate.1 = (f32[288,128]{1,0:T(8,128)}, f32[288,128]{1,0:T(8,128)}, f32[88,128]{1,0:T(8,128)}) custom-call(f32[16,176,128]{2,1,0:T(8,128)S(1)} %get-tuple-element.8.e, bf16[2,320,192]{2,1,0:T(8,128)(2,1)S(1)} %get-tuple-element.9.w), custom_call_target="tpu_custom_call" | custom-call | tf_op jit(solution)/shard_map/plate/pallas_call | solution.py:421

commit v3 on v2

v3 whole, which is shorter than its diff:
```python
import jax
import jax.numpy as jnp
from jax import lax
from jax.experimental import pallas as pl
from jax.experimental.pallas import tpu as pltpu
from jax.sharding import PartitionSpec as P

EMIN = 0.001
MESH = pl.DeviceIdType.MESH
F32 = jnp.float32
BF16 = jnp.bfloat16

ROWS = 8
TILES = 16
LEFT, RIGHT = 14, 15
U, S, A, D, B, LOAD, Q, PLANES = 0, 36, 48, 84, 96, 132, 136, 176
DEEP = 96
GROUP = 40
OUT = 8 * GROUP
WIDE = 6 * GROUP
DEPTH = 2 * WIDE


def banded_weights(stiff, w):
    def split(place):
        comp = (place >= 12).astype(jnp.int32) + (place >= 24).astype(jnp.int32)
        return comp, place - 12 * comp

    iota = lambda shape, d: lax.broadcasted_iota(jnp.int32, shape, d)
    group, r = iota((8, GROUP, 24), 0), iota((8, GROUP, 24), 1)
    dz = group & 1
    comp, layer = split(r)
    element = layer - dz
    real = (r < 36) & (element >= 0) & (element <= 10)
    pick = jnp.where(real & (iota((8, GROUP, 24), 2) == comp * 8 + 4 * dz + (group >> 1)), 1.0, 0.0)
    pick = pick.reshape(OUT, 24).astype(BF16)

    def columns(shape):
        q = iota(shape, len(shape) - 1)
        block = sum((q >= GROUP * k).astype(jnp.int32) for k in range(1, 12))
        s = q - GROUP * block
        dx = (block >= 6).astype(jnp.int32)
        block = block - 6 * dx
        dy = ((block == 2) | (block == 3) | (block == 5)).astype(jnp.int32)
        return (2 * dx + dy, block >= 4, s) + split(s)

    place, fine, s, comp, _ = columns((24, DEPTH))
    offset = columns((8, GROUP, DEPTH))[4] - split(iota((8, GROUP, DEPTH), 1))[1] + (iota((8, GROUP, DEPTH), 0) & 1)
    offset = offset.reshape(OUT, DEPTH)
    low = stiff - stiff.astype(BF16).astype(F32)
    full = jnp.zeros((OUT, DEPTH), F32)
    for part, value in enumerate((stiff.astype(BF16), low.astype(BF16))):
        rows = jnp.dot(pick, value, preferred_element_type=F32).astype(BF16)
        for up in (0, 1):
            here = (s < 36) & (iota((24, DEPTH), 0) == comp * 8 + 4 * up + place) & (fine == bool(part))
            spread = jnp.where(here, 1.0, 0.0).astype(BF16)
            full = full + jnp.where(offset == up, jnp.dot(rows, spread, preferred_element_type=F32), 0.0)
    w[...] = full.astype(BF16)


def exchange_kernel(*refs):
    sources, (e, w), held, rest = refs[:10], refs[10:12], refs[12:22], refs[22:]
    u, b, a, q, den, step, fix, top, depth, stiff = held
    packed, from_left, from_right, load_sem, send_sem, recv_sem = rest
    gx, gy = lax.axis_index("gx"), lax.axis_index("gy")
    nx, ny = lax.axis_size("gx"), lax.axis_size("gy")
    has = {"down": gx > 0, "up": gx < nx - 1, "left": gy > 0, "right": gy < ny - 1}
    where = {"down": (gx - 1, gy), "up": (gx + 1, gy), "left": (gx, gy - 1), "right": (gx, gy + 1)}
    barrier = pltpu.get_barrier_semaphore()
    for side in where:
        @pl.when(has[side])
        def _(side=side):
            pl.semaphore_signal(barrier, inc=1, device_id=where[side], device_id_type=MESH)

    loads = [pltpu.make_async_copy(src, dst, load_sem.at[k]) for k, (src, dst) in enumerate(zip(sources, held))]
    for c in loads:
        c.start()
    for c in loads:
        c.wait()
    for r in range(ROWS):
        t = r + 3
        free = 1.0 - fix[pl.ds(r, 12, stride=8), :].astype(F32)
        e[t, U:U + 36] = u[pl.ds(r, 36, stride=8), :]
        e[t, S:S + 12] = free * step[pl.ds(r, 12, stride=8), :]
        e[t, A:A + 36] = a[pl.ds(r, 36, stride=8), :]
        e[t, D:D + 11] = den[pl.ds(r, 11, stride=8), :]
        e[t, D + 11:D + 12] = jnp.zeros((1, 128), F32)
        e[t, B:B + 36] = b[pl.ds(r, 36, stride=8), :]
        e[t, LOAD:LOAD + 1] = top[r:r + 1, :]
        e[t, LOAD + 1:LOAD + 2] = depth[r:r + 1, :].astype(F32)
        e[t, LOAD + 2:LOAD + 4] = jnp.zeros((2, 128), F32)
        e[t, Q:Q + 36] = q[pl.ds(r, 36, stride=8), :]
        e[t, Q + 36:Q + 40] = jnp.zeros((4, 128), F32)
    for t in (0, 13):
        e[t, DEEP:PLANES] = jnp.zeros((PLANES - DEEP, 128), F32)

    @pl.when(gx == 0)
    def _():
        for t in (0, 1, 2):
            e[t] = jnp.zeros((PLANES, 128), F32)

    @pl.when(gx == nx - 1)
    def _():
        for t in (11, 12, 13):
            e[t] = jnp.zeros((PLANES, 128), F32)

    count = sum(has[side].astype(jnp.int32) for side in where)
    pl.semaphore_wait(barrier, count)

    def remote(src, dst, k, side):
        return pltpu.make_async_remote_copy(
            src_ref=src, dst_ref=dst, send_sem=send_sem.at[k], recv_sem=recv_sem.at[k],
            device_id=where[side], device_id_type=MESH,
        )

    down = [
        remote(e.at[3:6, 0:DEEP], e.at[11:14, 0:DEEP], 0, "down"),
        remote(e.at[3:5, DEEP:PLANES], e.at[11:13, DEEP:PLANES], 1, "down"),
    ]
    up = [
        remote(e.at[8:11, 0:DEEP], e.at[0:3, 0:DEEP], 2, "up"),
        remote(e.at[9:11, DEEP:PLANES], e.at[1:3, DEEP:PLANES], 3, "up"),
    ]

    @pl.when(has["down"])
    def _():
        for c in down:
            c.start()

    @pl.when(has["up"])
    def _():
        for c in up:
            c.start()

    lane = lax.broadcasted_iota(jnp.int32, (PLANES, 128), 1)
    row_of = ((lane + 1) & 127) >> 3
    column = ((lane + 1) & 7) - 1

    def pack(tiles):
        total = packed[...]
        for t in tiles:
            total = jnp.where(row_of == t, pltpu.roll(e[t], 8 * t + 3, 1), total)
        packed[...] = total

    packed[...] = jnp.zeros((PLANES, 128), F32)
    pack(range(3, 11))

    banded_weights(stiff[...], w)

    @pl.when(has["down"])
    def _():
        for c in up:
            c.wait_recv()

    @pl.when(has["up"])
    def _():
        for c in down:
            c.wait_recv()

    pack((0, 1, 2, 11, 12, 13))
    to_left = remote(packed, from_right, 4, "left")
    to_right = remote(packed, from_left, 5, "right")

    @pl.when(has["left"])
    def _():
        to_left.start()

    @pl.when(has["right"])
    def _():
        to_right.start()

    e[LEFT] = jnp.where(column >= 3, packed[...], 0.0)
    e[RIGHT] = jnp.where(column <= 2, packed[...], 0.0)

    @pl.when(has["left"])
    def _():
        to_right.wait_recv()
        e[LEFT] = jnp.where(column <= 2, from_left[...], e[LEFT])

    @pl.when(has["right"])
    def _():
        to_left.wait_recv()
        e[RIGHT] = jnp.where(column >= 3, from_right[...], e[RIGHT])

    @pl.when(has["down"])
    def _():
        for c in down:
            c.wait_send()

    @pl.when(has["up"])
    def _():
        for c in up:
            c.wait_send()

    @pl.when(has["left"])
    def _():
        to_left.wait_send()

    @pl.when(has["right"])
    def _():
        to_right.wait_send()


def halves(v):
    high = v.astype(BF16).astype(F32)
    return high, v - high


def spread_halves(here, rolled):
    (h, l), (hr, lr) = here, rolled
    return [jnp.concatenate(x, 0).astype(BF16) for x in ((h, l), (hr, lr), (h, hr))]


def plate_kernel(e, w, first_out, second_out, sens_out, fac, fup, srep, load, u0r, u1, u1r, u2, u2r, a2, a1, acc0, acc1, xu0, xu1, xz3, xz2, xz1, xs, first, second, sens, out_sem):
    lane = lax.broadcasted_iota(jnp.int32, (GROUP, 128), 1)
    layer = lax.broadcasted_iota(jnp.int32, (12, 128), 0).astype(F32)
    edge = (lane == 0) | (lane == 127)
    from_left = ((lane + 1) & 7) >= 4
    roll = lambda v, by: pltpu.roll(v, by, 1) if by else v
    tile_rows = lambda at: (lambda t: e[t, at:at + GROUP])
    of = lambda ref: (lambda t: ref[t])
    u_now, u_before, adj_next, adj_later = (tile_rows(at) for at in (U, B, A, Q))

    def put(x, t, v, rolled_ref=None):
        here = halves(v)
        if rolled_ref is None:
            rolled = tuple(roll(part, 127) for part in here)
        else:
            vr = roll(v, 127)
            rolled_ref[t] = vr
            rolled = halves(vr)
        for k, part in enumerate(spread_halves(here, rolled)):
            x[t, 80 * k:80 * k + 80] = part

    def put_seam(n, side, v):
        here = halves(v)
        cols = slice(128 * side, 128 * side + 128)
        at = 0
        for pair in ((0, 127), (120, 119)):
            parts = spread_halves(*(tuple(roll(part, by) for part in here) for by in pair))
            for part in parts:
                xs[n, at:at + 80, cols] = part
                at += 80

    def prepare(t):
        d = e[t, D:D + 12]
        f = jnp.where(d > 0.0, EMIN + (1.0 - EMIN) * (d * d * d), 0.0)
        s = e[t, S:S + 12]
        top = jnp.where(e[t, LOAD + 1:LOAD + 2] == layer, e[t, LOAD:LOAD + 1], 0.0)
        fac[t, 36:40] = jnp.zeros((4, 128), F32)
        fup[t, 0:1] = jnp.zeros((1, 128), F32)
        fup[t, 36:40] = jnp.zeros((4, 128), F32)
        srep[t, 36:40] = jnp.zeros((4, 128), F32)
        load[t, 0:24] = jnp.zeros((24, 128), F32)
        load[t, 24:36] = top
        load[t, 36:40] = jnp.zeros((4, 128), F32)
        for c in (0, 12, 24):
            fac[t, c:c + 12] = f
            fup[t, c + 1:c + 12] = f[0:11]
            if c:
                fup[t, c:c + 1] = jnp.zeros((1, 128), F32)
            srep[t, c:c + 12] = s

    def weigh(t, f):
        return [
            fac[t] * f[(2 * k) * GROUP:(2 * k + 1) * GROUP] + fup[t] * f[(2 * k + 1) * GROUP:(2 * k + 2) * GROUP]
            for k in range(4)
        ]

    def collect(t, f, corners, fresh):
        for dz, acc in ((0, acc0), (1, acc1)):
            total = None if fresh else acc[t]
            for k in range(4):
                term = f[(2 * k + dz) * GROUP:(2 * k + dz + 1) * GROUP] * corners[k]
                total = term if total is None else total + term
            acc[t] = total

    def seam_map(n, finish, state=None, fresh=False):
        f = jnp.dot(w[...], xs[n], preferred_element_type=F32)
        outs = []
        for side in (0, 1):
            t = LEFT + side
            part = f[:, 128 * side:128 * side + 128]
            if state is not None and side == 1:
                v = state(t)
                collect(t, part, [roll(v, by) for by in (0, 127, 120, 119)], fresh)
            g = weigh(t, part)
            outs.append(g[0] + roll(g[1], 1) + roll(g[2], 8) + roll(g[3], 9))
            if finish is not None:
                finish(side, outs[-1])
        return jnp.where(from_left, outs[0], outs[1])

    def main_map(x, start, stop, seam, finish, state=None, fresh=False):
        below = below_rolled = None
        pending = None

        def post(t0, f):
            nonlocal below, below_rolled
            for k in (0, 1):
                t = t0 + k
                if t >= stop:
                    continue
                part = f[:, 128 * k:128 * k + 128]
                if state is not None and 3 <= t <= 10:
                    now, rolled = state
                    collect(t, part, [now(t), rolled(t), now(t + 1), rolled(t + 1)], fresh)
                g = weigh(t, part)
                if below is not None:
                    out = g[0] + below + roll(g[1] + below_rolled, 1)
                    finish(t, jnp.where(edge, roll(seam, 125 - 8 * t), out))
                below, below_rolled = g[2], g[3]

        for t0 in range(start, stop, 2):
            wide = [jnp.concatenate([x[t], x[t + 1]], 0) for t in (t0, t0 + 1)]
            f = jnp.dot(w[...], jnp.concatenate(wide, 1), preferred_element_type=F32)
            if pending is not None:
                post(*pending)
            pending = (t0, f)
        post(*pending)

    def step_u(t, now, before, out):
        s = srep[t]
        return jnp.where(s > 0.0, 2.0 * now(t) - before(t) + s * (load[t] - out), 0.0)

    def step_a(t, now, before, out):
        return 2.0 * now(t) - before(t) + load[t] - out

    for t in (LEFT, RIGHT):
        prepare(t)
        put_seam(0, t - LEFT, u_now(t))
        put_seam(2, t - LEFT, srep[t] * adj_next(t))

    def seam_u1(side, out):
        v = step_u(LEFT + side, u_now, u_before, out)
        u1[LEFT + side] = v
        put_seam(1, side, v)

    def seam_u2(side, out):
        u2[LEFT + side] = step_u(LEFT + side, of(u1), u_now, out)

    def seam_a2(side, out):
        v = step_a(LEFT + side, adj_next, adj_later, out)
        a2[LEFT + side] = v
        put_seam(3, side, srep[LEFT + side] * v)

    def seam_a1(side, out):
        v = step_a(LEFT + side, of(a2), adj_next, out)
        put_seam(4, side, srep[LEFT + side] * v)

    for t in range(14):
        prepare(t)
        put(xu0, t, u_now(t), u0r)
    k1 = seam_map(0, seam_u1)
    k2 = seam_map(1, seam_u2)
    for t in range(14):
        put(xz3, t, srep[t] * adj_next(t))
    k3 = seam_map(2, seam_a2, of(u2), True)
    k4 = seam_map(3, seam_a1, of(u1))
    k5 = seam_map(4, None, u_now)

    def main_u1(t, out):
        v = step_u(t, u_now, u_before, out)
        u1[t] = v
        put(xu1, t, v, u1r)

    def main_u2(t, out):
        v = step_u(t, of(u1), u_now, out)
        u2[t] = v
        u2r[t] = roll(v, 127)

    def main_a2(t, out):
        v = step_a(t, adj_next, adj_later, out)
        a2[t] = v
        put(xz2, t, srep[t] * v)

    def main_a1(t, out):
        v = step_a(t, of(a2), adj_next, out)
        a1[t] = v
        put(xz1, t, srep[t] * v)
        if 3 <= t <= 10:
            second[pl.ds(t - 3, 36, stride=8), :] = v[0:36]

    def main_a0(t, out):
        first[pl.ds(t - 3, 36, stride=8), :] = step_a(t, of(a1), of(a2), out)[0:36]

    main_map(xu0, 1, 13, k1, main_u1)
    main_map(xu1, 2, 12, k2, main_u2)
    main_map(xz3, 0, 13, k3, main_a2, (of(u2), of(u2r)), True)
    main_map(xz2, 1, 12, k4, main_a1, (of(u1), of(u1r)))
    copy_second = pltpu.make_async_copy(second, second_out, out_sem.at[1])
    copy_second.start()
    main_map(xz1, 2, 11, k5, main_a0, (u_now, of(u0r)))
    copy_first = pltpu.make_async_copy(first, first_out, out_sem.at[0])
    copy_first.start()

    def total(t):
        return sum(acc0[t, c:c + 11] + acc1[t, c + 1:c + 12] for c in (0, 12, 24))

    seam = total(RIGHT)
    last = lax.broadcasted_iota(jnp.int32, (11, 128), 1) == 127
    for r in range(ROWS):
        t = r + 3
        d = e[t, D:D + 11]
        both = jnp.where(last, roll(seam, 125 - 8 * t), total(t))
        sens[pl.ds(r, 11, stride=8), :] = (-3.0 * (1.0 - EMIN)) * (d * d) * both
    copy_sens = pltpu.make_async_copy(sens, sens_out, out_sem.at[2])
    copy_sens.start()
    copy_second.wait()
    copy_first.wait()
    copy_sens.wait()


def local(u_now, u_prev, adjoint_next, adjoint_later, density, step_factor, fixed_nodes, load_top, load_depth, brick_stiffness):
    vmem = pl.BlockSpec(memory_space=pltpu.VMEM)
    flat = lambda x: x.reshape(-1, 128)
    sources = (
        flat(u_now), flat(u_prev), flat(adjoint_next), flat(adjoint_later), flat(density), flat(step_factor),
        flat(fixed_nodes), load_top, load_depth, brick_stiffness,
    )
    e, w = pl.pallas_call(
        exchange_kernel,
        out_shape=(
            jax.ShapeDtypeStruct((TILES, PLANES, 128), F32),
            jax.ShapeDtypeStruct((OUT, DEPTH), BF16),
        ),
        in_specs=[pl.BlockSpec(memory_space=pltpu.HBM)] * 10,
        out_specs=(vmem, vmem),
        scratch_shapes=[pltpu.VMEM(x.shape, x.dtype) for x in sources] + [
            pltpu.VMEM((PLANES, 128), F32),
            pltpu.VMEM((PLANES, 128), F32),
            pltpu.VMEM((PLANES, 128), F32),
            pltpu.SemaphoreType.DMA((10,)),
            pltpu.SemaphoreType.DMA((6,)),
            pltpu.SemaphoreType.DMA((6,)),
        ],
        compiler_params=pltpu.CompilerParams(collective_id=0, has_side_effects=True, vmem_limit_bytes=48 * 2**20),
        name="exchange",
    )(*(pltpu.with_memory_space_constraint(x, pltpu.HBM) for x in sources))
    tile = pltpu.VMEM((TILES, GROUP, 128), F32)
    wide = pltpu.VMEM((TILES, WIDE, 128), BF16)
    results = ((36 * ROWS, 128), (36 * ROWS, 128), (11 * ROWS, 128))
    first, second, sens = pl.pallas_call(
        plate_kernel,
        out_shape=tuple(jax.ShapeDtypeStruct(shape, F32) for shape in results),
        in_specs=[vmem] * 2,
        out_specs=(pl.BlockSpec(memory_space=pltpu.HBM),) * 3,
        scratch_shapes=[tile] * 13 + [wide] * 5
        + [pltpu.VMEM((5, DEPTH, 256), BF16)]
        + [pltpu.VMEM(shape, F32) for shape in results]
        + [pltpu.SemaphoreType.DMA((3,))],
        compiler_params=pltpu.CompilerParams(vmem_limit_bytes=48 * 2**20),
        name="plate",
    )(e, w)
    return (
        first.reshape(u_now.shape),
        second.reshape(u_now.shape),
        sens.reshape(density.shape),
    )


def solution(mesh):
    in_specs = (
        P(None, None, "gx", "gy"),
        P(None, None, "gx", "gy"),
        P(None, None, "gx", "gy"),
        P(None, None, "gx", "gy"),
        P(None, "gx", "gy"),
        P(None, "gx", "gy"),
        P(None, "gx", "gy"),
        P("gx", "gy"),
        P("gx", "gy"),
        P(),
    )
    out_specs = (P(None, None, "gx", "gy"), P(None, None, "gx", "gy"), P(None, "gx", "gy"))
    return jax.shard_map(local, mesh=mesh, in_specs=in_specs, out_specs=out_specs, check_vma=False)
```

time: 35.7 us -> 21.3 us (0.60)
  Pallas kernels: 34.9 us -> 20.6 us
    pallas_call x1, Pallas kernels: 20.2 us -> 5.8 us  [local(): pl.pallas_call(plate_kernel, out_shape=tuple((jax.ShapeDtypeStruct(shape,...]
where the time goes in v3:
time: 21.3 us; the launch traced here: 21.2 us
  Pallas kernels  20.6 us (97%)
  between operations  0.64 us (3%)
    pallas_call x1, Pallas kernels, local(): pl.pallas_call(exchange_kernel, out_shape=(jax.ShapeDtypeStruct((TILES, P...  14.8 us
    pallas_call x1, Pallas kernels, local(): pl.pallas_call(plate_kernel, out_shape=tuple((jax.ShapeDtypeStruct(shape,...  5.8 us

profile of v3, /device:TPU:96, one launch (start us, length us, event | category | flops | bytes accessed | tf_op | source)
XLA Modules:
  0.0 21.2 jit_solution(602871436821314897)
XLA Ops:
  0.6 14.8 %exchange.1 = (f32[16,176,128]{2,1,0:T(8,128)S(1)}, bf16[320,480]{1,0:T(8,128)(2,1)S(1)}) custom-call(f32[288,128]{1,0:T(8,128)} %bitcast.10, f32[288,128]{1,0:T(8,128)} %bitcast.11, f32[288,128]{1,0:T(8,128)} %bitcast.12, f32[288,128]{1,0:T(8,128)} %bitcast.13, f32[88,128]{1,0:T(8,128)} %bitcast.16, f32[96,128]{1,0:T(8,128)} %bitcast.14, ...), custom_call_target="tpu_custom_call" | custom-call | tf_op jit(solution)/shard_map/exchange/pallas_call | solution.py:420
  15.4 5.8 %plate.1 = (f32[288,128]{1,0:T(8,128)}, f32[288,128]{1,0:T(8,128)}, f32[88,128]{1,0:T(8,128)}) custom-call(f32[16,176,128]{2,1,0:T(8,128)S(1)} %get-tuple-element.8.e, bf16[320,480]{1,0:T(8,128)(2,1)S(1)} %get-tuple-element.9.w), custom_call_target="tpu_custom_call" | custom-call | tf_op jit(solution)/shard_map/plate/pallas_call | solution.py:442

commit v4 on v3

v4 whole, which is shorter than its diff:
```python
import jax
import jax.numpy as jnp
from jax import lax
from jax.experimental import pallas as pl
from jax.experimental.pallas import tpu as pltpu
from jax.sharding import PartitionSpec as P

EMIN = 0.001
MESH = pl.DeviceIdType.MESH
F32 = jnp.float32
BF16 = jnp.bfloat16

ROWS = 8
OWN = range(3, 11)
MAIN = 14
LEFT, RIGHT = 14, 15
TILES = 16
U, S, A, D, B, LOAD, Q, PLANES = 0, 36, 48, 84, 96, 132, 136, 192
FOLD = 48
GROUP = 40
OUT = 8 * GROUP
WIDE = 6 * GROUP
DEPTH = 2 * WIDE


def banded_weights(stiff, w):
    def split(place):
        comp = (place >= 12).astype(jnp.int32) + (place >= 24).astype(jnp.int32)
        return comp, place - 12 * comp

    iota = lambda shape, d: lax.broadcasted_iota(jnp.int32, shape, d)
    group, r = iota((8, GROUP, 24), 0), iota((8, GROUP, 24), 1)
    dz = group & 1
    comp, layer = split(r)
    element = layer - dz
    real = (r < 36) & (element >= 0) & (element <= 10)
    pick = jnp.where(real & (iota((8, GROUP, 24), 2) == comp * 8 + 4 * dz + (group >> 1)), 1.0, 0.0)
    pick = pick.reshape(OUT, 24).astype(BF16)

    def columns(shape):
        q = iota(shape, len(shape) - 1)
        block = sum((q >= GROUP * k).astype(jnp.int32) for k in range(1, 12))
        s = q - GROUP * block
        dx = (block >= 6).astype(jnp.int32)
        block = block - 6 * dx
        dy = ((block == 2) | (block == 3) | (block == 5)).astype(jnp.int32)
        return (2 * dx + dy, block >= 4, s) + split(s)

    place, fine, s, comp, _ = columns((24, DEPTH))
    offset = columns((8, GROUP, DEPTH))[4] - split(iota((8, GROUP, DEPTH), 1))[1] + (iota((8, GROUP, DEPTH), 0) & 1)
    offset = offset.reshape(OUT, DEPTH)
    low = stiff - stiff.astype(BF16).astype(F32)
    full = jnp.zeros((OUT, DEPTH), F32)
    for part, value in enumerate((stiff.astype(BF16), low.astype(BF16))):
        rows = jnp.dot(pick, value, preferred_element_type=F32).astype(BF16)
        for up in (0, 1):
            here = (s < 36) & (iota((24, DEPTH), 0) == comp * 8 + 4 * up + place) & (fine == bool(part))
            spread = jnp.where(here, 1.0, 0.0).astype(BF16)
            full = full + jnp.where(offset == up, jnp.dot(rows, spread, preferred_element_type=F32), 0.0)
    w[...] = full.astype(BF16)


def roll(v, by):
    return pltpu.roll(v, by % 128, 1) if by % 128 else v


def lanes(rows):
    return lax.broadcasted_iota(jnp.int32, (rows, 128), 1)


def halves(v):
    high = v.astype(BF16).astype(F32)
    return high, v - high


def spread_halves(here, rolled):
    (h, l), (hr, lr) = here, rolled
    return [jnp.concatenate(x, 0).astype(BF16) for x in ((h, l), (hr, lr), (h, hr))]


def put(x, t, v, rolled_ref=None):
    here = halves(v)
    if rolled_ref is None:
        rolled = tuple(roll(part, 127) for part in here)
    else:
        vr = roll(v, 127)
        rolled_ref[t] = vr
        rolled = halves(vr)
    for k, part in enumerate(spread_halves(here, rolled)):
        x[t, 80 * k:80 * k + 80] = part


def prepare(at, tile, fac, fup, srep, load):
    layer = lax.broadcasted_iota(jnp.int32, (12, 128), 0).astype(F32)
    d = tile[D:D + 12]
    f = jnp.where(d > 0.0, EMIN + (1.0 - EMIN) * (d * d * d), 0.0)
    s = tile[S:S + 12]
    zeros = lambda n: jnp.zeros((n, 128), F32)
    fac[at, 36:40] = zeros(4)
    fup[at, 36:40] = zeros(4)
    srep[at, 36:40] = zeros(4)
    load[at, 0:24] = zeros(24)
    load[at, 24:36] = jnp.where(tile[LOAD + 1:LOAD + 2] == layer, tile[LOAD:LOAD + 1], 0.0)
    load[at, 36:40] = zeros(4)
    for c in (0, 12, 24):
        fac[at, c:c + 12] = f
        fup[at, c:c + 1] = zeros(1)
        fup[at, c + 1:c + 12] = f[0:11]
        srep[at, c:c + 12] = s


def weigh(f, above, below):
    return [
        above * f[(2 * k) * GROUP:(2 * k + 1) * GROUP] + below * f[(2 * k + 1) * GROUP:(2 * k + 2) * GROUP]
        for k in range(4)
    ]


def pairs_of(w, jobs, post):
    pending = []
    for at in range(0, len(jobs), 2):
        two = jobs[at:at + 2]
        wide = [jnp.concatenate([x, y], 0) for _, x, y in two]
        wide = wide[0] if len(wide) == 1 else jnp.concatenate(wide, 1)
        f = jnp.dot(w[...], wide, preferred_element_type=F32)
        for job in pending:
            post(*job)
        pending = [(key, f[:, 128 * k:128 * k + 128]) for k, (key, _, _) in enumerate(two)]
    for job in pending:
        post(*job)


def exchange_kernel(*refs):
    sources, refs = refs[:10], refs[10:]
    e, w, mine, near, corner, fac, fup, srep, load, u0r, xu0, xz3, o1, o3, p1, p3, f3 = refs[:17]
    held, (corner_out, load_sem, send_sem, recv_sem) = refs[17:27], refs[27:]
    u, b, a, q, den, step, fix, top, depth, stiff = held
    gx, gy = lax.axis_index("gx"), lax.axis_index("gy")
    nx, ny = lax.axis_size("gx"), lax.axis_size("gy")
    down, up, left, right = gx > 0, gx < nx - 1, gy > 0, gy < ny - 1
    sides = {
        (-1, 0): down, (1, 0): up, (0, -1): left, (0, 1): right,
        (-1, -1): down & left, (1, -1): up & left, (-1, 1): down & right, (1, 1): up & right,
    }
    barrier = pltpu.get_barrier_semaphore()
    for (dx, dy), there in sides.items():
        @pl.when(there)
        def _(dx=dx, dy=dy):
            pl.semaphore_signal(barrier, inc=1, device_id=(gx + dx, gy + dy), device_id_type=MESH)

    loads = [pltpu.make_async_copy(src, dst, load_sem.at[k]) for k, (src, dst) in enumerate(zip(sources, held))]
    for c in loads:
        c.start()
    zeros = lambda n: jnp.zeros((n, 128), F32)
    e[0, 0:32] = zeros(32)
    e[0, 96:PLANES] = zeros(PLANES - 96)
    e[1, 96:128] = zeros(32)
    for t in (1, 2, 11, 12):
        e[t, 176:PLANES] = zeros(PLANES - 176)
    e[13, 88:PLANES] = zeros(PLANES - 88)

    @pl.when(jnp.logical_not(down))
    def _():
        for t in (0, 1, 2):
            e[t] = zeros(PLANES)

    @pl.when(jnp.logical_not(up))
    def _():
        for t in (11, 12, 13):
            e[t] = zeros(PLANES)

    for k, dy in enumerate((-1, 1)):
        @pl.when(jnp.logical_not(sides[0, dy]))
        def _(k=k):
            near[k] = zeros(FOLD)

        for j, dx in enumerate((-1, 1)):
            @pl.when(jnp.logical_not(sides[dx, dy]))
            def _(k=k, j=j):
                corner[2 * k + j] = zeros(FOLD // 2)

    for c in loads:
        c.wait()
    for r in range(ROWS):
        t = r + 3
        free = 1.0 - fix[pl.ds(r, 12, stride=8), :].astype(F32)
        e[t, U:U + 36] = u[pl.ds(r, 36, stride=8), :]
        e[t, S:S + 12] = free * step[pl.ds(r, 12, stride=8), :]
        e[t, A:A + 36] = a[pl.ds(r, 36, stride=8), :]
        e[t, D:D + 11] = den[pl.ds(r, 11, stride=8), :]
        e[t, D + 11:D + 12] = zeros(1)
        e[t, B:B + 36] = b[pl.ds(r, 36, stride=8), :]
        e[t, LOAD:LOAD + 1] = top[r:r + 1, :]
        e[t, LOAD + 1:LOAD + 2] = depth[r:r + 1, :].astype(F32)
        e[t, LOAD + 2:LOAD + 4] = zeros(2)
        e[t, Q:Q + 36] = q[pl.ds(r, 36, stride=8), :]
        e[t, Q + 36:PLANES] = zeros(PLANES - Q - 36)

    lane = lanes(FOLD)
    first_cols, last_cols = zeros(FOLD), zeros(FOLD)
    for g in range(4):
        for r in range(ROWS):
            slot = 16 * (g >> 1) + 2 * r + (g & 1)
            v = roll(e[r + 3, FOLD * g:FOLD * g + FOLD], 4 * slot + 3)
            first_cols = jnp.where(((lane - 3) & 127) >> 2 == slot, v, first_cols)
            last_cols = jnp.where(((lane + 1) & 127) >> 2 == slot, v, last_cols)
    mine[0] = first_cols
    mine[1] = last_cols
    half = FOLD // 2
    lane = lanes(half)
    for k, cols in enumerate((first_cols, last_cols)):
        low = ((lane - 3 + 4 * k) & 63) < 32
        corner_out[2 * k] = jnp.where(low, cols[0:half], roll(cols[half:FOLD], 32))
        corner_out[2 * k + 1] = jnp.where(low, roll(cols[half:FOLD], -32), cols[0:half])

    pl.semaphore_wait(barrier, sum(there.astype(jnp.int32) for there in sides.values()))
    plan = [
        ((-1, -1), corner_out.at[0], corner.at[3]),
        ((1, -1), corner_out.at[1], corner.at[2]),
        ((-1, 1), corner_out.at[2], corner.at[1]),
        ((1, 1), corner_out.at[3], corner.at[0]),
        ((0, -1), mine.at[0], near.at[1]),
        ((0, 1), mine.at[1], near.at[0]),
        ((-1, 0), e.at[3:5, 0:176], e.at[11:13, 0:176]),
        ((1, 0), e.at[9:11, 0:96], e.at[1:3, 0:96]),
        ((1, 0), e.at[9:11, 128:176], e.at[1:3, 128:176]),
        ((-1, 0), e.at[5, 0:88], e.at[13, 0:88]),
        ((1, 0), e.at[8, 32:96], e.at[0, 32:96]),
        ((1, 0), e.at[10, 96:128], e.at[2, 96:128]),
    ]
    copies = []
    for k, ((dx, dy), src, dst) in enumerate(plan):
        copies.append(((dx, dy), pltpu.make_async_remote_copy(
            src_ref=src, dst_ref=dst, send_sem=send_sem.at[k], recv_sem=recv_sem.at[k],
            device_id=(gx + dx, gy + dy), device_id_type=MESH,
        )))
    for to, c in copies:
        @pl.when(sides[to])
        def _(c=c):
            c.start()

    banded_weights(stiff[...], w)
    for t in OWN:
        k = t - 3
        prepare(k, e.at[t], fac, fup, srep, load)
        put(xu0, k, e[t, U:U + GROUP], u0r)
        put(xz3, k, srep[k] * e[t, A:A + GROUP])

    carry = {}

    def post(key, f):
        kind, k = key
        out, pieces = ((o1, p1), (o3, p3))[kind]
        if kind:
            f3[k] = f
        g = weigh(f, fac[k], fup[k])
        if k == 0:
            pieces[0], pieces[1] = g[0], g[1]
        else:
            out[k - 1] = g[0] + carry[kind][0] + roll(g[1] + carry[kind][1], 1)
        if k == 6:
            pieces[2], pieces[3] = g[2], g[3]
        carry[kind] = g[2:]

    pairs_of(w, [((kind, k), x[k], x[k + 1]) for kind, x in ((0, xu0), (1, xz3)) for k in range(7)], post)

    for (dx, dy), c in copies:
        @pl.when(sides[-dx, -dy])
        def _(c=c):
            c.wait_recv()
    for to, c in copies:
        @pl.when(sides[to])
        def _(c=c):
            c.wait_send()


class Split:
    def __init__(self, own, others):
        self.own, self.others = own, others

    def spot(self, t):
        if t in OWN:
            return self.own, t - 3
        return self.others, t if t < 3 else t - 8

    def __getitem__(self, t):
        ref, at = self.spot(t)
        return ref[at]


def plate_kernel(*refs):
    e, w, mine, near, corner = refs[:5]
    own = refs[5:12]
    o1, o3, p1, p3, f3 = refs[12:17]
    first_out, second_out, sens_out = refs[17:20]
    others = refs[20:27]
    u1, u1r, u2, u2r, a2, a1, acc0, acc1, xu1, xz2, xz1, xs, es, first, second, sens, out_sem = refs[27:]
    fac, fup, srep, load, u0r, xu0, xz3 = (Split(x, y) for x, y in zip(own, others))
    lane = lanes(GROUP)
    edge = (lane == 0) | (lane == 127)
    from_left = ((lane + 1) & 7) >= 4

    def tile_rows(at):
        return lambda t: es[t - LEFT, at:at + GROUP] if t >= LEFT else e[t, at:at + GROUP]

    of = lambda ref: (lambda t: ref[t])
    u_now, u_before, adj_next, adj_later = (tile_rows(at) for at in (U, B, A, Q))

    wide_lane = lanes(FOLD)
    row = ((wide_lane + 1) & 127) >> 3
    late = ((wide_lane + 1) & 7) >= 4
    inner, low, high = (row >= 3) & (row <= 10), row < 3, (row > 10) & (row < 14)
    half = FOLD // 2
    for g in range(4):
        by = 24 - 64 * (g >> 1) - 4 * (g & 1)
        planes = slice(FOLD * g, FOLD * g + FOLD)
        ghost = jnp.zeros((FOLD, 128), F32)
        for t in (0, 1, 2, 11, 12, 13):
            ghost = jnp.where(row == t, roll(e[t, planes], 8 * t + 3), ghost)
        for side in (0, 1):
            near_cols = roll(near[side], by)
            own_cols = roll(mine[side], by)
            below = jnp.concatenate([roll(corner[2 * side], by + 64), roll(corner[2 * side], by + 96)], 0)
            above = jnp.concatenate([roll(corner[2 * side + 1], by + 64), roll(corner[2 * side + 1], by + 32)], 0)
            far = jnp.where(inner, near_cols, jnp.where(low, below, jnp.where(high, above, 0.0)))
            here = jnp.where(inner, own_cols, ghost)
            es[side, planes] = jnp.where(late, here, far) if side == 0 else jnp.where(late, far, here)

    def put_seam(n, side, v):
        here = halves(v)
        cols = slice(128 * side, 128 * side + 128)
        at = 0
        for pair in ((0, 127), (120, 119)):
            parts = spread_halves(*(tuple(roll(part, by) for part in here) for by in pair))
            for part in parts:
                xs[n, at:at + 80, cols] = part
                at += 80

    def collect(t, f, corners, fresh):
        for dz, acc in ((0, acc0), (1, acc1)):
            total = None if fresh else acc[t]
            for k in range(4):
                term = f[(2 * k + dz) * GROUP:(2 * k + dz + 1) * GROUP] * corners[k]
                total = term if total is None else total + term
            acc[t] = total

    def seam_map(n, finish, state=None, fresh=False):
        f = jnp.dot(w[...], xs[n], preferred_element_type=F32)
        outs = []
        for side in (0, 1):
            t = LEFT + side
            part = f[:, 128 * side:128 * side + 128]
            if state is not None and side == 1:
                v = state(t)
                collect(t, part, [roll(v, by) for by in (0, 127, 120, 119)], fresh)
            g = weigh(part, fac[t], fup[t])
            outs.append(g[0] + roll(g[1], 1) + roll(g[2], 8) + roll(g[3], 9))
            if finish is not None:
                finish(side, outs[-1])
        return jnp.where(from_left, outs[0], outs[1])

    def fixed(t, out, seam):
        return jnp.where(edge, roll(seam, 125 - 8 * t), out)

    def main_map(x, elements, seam, finish, state=None, fresh=False, done=None):
        carry = None

        def node(t, above, below):
            out = above[0] + below[0] + roll(above[1] + below[1], 1)
            finish(t, fixed(t, out, seam))

        def post(t, f):
            nonlocal carry
            if state is not None and t in OWN:
                now, rolled = state
                collect(t, f, [now(t), rolled(t), now(t + 1), rolled(t + 1)], fresh)
            g = weigh(f, fac[t], fup[t])
            if done is not None and t == 10:
                node(t, g[0:2], (done[1][2], done[1][3]))
            elif carry is not None:
                node(t, g[0:2], carry)
            carry = g[2:]
            if done is not None and t == 2:
                node(3, (done[1][0], done[1][1]), carry)
                for k in range(6):
                    finish(k + 4, fixed(k + 4, done[0][k], seam))

        pairs_of(w, [(t, x[t], x[t + 1]) for t in elements], post)

    def step_u(t, now, before, out):
        s = srep[t]
        return jnp.where(s > 0.0, 2.0 * now(t) - before(t) + s * (load[t] - out), 0.0)

    def step_a(t, now, before, out):
        return 2.0 * now(t) - before(t) + load[t] - out

    for t in (LEFT, RIGHT):
        prepare(t - 8, es.at[t - LEFT], *others[0:4])
        put_seam(0, t - LEFT, u_now(t))
        put_seam(2, t - LEFT, srep[t] * adj_next(t))

    def seam_u1(side, out):
        v = step_u(LEFT + side, u_now, u_before, out)
        u1[LEFT + side] = v
        put_seam(1, side, v)

    def seam_u2(side, out):
        u2[LEFT + side] = step_u(LEFT + side, of(u1), u_now, out)

    def seam_a2(side, out):
        v = step_a(LEFT + side, adj_next, adj_later, out)
        a2[LEFT + side] = v
        put_seam(3, side, srep[LEFT + side] * v)

    def seam_a1(side, out):
        v = step_a(LEFT + side, of(a2), adj_next, out)
        put_seam(4, side, srep[LEFT + side] * v)

    for t in (0, 1, 2, 11, 12, 13):
        at = t if t < 3 else t - 8
        prepare(at, e.at[t], *others[0:4])
        put(xu0.others, at, u_now(t), u0r.others)
    k1 = seam_map(0, seam_u1)
    k2 = seam_map(1, seam_u2)
    for t in (0, 1, 2, 11, 12, 13):
        put(xz3.others, t if t < 3 else t - 8, srep[t] * adj_next(t))
    k3 = seam_map(2, seam_a2, of(u2), True)
    k4 = seam_map(3, seam_a1, of(u1))
    k5 = seam_map(4, None, u_now)

    def main_u1(t, out):
        v = step_u(t, u_now, u_before, out)
        u1[t] = v
        put(xu1, t, v, u1r)

    def main_u2(t, out):
        v = step_u(t, of(u1), u_now, out)
        u2[t] = v
        u2r[t] = roll(v, 127)

    def main_a2(t, out):
        v = step_a(t, adj_next, adj_later, out)
        a2[t] = v
        put(xz2, t, srep[t] * v)

    def main_a1(t, out):
        v = step_a(t, of(a2), adj_next, out)
        a1[t] = v
        put(xz1, t, srep[t] * v)
        if t in OWN:
            second[pl.ds(t - 3, 36, stride=8), :] = v[0:36]

    def main_a0(t, out):
        first[pl.ds(t - 3, 36, stride=8), :] = step_a(t, of(a1), of(a2), out)[0:36]

    main_map(xu0, (1, 2, 10, 11, 12), k1, main_u1, done=(o1, p1))
    main_map(xu1, range(2, 12), k2, main_u2)
    for t in range(3, 10):
        collect(t, f3[t - 3], [u2[t], u2r[t], u2[t + 1], u2r[t + 1]], True)
    main_map(xz3, (0, 1, 2, 10, 11, 12), k3, main_a2, (of(u2), of(u2r)), True, done=(o3, p3))
    main_map(xz2, range(1, 12), k4, main_a1, (of(u1), of(u1r)))
    copy_second = pltpu.make_async_copy(second, second_out, out_sem.at[1])
    copy_second.start()
    main_map(xz1, range(2, 11), k5, main_a0, (u_now, of(u0r)))
    copy_first = pltpu.make_async_copy(first, first_out, out_sem.at[0])
    copy_first.start()

    def total(t):
        return sum(acc0[t, c:c + 11] + acc1[t, c + 1:c + 12] for c in (0, 12, 24))

    seam = total(RIGHT)
    last = lanes(11) == 127
    for r in range(ROWS):
        t = r + 3
        d = e[t, D:D + 11]
        both = jnp.where(last, roll(seam, 125 - 8 * t), total(t))
        sens[pl.ds(r, 11, stride=8), :] = (-3.0 * (1.0 - EMIN)) * (d * d) * both
    copy_sens = pltpu.make_async_copy(sens, sens_out, out_sem.at[2])
    copy_sens.start()
    copy_second.wait()
    copy_first.wait()
    copy_sens.wait()


def local(u_now, u_prev, adjoint_next, adjoint_later, density, step_factor, fixed_nodes, load_top, load_depth, brick_stiffness):
    vmem = pl.BlockSpec(memory_space=pltpu.VMEM)
    hbm = pl.BlockSpec(memory_space=pltpu.HBM)
    flat = lambda x: x.reshape(-1, 128)
    sources = (
        flat(u_now), flat(u_prev), flat(adjoint_next), flat(adjoint_later), flat(density), flat(step_factor),
        flat(fixed_nodes), load_top, load_depth, brick_stiffness,
    )
    f32 = lambda *shape: jax.ShapeDtypeStruct(shape + (128,), F32)
    bf16 = lambda *shape: jax.ShapeDtypeStruct(shape, BF16)
    passed = (
        [f32(MAIN, PLANES), bf16(OUT, DEPTH), f32(2, FOLD), f32(2, FOLD), f32(4, FOLD // 2)]
        + [f32(ROWS, GROUP)] * 5 + [bf16(ROWS, WIDE, 128)] * 2
        + [f32(6, GROUP)] * 2 + [f32(4, GROUP)] * 2 + [f32(7, OUT)]
    )
    gathered = pl.pallas_call(
        exchange_kernel,
        out_shape=passed,
        in_specs=[hbm] * 10,
        out_specs=[vmem] * len(passed),
        scratch_shapes=[pltpu.VMEM(x.shape, x.dtype) for x in sources] + [
            pltpu.VMEM((4, FOLD // 2, 128), F32),
            pltpu.SemaphoreType.DMA((10,)),
            pltpu.SemaphoreType.DMA((12,)),
            pltpu.SemaphoreType.DMA((12,)),
        ],
        compiler_params=pltpu.CompilerParams(collective_id=0, has_side_effects=True, vmem_limit_bytes=32 * 2**20),
        name="exchange",
    )(*(pltpu.with_memory_space_constraint(x, pltpu.HBM) for x in sources))
    scratch = lambda n, shape, kind: [pltpu.VMEM((n, shape, 128), kind)]
    results = ((36 * ROWS, 128), (36 * ROWS, 128), (11 * ROWS, 128))
    first, second, sens = pl.pallas_call(
        plate_kernel,
        out_shape=tuple(jax.ShapeDtypeStruct(shape, F32) for shape in results),
        in_specs=[vmem] * len(passed),
        out_specs=(hbm,) * 3,
        scratch_shapes=scratch(8, GROUP, F32) * 5 + scratch(8, WIDE, BF16) * 2
        + scratch(TILES, GROUP, F32) * 8 + scratch(TILES, WIDE, BF16) * 3
        + [pltpu.VMEM((5, DEPTH, 256), BF16), pltpu.VMEM((2, PLANES, 128), F32)]
        + [pltpu.VMEM(shape, F32) for shape in results]
        + [pltpu.SemaphoreType.DMA((3,))],
        compiler_params=pltpu.CompilerParams(vmem_limit_bytes=40 * 2**20),
        name="plate",
    )(*gathered)
    return (
        first.reshape(u_now.shape),
        second.reshape(u_now.shape),
        sens.reshape(density.shape),
    )


def solution(mesh):
    in_specs = (
        P(None, None, "gx", "gy"),
        P(None, None, "gx", "gy"),
        P(None, None, "gx", "gy"),
        P(None, None, "gx", "gy"),
        P(None, "gx", "gy"),
        P(None, "gx", "gy"),
        P(None, "gx", "gy"),
        P("gx", "gy"),
        P("gx", "gy"),
        P(),
    )
    out_specs = (P(None, None, "gx", "gy"), P(None, None, "gx", "gy"), P(None, "gx", "gy"))
    return jax.shard_map(local, mesh=mesh, in_specs=in_specs, out_specs=out_specs, check_vma=False)
```

time: 21.3 us -> 16.3 us (0.77)
  the two profiles are of different devices: /device:TPU:96 before, /device:TPU:56 now
where the time goes in v4:
time: 16.3 us; the launch traced here: 16 us
  Pallas kernels  15.4 us (94%)
  between operations  0.64 us (4%)
    pallas_call x1, Pallas kernels, local(): pl.pallas_call(exchange_kernel, out_shape=passed, in_specs=[hbm] * 10, ou...  9.7 us
    pallas_call x1, Pallas kernels, local(): pl.pallas_call(plate_kernel, out_shape=tuple((jax.ShapeDtypeStruct(shape,...  5.7 us

profile of v4, /device:TPU:56, one launch (start us, length us, event | category | flops | bytes accessed | tf_op | source)
XLA Modules:
  0.0 16.0 jit_solution(8294322345786416411)
XLA Ops:
  0.6 9.7 %exchange.1 = (f32[14,192,128]{2,1,0:T(8,128)S(1)}, bf16[320,480]{1,0:T(8,128)(2,1)S(1)}, f32[2,48,128]{2,1,0:T(8,128)S(1)}, f32[2,48,128]{2,1,0:T(8,128)S(1)}, ...) custom-call(f32[288,128]{1,0:T(8,128)} %bitcast.10, ...), custom_call_target="tpu_custom_call" | custom-call | tf_op jit(solution)/shard_map/exchange/pallas_call | solution.py:500
  10.3 5.7 %plate.1 = (f32[288,128]{1,0:T(8,128)}, f32[288,128]{1,0:T(8,128)}, f32[88,128]{1,0:T(8,128)}) custom-call(f32[14,192,128]{2,1,0:T(8,128)S(1)} %get-tuple-element.23.refs_0_, bf16[320,480]{1,0:T(8,128)(2,1)S(1)} %get-tuple-element.24.refs_1_, f32[2,48,128]{2,1,0:T(8,128)S(1)} %get-tuple-element.25.refs_2_, f32[2,48,128]{2,1,0:T(8,128)S(1)} %get-tuple-element.26.refs_3_, ...), custom_call_target="tpu_custom_call" | custom-call | tf_op jit(solution)/shard_map/plate/pallas_call | solution.py:516

commit v5 on v4

v5 whole, which is shorter than its diff:
```python
import jax
import jax.numpy as jnp
from jax import lax
from jax.experimental import pallas as pl
from jax.experimental.pallas import tpu as pltpu
from jax.sharding import PartitionSpec as P

EMIN = 0.001
MESH = pl.DeviceIdType.MESH
F32 = jnp.float32
BF16 = jnp.bfloat16

ROWS = 8
OWN = range(3, 11)
MAIN = 14
LEFT, RIGHT = 14, 15
TILES = 16
U, S, B, D, A, LOAD, Q, PLANES = 0, 36, 48, 84, 96, 136, 144, 192
FOLD = 48
GROUP = 40
OUT = 8 * GROUP
WIDE = 6 * GROUP
DEPTH = 2 * WIDE


def banded_weights(stiff, w):
    def split(place):
        comp = (place >= 12).astype(jnp.int32) + (place >= 24).astype(jnp.int32)
        return comp, place - 12 * comp

    iota = lambda shape, d: lax.broadcasted_iota(jnp.int32, shape, d)
    group, r = iota((8, GROUP, 24), 0), iota((8, GROUP, 24), 1)
    dz = group & 1
    comp, layer = split(r)
    element = layer - dz
    real = (r < 36) & (element >= 0) & (element <= 10)
    pick = jnp.where(real & (iota((8, GROUP, 24), 2) == comp * 8 + 4 * dz + (group >> 1)), 1.0, 0.0)
    pick = pick.reshape(OUT, 24).astype(BF16)

    def columns(shape):
        q = iota(shape, len(shape) - 1)
        block = sum((q >= GROUP * k).astype(jnp.int32) for k in range(1, 12))
        s = q - GROUP * block
        dx = (block >= 6).astype(jnp.int32)
        block = block - 6 * dx
        dy = ((block == 2) | (block == 3) | (block == 5)).astype(jnp.int32)
        return (2 * dx + dy, block >= 4, s) + split(s)

    place, fine, s, comp, _ = columns((24, DEPTH))
    offset = columns((8, GROUP, DEPTH))[4] - split(iota((8, GROUP, DEPTH), 1))[1] + (iota((8, GROUP, DEPTH), 0) & 1)
    offset = offset.reshape(OUT, DEPTH)
    low = stiff - stiff.astype(BF16).astype(F32)
    full = jnp.zeros((OUT, DEPTH), F32)
    for part, value in enumerate((stiff.astype(BF16), low.astype(BF16))):
        rows = jnp.dot(pick, value, preferred_element_type=F32).astype(BF16)
        for up in (0, 1):
            here = (s < 36) & (iota((24, DEPTH), 0) == comp * 8 + 4 * up + place) & (fine == bool(part))
            spread = jnp.where(here, 1.0, 0.0).astype(BF16)
            full = full + jnp.where(offset == up, jnp.dot(rows, spread, preferred_element_type=F32), 0.0)
    w[...] = full.astype(BF16)


def roll(v, by):
    return pltpu.roll(v, by % 128, 1) if by % 128 else v


def lanes(rows):
    return lax.broadcasted_iota(jnp.int32, (rows, 128), 1)


def halves(v):
    high = v.astype(BF16).astype(F32)
    return high, v - high


def spread_halves(here, by):
    high, _ = here
    both = jnp.concatenate(here, 0).astype(BF16)
    rolled = roll(both, by)
    rolled_high = rolled.astype(F32)[0:GROUP]
    return both, rolled, jnp.concatenate([high, rolled_high], 0).astype(BF16)


def put(x, t, v):
    for k, part in enumerate(spread_halves(halves(v), 127)):
        x[t, 80 * k:80 * k + 80] = part


def put_seam(xs, n, side, v):
    high, low = halves(v)
    both = jnp.concatenate([high, low], 0).astype(BF16)
    at = 0
    for pair in ((0, 127), (120, 119)):
        two = [roll(both, by) for by in pair]
        third = jnp.concatenate([x.astype(F32)[0:GROUP] for x in two], 0).astype(BF16)
        for part in two + [third]:
            xs[n, at:at + 80, 128 * side:128 * side + 128] = part
            at += 80


def prepare(at, tile, fac, fup, srep, load):
    layer = lax.broadcasted_iota(jnp.int32, (12, 128), 0).astype(F32)
    d = tile[D:D + 12]
    f = jnp.where(d > 0.0, EMIN + (1.0 - EMIN) * (d * d * d), 0.0)
    s = tile[S:S + 12]
    zeros = lambda n: jnp.zeros((n, 128), F32)
    fac[at, 36:40] = zeros(4)
    fup[at, 36:40] = zeros(4)
    srep[at, 36:40] = zeros(4)
    load[at, 0:24] = zeros(24)
    load[at, 24:36] = jnp.where(tile[LOAD + 1:LOAD + 2] == layer, tile[LOAD:LOAD + 1], 0.0)
    load[at, 36:40] = zeros(4)
    for c in (0, 12, 24):
        fac[at, c:c + 12] = f
        fup[at, c:c + 1] = zeros(1)
        fup[at, c + 1:c + 12] = f[0:11]
        srep[at, c:c + 12] = s


def weigh(f, above, below):
    return [
        above * f[(2 * k) * GROUP:(2 * k + 1) * GROUP] + below * f[(2 * k + 1) * GROUP:(2 * k + 2) * GROUP]
        for k in range(4)
    ]


def pairs_of(w, jobs, post):
    pending = []
    for at in range(0, len(jobs), 2):
        two = jobs[at:at + 2]
        wide = [jnp.concatenate([x, y], 0) for _, x, y in two]
        wide = wide[0] if len(wide) == 1 else jnp.concatenate(wide, 1)
        f = jnp.dot(w[...], wide, preferred_element_type=F32)
        for job in pending:
            post(*job)
        pending = [(key, f[:, 128 * k:128 * k + 128]) for k, (key, _, _) in enumerate(two)]
    for job in pending:
        post(*job)


def seam_planes(es, e, near, corner, side, g, start, stop):
    lane = lanes(stop - start)
    row = ((lane + 1) & 127) >> 3
    late = ((lane + 1) & 7) >= 4
    inner, low, high = (row >= 3) & (row <= 10), row < 3, (row > 10) & (row < 14)
    by = 24 - 64 * (g >> 1) - 4 * (g & 1)
    planes = slice(FOLD * g + start, FOLD * g + stop)
    half = FOLD // 2

    def unfold(ref, first, second):
        parts = []
        if start < half:
            parts.append(roll(ref[start:min(stop, half)], by + first))
        if stop > half:
            parts.append(roll(ref[max(start, half) - half:stop - half], by + second))
        return parts[0] if len(parts) == 1 else jnp.concatenate(parts, 0)

    ghost = es[side, planes]
    for t in (0, 1, 2, 11, 12, 13):
        ghost = jnp.where(row == t, roll(e[t, planes], 8 * t + 3), ghost)
    below = unfold(corner.at[2 * side], 64, 96)
    above = unfold(corner.at[2 * side + 1], 64, 32)
    far = jnp.where(inner, roll(near[side, start:stop], by), jnp.where(low, below, jnp.where(high, above, 0.0)))
    return jnp.where(late, ghost, far) if side == 0 else jnp.where(late, far, ghost)


class Split:
    def __init__(self, ref, other, places):
        self.ref, self.other, self.places = ref, other, places

    def __getitem__(self, t):
        return self.other[self.places[t]] if t in self.places else self.ref[t]


class Maps:
    def __init__(self, w, xs, fac, fup, srep, load, acc):
        self.w, self.xs, self.fac, self.fup, self.srep, self.load, self.acc = w, xs, fac, fup, srep, load, acc
        lane = lanes(GROUP)
        self.edge = (lane == 0) | (lane == 127)
        self.from_left = ((lane + 1) & 7) >= 4

    def collect(self, t, f, corners, so_far):
        for dz in (0, 1):
            total = None if so_far is None else so_far[dz][t]
            for k in range(4):
                term = f[(2 * k + dz) * GROUP:(2 * k + dz + 1) * GROUP] * corners[k]
                total = term if total is None else total + term
            self.acc[dz][t] = total

    def seam(self, n, finish, state=None, so_far=None):
        f = jnp.dot(self.w[...], self.xs[n], preferred_element_type=F32)
        outs = []
        for side in (0, 1):
            t = LEFT + side
            part = f[:, 128 * side:128 * side + 128]
            if state is not None and side == 1:
                v = state(t)
                self.collect(t, part, [roll(v, by) for by in (0, 127, 120, 119)], so_far)
            g = weigh(part, self.fac[t], self.fup[t])
            outs.append(g[0] + roll(g[1], 1) + roll(g[2], 8) + roll(g[3], 9))
            if finish is not None:
                finish(side, outs[-1])
        return jnp.where(self.from_left, outs[0], outs[1])

    def fixed(self, t, out, seam):
        return jnp.where(self.edge, roll(seam, 125 - 8 * t), out)

    def main(self, x, elements, seam, finish, state=None, so_far=None, done=None):
        carry = None

        def node(t, above, below):
            out = above[0] + below[0] + roll(above[1] + below[1], 1)
            finish(t, self.fixed(t, out, seam))

        def post(t, f):
            nonlocal carry
            if state is not None and t in OWN:
                now, rolled = state
                self.collect(t, f, [now(t), rolled(t), now(t + 1), rolled(t + 1)], so_far)
            g = weigh(f, self.fac[t], self.fup[t])
            if done is not None and t == 10:
                node(t, g[0:2], (done[1][2], done[1][3]))
            elif carry is not None:
                node(t, g[0:2], carry)
            carry = g[2:]
            if done is not None and t == 2:
                node(3, (done[1][0], done[1][1]), carry)
                for k in range(6):
                    finish(k + 4, self.fixed(k + 4, done[0][k], seam))

        pairs_of(self.w, [(t, x[t], x[t + 1]) for t in elements], post)

    def step_u(self, t, now, before, out):
        s = self.srep[t]
        return jnp.where(s > 0.0, 2.0 * now(t) - before(t) + s * (self.load[t] - out), 0.0)

    def step_a(self, t, now, before, out):
        return 2.0 * now(t) - before(t) + self.load[t] - out


def of(ref):
    return lambda t: ref[t]


def exchange_kernel(*refs):
    sources, refs = refs[:10], refs[10:]
    e, w, mine, near, corner, es, fac, fup, srep, load, u0r, u1, u1r, u2, u2r, acc0, acc1, xz3, o3, p3 = refs[:20]
    held, (corner_out, xu0, xu1, o1, p1, f3, xs, load_sem, send_sem, recv_sem) = refs[20:30], refs[30:]
    u, b, a, q, den, step, fix, top, depth, stiff = held
    gx, gy = lax.axis_index("gx"), lax.axis_index("gy")
    nx, ny = lax.axis_size("gx"), lax.axis_size("gy")
    down, up, left, right = gx > 0, gx < nx - 1, gy > 0, gy < ny - 1
    sides = {
        (-1, 0): down, (1, 0): up, (0, -1): left, (0, 1): right,
        (-1, -1): down & left, (1, -1): up & left, (-1, 1): down & right, (1, 1): up & right,
    }
    barrier = pltpu.get_barrier_semaphore()
    for (dx, dy), there in sides.items():
        @pl.when(there)
        def _(dx=dx, dy=dy):
            pl.semaphore_signal(barrier, inc=1, device_id=(gx + dx, gy + dy), device_id_type=MESH)

    loads = [pltpu.make_async_copy(src, dst, load_sem.at[k]) for k, (src, dst) in enumerate(zip(sources, held))]
    for c in loads:
        c.start()
    zeros = lambda n: jnp.zeros((n, 128), F32)
    empty = {0: ((0, 32), (48, 80), (136, PLANES)), 1: ((48, 80), (184, PLANES)), 13: ((48, 96), (136, PLANES))}
    for t in (0, 1, 2, 11, 12, 13):
        for start, stop in empty.get(t, ((184, PLANES),)):
            e[t, start:stop] = zeros(stop - start)

    @pl.when(jnp.logical_not(down))
    def _():
        for t in (0, 1, 2):
            e[t] = zeros(PLANES)

    @pl.when(jnp.logical_not(up))
    def _():
        for t in (11, 12, 13):
            e[t] = zeros(PLANES)

    for k, dy in enumerate((-1, 1)):
        @pl.when(jnp.logical_not(sides[0, dy]))
        def _(k=k):
            near[k] = zeros(FOLD)

        for j, dx in enumerate((-1, 1)):
            @pl.when(jnp.logical_not(sides[dx, dy]))
            def _(k=k, j=j):
                corner[2 * k + j] = zeros(FOLD // 2)

    for c in loads:
        c.wait()
    for r in range(ROWS):
        t = r + 3
        free = 1.0 - fix[pl.ds(r, 12, stride=8), :].astype(F32)
        e[t, U:U + 36] = u[pl.ds(r, 36, stride=8), :]
        e[t, S:S + 12] = free * step[pl.ds(r, 12, stride=8), :]
        e[t, B:B + 36] = b[pl.ds(r, 36, stride=8), :]
        e[t, D:D + 11] = den[pl.ds(r, 11, stride=8), :]
        e[t, D + 11:D + 12] = zeros(1)
        e[t, A:A + 36] = a[pl.ds(r, 36, stride=8), :]
        e[t, A + 36:A + 40] = zeros(4)
        e[t, LOAD:LOAD + 1] = top[r:r + 1, :]
        e[t, LOAD + 1:LOAD + 2] = depth[r:r + 1, :].astype(F32)
        e[t, LOAD + 2:LOAD + 8] = zeros(6)
        e[t, Q:Q + 36] = q[pl.ds(r, 36, stride=8), :]
        e[t, Q + 36:PLANES] = zeros(PLANES - Q - 36)

    lane = lanes(FOLD)
    first_cols, last_cols = zeros(FOLD), zeros(FOLD)
    for g in range(4):
        for r in range(ROWS):
            slot = 16 * (g >> 1) + 2 * r + (g & 1)
            v = roll(e[r + 3, FOLD * g:FOLD * g + FOLD], 4 * slot + 3)
            first_cols = jnp.where(((lane - 3) & 127) >> 2 == slot, v, first_cols)
            last_cols = jnp.where(((lane + 1) & 127) >> 2 == slot, v, last_cols)
    mine[0] = first_cols
    mine[1] = last_cols
    half = FOLD // 2
    lane = lanes(half)
    for k, cols in enumerate((first_cols, last_cols)):
        low = ((lane - 3 + 4 * k) & 63) < 32
        corner_out[2 * k] = jnp.where(low, cols[0:half], roll(cols[half:FOLD], 32))
        corner_out[2 * k + 1] = jnp.where(low, roll(cols[half:FOLD], -32), cols[0:half])

    pl.semaphore_wait(barrier, sum(there.astype(jnp.int32) for there in sides.values()))

    def rows(to, start, stop, first, last):
        if to == 1:
            src, dst = e.at[11 - last:11 - first, start:stop], e.at[3 - last:3 - first, start:stop]
        else:
            src, dst = e.at[3 + first:3 + last, start:stop], e.at[11 + first:11 + last, start:stop]
        return ((to, 0), src, dst)

    early = [
        ((-1, -1), corner_out.at[0], corner.at[3]),
        ((1, -1), corner_out.at[1], corner.at[2]),
        ((-1, 1), corner_out.at[2], corner.at[1]),
        ((1, 1), corner_out.at[3], corner.at[0]),
        ((0, -1), mine.at[0], near.at[1]),
        ((0, 1), mine.at[1], near.at[0]),
        rows(-1, 0, 96, 0, 2),
        rows(1, 0, 48, 0, 2),
        rows(1, 80, 96, 0, 3),
        rows(1, 32, 48, 2, 3),
        rows(1, 48, 80, 0, 1),
        rows(-1, 0, 48, 2, 3),
        rows(-1, 136, 144, 0, 2),
        rows(1, 136, 144, 0, 2),
    ]
    later = [
        rows(-1, 96, 136, 0, 3),
        rows(1, 96, 136, 0, 3),
        rows(-1, 144, 184, 0, 2),
        rows(1, 144, 184, 0, 2),
    ]
    copies = []
    for k, (to, src, dst) in enumerate(early + later):
        copies.append((to, pltpu.make_async_remote_copy(
            src_ref=src, dst_ref=dst, send_sem=send_sem.at[k], recv_sem=recv_sem.at[k],
            device_id=(gx + to[0], gy + to[1]), device_id_type=MESH,
        )))
    for to, c in copies:
        @pl.when(sides[to])
        def _(c=c):
            c.start()

    def arrived(some):
        for (dx, dy), c in some:
            @pl.when(sides[-dx, -dy])
            def _(c=c):
                c.wait_recv()

    banded_weights(stiff[...], w)
    arrays = (fac, fup, srep, load)
    for t in OWN:
        prepare(t, e.at[t], *arrays)
        now = e[t, U:U + GROUP]
        u0r[t] = roll(now, 127)
        put(xu0, t, now)
        put(xz3, t - 3, srep[t] * e[t, A:A + GROUP])
    lane = lanes(FOLD)
    inner = (((lane + 1) & 127) >> 3 >= 3) & (((lane + 1) & 127) >> 3 <= 10)
    late = ((lane + 1) & 7) >= 4
    for g in range(4):
        by = 24 - 64 * (g >> 1) - 4 * (g & 1)
        for side in (0, 1):
            es[side, FOLD * g:FOLD * g + FOLD] = jnp.where(inner & (late == (side == 0)), roll(mine[side], by), 0.0)

    carry = {}

    def post(key, f):
        kind, t = key
        out, pieces = ((o1, p1), (o3, p3))[kind]
        if kind:
            f3[t - 3] = f
        g = weigh(f, fac[t], fup[t])
        if t == 3:
            pieces[0], pieces[1] = g[0], g[1]
        else:
            out[t - 4] = g[0] + carry[kind][0] + roll(g[1] + carry[kind][1], 1)
        if t == 9:
            pieces[2], pieces[3] = g[2], g[3]
        carry[kind] = g[2:]

    jobs = [((0, t), xu0[t], xu0[t + 1]) for t in range(3, 10)] + [((1, t), xz3[t - 3], xz3[t - 2]) for t in range(3, 10)]
    pairs_of(w, jobs, post)

    arrived(copies[:len(early)])
    maps = Maps(w, xs, fac, fup, srep, load, (acc0, acc1))

    def tile_rows(at):
        return lambda t: es[t - LEFT, at:at + GROUP] if t >= LEFT else e[t, at:at + GROUP]

    u_now, u_before = tile_rows(U), tile_rows(B)
    for side in (0, 1):
        for g, start, stop in ((0, 0, 48), (1, 0, 48), (2, 40, 48)):
            es[side, FOLD * g + start:FOLD * g + stop] = seam_planes(es, e, near, corner, side, g, start, stop)
        prepare(LEFT + side, es.at[side], *arrays)
        put_seam(xs, 0, side, u_now(LEFT + side))

    def seam_u1(side, out):
        v = maps.step_u(LEFT + side, u_now, u_before, out)
        u1[LEFT + side] = v
        put_seam(xs, 1, side, v)

    def seam_u2(side, out):
        u2[LEFT + side] = maps.step_u(LEFT + side, of(u1), u_now, out)

    def main_u1(t, out):
        v = maps.step_u(t, u_now, u_before, out)
        u1[t] = v
        if 3 <= t <= 11:
            u1r[t] = roll(v, 127)
        put(xu1, t, v)

    def main_u2(t, out):
        v = maps.step_u(t, of(u1), u_now, out)
        u2[t] = v
        u2r[t] = roll(v, 127)

    for t in (1, 2, 11, 12):
        prepare(t, e.at[t], *arrays)
    u0r[11] = roll(u_now(11), 127)
    for t in (1, 2, 11, 12, 13):
        put(xu0, t, u_now(t))
    k1 = maps.seam(0, seam_u1)
    k2 = maps.seam(1, seam_u2)
    maps.main(xu0, (1, 2, 10, 11, 12), k1, main_u1, done=(o1, p1))
    maps.main(xu1, range(2, 12), k2, main_u2)
    for t in range(3, 10):
        maps.collect(t, f3[t - 3], [u2[t], u2r[t], u2[t + 1], u2r[t + 1]], None)

    arrived(copies[len(early):])
    for to, c in copies:
        @pl.when(sides[to])
        def _(c=c):
            c.wait_send()


def plate_kernel(*refs):
    e, w, mine, near, corner, es, fac_in, fup_in, srep_in, load_in, u0r, u1, u1r, u2, u2r, acc0_in, acc1_in, xz3_in, o3, p3 = refs[:20]
    first_out, second_out, sens_out = refs[20:23]
    fac_more, fup_more, srep_more, load_more, xz3, acc0, acc1, a2, a1, xz2, xz1, xs, ea, first, second, sens, out_sem = refs[23:]
    ends = {0: 0, 13: 1}
    fac, fup, srep, load = (
        Split(x, y, ends) for x, y in ((fac_in, fac_more), (fup_in, fup_more), (srep_in, srep_more), (load_in, load_more))
    )
    xz = Split(xz3, xz3_in, {t: t - 3 for t in OWN})
    maps = Maps(w, xs, fac, fup, srep, load, (acc0, acc1))
    before = Split(acc0, acc0_in, {t: t for t in range(3, 10)}), Split(acc1, acc1_in, {t: t for t in range(3, 10)})

    def tile_rows(at, seams):
        return lambda t: seams[t - LEFT, at:at + GROUP] if t >= LEFT else e[t, at:at + GROUP]

    u_now, adj_next, adj_later = tile_rows(U, es), tile_rows(A, ea), tile_rows(Q, ea)
    for side in (0, 1):
        for g in (2, 3):
            ea[side, FOLD * g:FOLD * g + 40] = seam_planes(es, e, near, corner, side, g, 0, 40)
        put_seam(xs, 0, side, srep[LEFT + side] * adj_next(LEFT + side))

    def seam_a2(side, out):
        v = maps.step_a(LEFT + side, adj_next, adj_later, out)
        a2[LEFT + side] = v
        put_seam(xs, 1, side, srep[LEFT + side] * v)

    def seam_a1(side, out):
        v = maps.step_a(LEFT + side, of(a2), adj_next, out)
        put_seam(xs, 2, side, srep[LEFT + side] * v)

    def main_a2(t, out):
        v = maps.step_a(t, adj_next, adj_later, out)
        a2[t] = v
        put(xz2, t, srep[t] * v)

    def main_a1(t, out):
        v = maps.step_a(t, of(a2), adj_next, out)
        a1[t] = v
        put(xz1, t, srep[t] * v)
        if t in OWN:
            second[pl.ds(t - 3, 36, stride=8), :] = v[0:36]

    def main_a0(t, out):
        first[pl.ds(t - 3, 36, stride=8), :] = maps.step_a(t, of(a1), of(a2), out)[0:36]

    for t, at in ends.items():
        prepare(at, e.at[t], fac_more, fup_more, srep_more, load_more)
    for t in (0, 1, 2, 11, 12, 13):
        put(xz3, t, srep[t] * adj_next(t))
    k3 = maps.seam(0, seam_a2, of(u2))
    k4 = maps.seam(1, seam_a1, of(u1), (acc0, acc1))
    k5 = maps.seam(2, None, u_now, (acc0, acc1))
    maps.main(xz, (0, 1, 2, 10, 11, 12), k3, main_a2, (of(u2), of(u2r)), None, done=(o3, p3))
    maps.main(xz2, range(1, 12), k4, main_a1, (of(u1), of(u1r)), before)
    copy_second = pltpu.make_async_copy(second, second_out, out_sem.at[1])
    copy_second.start()
    maps.main(xz1, range(2, 11), k5, main_a0, (u_now, of(u0r)), (acc0, acc1))
    copy_first = pltpu.make_async_copy(first, first_out, out_sem.at[0])
    copy_first.start()

    def total(t):
        return sum(acc0[t, c:c + 11] + acc1[t, c + 1:c + 12] for c in (0, 12, 24))

    seam = total(RIGHT)
    last = lanes(11) == 127
    for r in range(ROWS):
        t = r + 3
        d = e[t, D:D + 11]
        both = jnp.where(last, roll(seam, 125 - 8 * t), total(t))
        sens[pl.ds(r, 11, stride=8), :] = (-3.0 * (1.0 - EMIN)) * (d * d) * both
    copy_sens = pltpu.make_async_copy(sens, sens_out, out_sem.at[2])
    copy_sens.start()
    copy_second.wait()
    copy_first.wait()
    copy_sens.wait()


def local(u_now, u_prev, adjoint_next, adjoint_later, density, step_factor, fixed_nodes, load_top, load_depth, brick_stiffness):
    vmem = pl.BlockSpec(memory_space=pltpu.VMEM)
    hbm = pl.BlockSpec(memory_space=pltpu.HBM)
    flat = lambda x: x.reshape(-1, 128)
    sources = (
        flat(u_now), flat(u_prev), flat(adjoint_next), flat(adjoint_later), flat(density), flat(step_factor),
        flat(fixed_nodes), load_top, load_depth, brick_stiffness,
    )
    f32 = lambda *shape: jax.ShapeDtypeStruct(shape + (128,), F32)
    bf16 = lambda *shape: jax.ShapeDtypeStruct(shape, BF16)
    passed = (
        [f32(MAIN, PLANES), bf16(OUT, DEPTH), f32(2, FOLD), f32(2, FOLD), f32(4, FOLD // 2), f32(2, PLANES)]
        + [f32(TILES, GROUP)] * 11 + [bf16(ROWS, WIDE, 128), f32(6, GROUP), f32(4, GROUP)]
    )
    tiles = lambda n, rows, kind: pltpu.VMEM((n, rows, 128), kind)
    gathered = pl.pallas_call(
        exchange_kernel,
        out_shape=passed,
        in_specs=[hbm] * 10,
        out_specs=[vmem] * len(passed),
        scratch_shapes=[pltpu.VMEM(x.shape, x.dtype) for x in sources] + [
            tiles(4, FOLD // 2, F32),
            tiles(MAIN, WIDE, BF16),
            tiles(MAIN, WIDE, BF16),
            tiles(6, GROUP, F32),
            tiles(4, GROUP, F32),
            tiles(7, OUT, F32),
            pltpu.VMEM((2, DEPTH, 256), BF16),
            pltpu.SemaphoreType.DMA((10,)),
            pltpu.SemaphoreType.DMA((18,)),
            pltpu.SemaphoreType.DMA((18,)),
        ],
        compiler_params=pltpu.CompilerParams(collective_id=0, has_side_effects=True, vmem_limit_bytes=32 * 2**20),
        name="exchange",
    )(*(pltpu.with_memory_space_constraint(x, pltpu.HBM) for x in sources))
    results = ((36 * ROWS, 128), (36 * ROWS, 128), (11 * ROWS, 128))
    first, second, sens = pl.pallas_call(
        plate_kernel,
        out_shape=tuple(jax.ShapeDtypeStruct(shape, F32) for shape in results),
        in_specs=[vmem] * len(passed),
        out_specs=(hbm,) * 3,
        scratch_shapes=[tiles(2, GROUP, F32)] * 4 + [tiles(MAIN, WIDE, BF16)] + [tiles(TILES, GROUP, F32)] * 4
        + [tiles(MAIN, WIDE, BF16)] * 2 + [pltpu.VMEM((3, DEPTH, 256), BF16), tiles(2, PLANES, F32)]
        + [pltpu.VMEM(shape, F32) for shape in results]
        + [pltpu.SemaphoreType.DMA((3,))],
        compiler_params=pltpu.CompilerParams(vmem_limit_bytes=32 * 2**20),
        name="plate",
    )(*gathered)
    return (
        first.reshape(u_now.shape),
        second.reshape(u_now.shape),
        sens.reshape(density.shape),
    )


def solution(mesh):
    in_specs = (
        P(None, None, "gx", "gy"),
        P(None, None, "gx", "gy"),
        P(None, None, "gx", "gy"),
        P(None, None, "gx", "gy"),
        P(None, "gx", "gy"),
        P(None, "gx", "gy"),
        P(None, "gx", "gy"),
        P("gx", "gy"),
        P("gx", "gy"),
        P(),
    )
    out_specs = (P(None, None, "gx", "gy"), P(None, None, "gx", "gy"), P(None, "gx", "gy"))
    return jax.shard_map(local, mesh=mesh, in_specs=in_specs, out_specs=out_specs, check_vma=False)
```

time: 16.3 us -> 16.7 us (1.025)
  the two profiles are of different devices: /device:TPU:56 before, /device:TPU:65 now
where the time goes in v5:
time: 16.7 us; the launch traced here: 16.5 us
  Pallas kernels  15.9 us (95%)
  between operations  0.64 us (4%)
    pallas_call x1, Pallas kernels, local(): pl.pallas_call(exchange_kernel, out_shape=passed, in_specs=[hbm] * 10, ou...  11.8 us
    pallas_call x1, Pallas kernels, local(): pl.pallas_call(plate_kernel, out_shape=tuple((jax.ShapeDtypeStruct(shape,...  4.06 us

profile of v5, /device:TPU:65, one launch (start us, length us, event | category | flops | bytes accessed | tf_op | source)
XLA Modules:
  0.0 16.5 jit_solution(17615197281486718913)
XLA Ops:
  0.6 11.8 %exchange.1 = (f32[14,192,128]{2,1,0:T(8,128)S(1)}, bf16[320,480]{1,0:T(8,128)(2,1)S(1)}, f32[2,48,128]{2,1,0:T(8,128)S(1)}, f32[2,48,128]{2,1,0:T(8,128)S(1)}, ...) custom-call(f32[288,128]{1,0:T(8,128)} %bitcast.10, ...), custom_call_target="tpu_custom_call" | custom-call | tf_op jit(solution)/shard_map/exchange/pallas_call | solution.py:554
  12.5 4.1 %plate.1 = (f32[288,128]{1,0:T(8,128)}, f32[288,128]{1,0:T(8,128)}, f32[88,128]{1,0:T(8,128)}) custom-call(f32[14,192,128]{2,1,0:T(8,128)S(1)} %get-tuple-element.26.refs_0_, bf16[320,480]{1,0:T(8,128)(2,1)S(1)} %get-tuple-element.27.refs_1_, f32[2,48,128]{2,1,0:T(8,128)S(1)} %get-tuple-element.28.refs_2_, f32[2,48,128]{2,1,0:T(8,128)S(1)} %get-tuple-element.29.refs_3_, ...), custom_call_target="tpu_custom_call" | custom-call | tf_op jit(solution)/shard_map/plate/pallas_call | solution.py:575

commit v6 on v5

v6 whole, which is shorter than its diff:
```python
import jax
import jax.numpy as jnp
from jax import lax
from jax.experimental import pallas as pl
from jax.experimental.pallas import tpu as pltpu
from jax.sharding import PartitionSpec as P

EMIN = 0.001
MESH = pl.DeviceIdType.MESH
F32 = jnp.float32
BF16 = jnp.bfloat16

ROWS = 8
OWN = range(3, 11)
DEEP_1, DEEP_2 = range(3, 10), range(4, 9)
ONCE, TWICE = range(4, 10), range(5, 9)
MAIN = 14
LEFT, RIGHT = 14, 15
TILES = 16
U, S, A, D, B, LOAD, Q, PLANES = 0, 36, 48, 84, 96, 132, 136, 192
FOLD = 48
GROUP = 40
OUT = 8 * GROUP
WIDE = 6 * GROUP
DEPTH = 2 * WIDE


def banded_weights(stiff, w):
    def split(place):
        comp = (place >= 12).astype(jnp.int32) + (place >= 24).astype(jnp.int32)
        return comp, place - 12 * comp

    iota = lambda shape, d: lax.broadcasted_iota(jnp.int32, shape, d)
    group, r = iota((8, GROUP, 24), 0), iota((8, GROUP, 24), 1)
    dz = group & 1
    comp, layer = split(r)
    element = layer - dz
    real = (r < 36) & (element >= 0) & (element <= 10)
    pick = jnp.where(real & (iota((8, GROUP, 24), 2) == comp * 8 + 4 * dz + (group >> 1)), 1.0, 0.0)
    pick = pick.reshape(OUT, 24).astype(BF16)

    def columns(shape):
        q = iota(shape, len(shape) - 1)
        block = sum((q >= GROUP * k).astype(jnp.int32) for k in range(1, 12))
        s = q - GROUP * block
        dx = (block >= 6).astype(jnp.int32)
        block = block - 6 * dx
        dy = ((block == 2) | (block == 3) | (block == 5)).astype(jnp.int32)
        return (2 * dx + dy, block >= 4, s) + split(s)

    place, fine, s, comp, _ = columns((24, DEPTH))
    offset = columns((8, GROUP, DEPTH))[4] - split(iota((8, GROUP, DEPTH), 1))[1] + (iota((8, GROUP, DEPTH), 0) & 1)
    offset = offset.reshape(OUT, DEPTH)
    low = stiff - stiff.astype(BF16).astype(F32)
    full = jnp.zeros((OUT, DEPTH), F32)
    for part, value in enumerate((stiff.astype(BF16), low.astype(BF16))):
        rows = jnp.dot(pick, value, preferred_element_type=F32).astype(BF16)
        for up in (0, 1):
            here = (s < 36) & (iota((24, DEPTH), 0) == comp * 8 + 4 * up + place) & (fine == bool(part))
            spread = jnp.where(here, 1.0, 0.0).astype(BF16)
            full = full + jnp.where(offset == up, jnp.dot(rows, spread, preferred_element_type=F32), 0.0)
    w[...] = full.astype(BF16)


def roll(v, by):
    return pltpu.roll(v, by % 128, 1) if by % 128 else v


def lanes(rows):
    return lax.broadcasted_iota(jnp.int32, (rows, 128), 1)


def halves(v):
    high = v.astype(BF16).astype(F32)
    return high, v - high


def spread_halves(here, by):
    high, _ = here
    both = jnp.concatenate(here, 0).astype(BF16)
    rolled = roll(both, by)
    rolled_high = rolled.astype(F32)[0:GROUP]
    return both, rolled, jnp.concatenate([high, rolled_high], 0).astype(BF16)


def put(x, t, v):
    for k, part in enumerate(spread_halves(halves(v), 127)):
        x[t, 80 * k:80 * k + 80] = part


def put_seam(xs, n, side, v):
    high, low = halves(v)
    both = jnp.concatenate([high, low], 0).astype(BF16)
    at = 0
    for pair in ((0, 127), (120, 119)):
        two = [roll(both, by) for by in pair]
        third = jnp.concatenate([x.astype(F32)[0:GROUP] for x in two], 0).astype(BF16)
        for part in two + [third]:
            xs[n, at:at + 80, 128 * side:128 * side + 128] = part
            at += 80


def prepare(at, tile, fac, fup, srep, load):
    layer = lax.broadcasted_iota(jnp.int32, (12, 128), 0).astype(F32)
    d = tile[D:D + 12]
    f = jnp.where(d > 0.0, EMIN + (1.0 - EMIN) * (d * d * d), 0.0)
    s = tile[S:S + 12]
    zeros = lambda n: jnp.zeros((n, 128), F32)
    fac[at, 36:40] = zeros(4)
    fup[at, 36:40] = zeros(4)
    srep[at, 36:40] = zeros(4)
    load[at, 0:24] = zeros(24)
    load[at, 24:36] = jnp.where(tile[LOAD + 1:LOAD + 2] == layer, tile[LOAD:LOAD + 1], 0.0)
    load[at, 36:40] = zeros(4)
    for c in (0, 12, 24):
        fac[at, c:c + 12] = f
        fup[at, c:c + 1] = zeros(1)
        fup[at, c + 1:c + 12] = f[0:11]
        srep[at, c:c + 12] = s


def weigh(f, above, below):
    return [
        above * f[(2 * k) * GROUP:(2 * k + 1) * GROUP] + below * f[(2 * k + 1) * GROUP:(2 * k + 2) * GROUP]
        for k in range(4)
    ]


def pairs_of(w, jobs, post):
    pending = []
    for at in range(0, len(jobs), 2):
        two = jobs[at:at + 2]
        wide = [jnp.concatenate([x, y], 0) for _, x, y in two]
        wide = wide[0] if len(wide) == 1 else jnp.concatenate(wide, 1)
        f = jnp.dot(w[...], wide, preferred_element_type=F32)
        for job in pending:
            post(*job)
        pending = [(key, f[:, 128 * k:128 * k + 128]) for k, (key, _, _) in enumerate(two)]
    for job in pending:
        post(*job)


def seam_planes(es, e, near, corner, side, g, start, stop):
    lane = lanes(stop - start)
    row = ((lane + 1) & 127) >> 3
    late = ((lane + 1) & 7) >= 4
    inner, low, high = (row >= 3) & (row <= 10), row < 3, (row > 10) & (row < 14)
    by = 24 - 64 * (g >> 1) - 4 * (g & 1)
    planes = slice(FOLD * g + start, FOLD * g + stop)
    half = FOLD // 2

    def unfold(ref, first, second):
        parts = []
        if start < half:
            parts.append(roll(ref[start:min(stop, half)], by + first))
        if stop > half:
            parts.append(roll(ref[max(start, half) - half:stop - half], by + second))
        return parts[0] if len(parts) == 1 else jnp.concatenate(parts, 0)

    ghost = es[side, planes]
    for t in (0, 1, 2, 11, 12, 13):
        ghost = jnp.where(row == t, roll(e[t, planes], 8 * t + 3), ghost)
    below = unfold(corner.at[2 * side], 64, 96)
    above = unfold(corner.at[2 * side + 1], 64, 32)
    far = jnp.where(inner, roll(near[side, start:stop], by), jnp.where(low, below, jnp.where(high, above, 0.0)))
    return jnp.where(late, ghost, far) if side == 0 else jnp.where(late, far, ghost)


class Tiles:
    def __init__(self, own, ref, more):
        self.own, self.ref, self.more = own, ref, more

    def __getitem__(self, t):
        return self.ref[t] if t in self.own else self.more[t]

    def __setitem__(self, t, v):
        self.more[t] = v


class Fresh:
    def __init__(self, own, ref):
        self.own, self.ref = own, ref

    def __getitem__(self, t):
        return self.ref[t] if t in self.own else None


class Field:
    def __init__(self, tile, at):
        self.tile, self.at = tile, at

    def __getitem__(self, t):
        return self.tile(t, self.at)


class Maps:
    def __init__(self, w, fac, fup, srep, load, acc):
        self.w, self.fac, self.fup, self.srep, self.load, self.acc = w, fac, fup, srep, load, acc

    def collect(self, t, f, corners, so_far):
        for dz in (0, 1):
            total = None if so_far is None else so_far[dz][t]
            for k in range(4):
                term = f[(2 * k + dz) * GROUP:(2 * k + dz + 1) * GROUP] * corners[k]
                total = term if total is None else total + term
            self.acc[dz][t] = total

    def seam_corners(self, v):
        return [roll(v, by) for by in (0, 127, 120, 119)]

    def seam(self, x, finish, state=None, so_far=None, forces=None):
        f = jnp.dot(self.w[...], x[...], preferred_element_type=F32)
        for side in (0, 1):
            t = LEFT + side
            part = f[:, 128 * side:128 * side + 128]
            if forces is not None:
                forces(t, part)
            if state is not None:
                v = state(t)
                self.collect(t, part, self.seam_corners(v), so_far)
            g = weigh(part, self.fac[t], self.fup[t])
            finish(t, g[0] + roll(g[1], 1) + roll(g[2], 8) + roll(g[3], 9))

    def main(self, x, elements, finish, state=None, so_far=None, pieces=None, keep=None, forces=None):
        carry = None
        first, last, ends = pieces if pieces is not None else (None, None, None)

        def node(t, above, below):
            finish(t, above[0] + below[0] + roll(above[1] + below[1], 1))

        def post(t, f):
            nonlocal carry
            if forces is not None:
                forces(t, f)
            if state is not None and t in OWN:
                now, rolled = state
                self.collect(t, f, [now[t], rolled[t], now[t + 1], rolled[t + 1]], so_far)
            g = weigh(f, self.fac[t], self.fup[t])
            if keep is not None and t == elements[0]:
                keep[0], keep[1] = g[0], g[1]
            if ends is not None and t == last + 1:
                node(t, g[0:2], (ends[2], ends[3]))
            elif carry is not None:
                node(t, g[0:2], carry)
            carry = g[2:]
            if ends is not None and t == first - 1:
                node(first, (ends[0], ends[1]), carry)
            if keep is not None and t == elements[-1]:
                keep[2], keep[3] = g[2], g[3]

        pairs_of(self.w, [(t, x[t], x[t + 1]) for t in elements], post)

    def step_u(self, t, now, before, out):
        s = self.srep[t]
        return jnp.where(s > 0.0, 2.0 * now - before + s * (self.load[t] - out), 0.0)

    def step_a(self, t, now, before, out):
        return 2.0 * now - before + self.load[t] - out


def exchange_kernel(*refs):
    sources, refs = refs[:10], refs[10:]
    e, w, near, corner, es, fac, fup, srep, load, u0r, u1, u1r, u2, a2, a1, acc0, acc1 = refs[:17]
    xu0, xz3, xu1, xz2, p1, p2, p3, p4, f3 = refs[17:26]
    held, (mine, corner_out, load_sem, send_sem, recv_sem) = refs[26:36], refs[36:]
    u, b, a, q, den, step, fix, top, depth, stiff = held
    gx, gy = lax.axis_index("gx"), lax.axis_index("gy")
    nx, ny = lax.axis_size("gx"), lax.axis_size("gy")
    down, up, left, right = gx > 0, gx < nx - 1, gy > 0, gy < ny - 1
    sides = {
        (-1, 0): down, (1, 0): up, (0, -1): left, (0, 1): right,
        (-1, -1): down & left, (1, -1): up & left, (-1, 1): down & right, (1, 1): up & right,
    }
    barrier = pltpu.get_barrier_semaphore()
    for (dx, dy), there in sides.items():
        @pl.when(there)
        def _(dx=dx, dy=dy):
            pl.semaphore_signal(barrier, inc=1, device_id=(gx + dx, gy + dy), device_id_type=MESH)

    loads = [pltpu.make_async_copy(src, dst, load_sem.at[k]) for k, (src, dst) in enumerate(zip(sources, held))]
    for c in loads:
        c.start()
    zeros = lambda n: jnp.zeros((n, 128), F32)
    e[0, 0:32] = zeros(32)
    e[0, 96:PLANES] = zeros(PLANES - 96)
    e[1, 96:128] = zeros(32)
    for t in (1, 2, 11, 12):
        e[t, 176:PLANES] = zeros(PLANES - 176)
    e[13, 88:PLANES] = zeros(PLANES - 88)

    @pl.when(jnp.logical_not(down))
    def _():
        for t in (0, 1, 2):
            e[t] = zeros(PLANES)

    @pl.when(jnp.logical_not(up))
    def _():
        for t in (11, 12, 13):
            e[t] = zeros(PLANES)

    for k, dy in enumerate((-1, 1)):
        @pl.when(jnp.logical_not(sides[0, dy]))
        def _(k=k):
            near[k] = zeros(FOLD)

        for j, dx in enumerate((-1, 1)):
            @pl.when(jnp.logical_not(sides[dx, dy]))
            def _(k=k, j=j):
                corner[2 * k + j] = zeros(FOLD // 2)

    for c in loads:
        c.wait()
    for r in range(ROWS):
        t = r + 3
        free = 1.0 - fix[pl.ds(r, 12, stride=8), :].astype(F32)
        e[t, U:U + 36] = u[pl.ds(r, 36, stride=8), :]
        e[t, S:S + 12] = free * step[pl.ds(r, 12, stride=8), :]
        e[t, A:A + 36] = a[pl.ds(r, 36, stride=8), :]
        e[t, D:D + 11] = den[pl.ds(r, 11, stride=8), :]
        e[t, D + 11:D + 12] = zeros(1)
        e[t, B:B + 36] = b[pl.ds(r, 36, stride=8), :]
        e[t, LOAD:LOAD + 1] = top[r:r + 1, :]
        e[t, LOAD + 1:LOAD + 2] = depth[r:r + 1, :].astype(F32)
        e[t, LOAD + 2:LOAD + 4] = zeros(2)
        e[t, Q:Q + 36] = q[pl.ds(r, 36, stride=8), :]
        e[t, Q + 36:PLANES] = zeros(PLANES - Q - 36)

    lane = lanes(FOLD)
    first_cols, last_cols = zeros(FOLD), zeros(FOLD)
    for g in range(4):
        for r in range(ROWS):
            slot = 16 * (g >> 1) + 2 * r + (g & 1)
            v = roll(e[r + 3, FOLD * g:FOLD * g + FOLD], 4 * slot + 3)
            first_cols = jnp.where(((lane - 3) & 127) >> 2 == slot, v, first_cols)
            last_cols = jnp.where(((lane + 1) & 127) >> 2 == slot, v, last_cols)
    mine[0] = first_cols
    mine[1] = last_cols
    half = FOLD // 2
    lane = lanes(half)
    for k, cols in enumerate((first_cols, last_cols)):
        low = ((lane - 3 + 4 * k) & 63) < 32
        corner_out[2 * k] = jnp.where(low, cols[0:half], roll(cols[half:FOLD], 32))
        corner_out[2 * k + 1] = jnp.where(low, roll(cols[half:FOLD], -32), cols[0:half])

    pl.semaphore_wait(barrier, sum(there.astype(jnp.int32) for there in sides.values()))
    plan = [
        ((-1, -1), corner_out.at[0], corner.at[3]),
        ((1, -1), corner_out.at[1], corner.at[2]),
        ((-1, 1), corner_out.at[2], corner.at[1]),
        ((1, 1), corner_out.at[3], corner.at[0]),
        ((0, -1), mine.at[0], near.at[1]),
        ((0, 1), mine.at[1], near.at[0]),
        ((-1, 0), e.at[3:5, 0:176], e.at[11:13, 0:176]),
        ((1, 0), e.at[9:11, 0:96], e.at[1:3, 0:96]),
        ((1, 0), e.at[9:11, 128:176], e.at[1:3, 128:176]),
        ((-1, 0), e.at[5, 0:88], e.at[13, 0:88]),
        ((1, 0), e.at[8, 32:96], e.at[0, 32:96]),
        ((1, 0), e.at[10, 96:128], e.at[2, 96:128]),
    ]
    copies = []
    for k, ((dx, dy), src, dst) in enumerate(plan):
        copies.append(((dx, dy), pltpu.make_async_remote_copy(
            src_ref=src, dst_ref=dst, send_sem=send_sem.at[k], recv_sem=recv_sem.at[k],
            device_id=(gx + dx, gy + dy), device_id_type=MESH,
        )))
    for to, c in copies:
        @pl.when(sides[to])
        def _(c=c):
            c.start()

    banded_weights(stiff[...], w)
    for t in OWN:
        prepare(t, e.at[t], fac, fup, srep, load)
        now = e[t, U:U + GROUP]
        u0r[t] = roll(now, 127)
        put(xu0, t, now)
        put(xz3, t, srep[t] * e[t, A:A + GROUP])
    maps = Maps(w, fac, fup, srep, load, (acc0, acc1))

    def main_u1(t, out):
        v = maps.step_u(t, e[t, U:U + GROUP], e[t, B:B + GROUP], out)
        u1[t] = v
        u1r[t] = roll(v, 127)
        put(xu1, t, v)

    def main_a2(t, out):
        v = maps.step_a(t, e[t, A:A + GROUP], e[t, Q:Q + GROUP], out)
        a2[t] = v
        put(xz2, t, srep[t] * v)

    def main_u2(t, out):
        u2[t] = maps.step_u(t, u1[t], e[t, U:U + GROUP], out)

    def main_a1(t, out):
        a1[t] = maps.step_a(t, a2[t], e[t, A:A + GROUP], out)

    def keep_forces(t, f):
        f3[t - 3] = f

    maps.main(xu0, DEEP_1, main_u1, keep=p1)
    maps.main(xz3, DEEP_1, main_a2, keep=p3, forces=keep_forces)
    maps.main(xu1, DEEP_2, main_u2, keep=p2)
    maps.main(xz2, DEEP_2, main_a1, (u1, u1r), None, keep=p4)
    lane = lanes(FOLD)
    inner = (((lane + 1) & 127) >> 3 >= 3) & (((lane + 1) & 127) >> 3 <= 10)
    late = ((lane + 1) & 7) >= 4
    for g in range(4):
        by = 24 - 64 * (g >> 1) - 4 * (g & 1)
        for side in (0, 1):
            es[side, FOLD * g:FOLD * g + FOLD] = jnp.where(inner & (late == (side == 0)), roll(mine[side], by), 0.0)

    for (dx, dy), c in copies:
        @pl.when(sides[-dx, -dy])
        def _(c=c):
            c.wait_recv()
    for to, c in copies:
        @pl.when(sides[to])
        def _(c=c):
            c.wait_send()


def plate_kernel(*refs):
    e, w, near, corner, es, fac_in, fup_in, srep_in, load_in, u0r_in, u1_in, u1r_in, u2_in, a2_in, a1_in, acc0_in, acc1_in = refs[:17]
    xu0_in, xz3_in, xu1_in, xz2_in, p1, p2, p3, p4, f3 = refs[17:26]
    first_out, second_out, sens_out = refs[26:29]
    more, (f10, fseam, ea, xs, first, second, sens, out_sem) = refs[29:47], refs[47:]
    fac, fup, srep, load, u0r = (Tiles(OWN, x, y) for x, y in zip((fac_in, fup_in, srep_in, load_in, u0r_in), more))
    u1, u1r, a2 = (Tiles(ONCE, x, y) for x, y in zip((u1_in, u1r_in, a2_in), more[5:]))
    u2, u2r, acc0, acc1, a1 = more[8:13]
    xu0, xz3 = (Tiles(OWN, x, y) for x, y in zip((xu0_in, xz3_in), more[13:]))
    xu1, xz2 = (Tiles(ONCE, x, y) for x, y in zip((xu1_in, xz2_in), more[15:]))
    xz1 = more[17]
    maps = Maps(w, fac, fup, srep, load, (acc0, acc1))
    so_far = Tiles(DEEP_2, acc0_in, acc0), Tiles(DEEP_2, acc1_in, acc1)
    fresh = Fresh(DEEP_2, acc0_in), Fresh(DEEP_2, acc1_in)
    lane = lanes(GROUP)
    from_left = ((lane + 1) & 7) >= 4
    edge = (lane == 0) | (lane == 127)
    edges = (lane <= 1) | (lane >= 126)
    ghosts = (0, 1, 2, 11, 12, 13)
    seams = (LEFT, RIGHT)

    def tile(t, at):
        return ea[t - LEFT, at:at + GROUP] if t >= LEFT else e[t, at:at + GROUP]

    def fixed(t, v, where, ref):
        return jnp.where(where, roll(jnp.where(from_left, ref[LEFT], ref[RIGHT]), 125 - 8 * t), v)

    def value_u1(t, out):
        v = maps.step_u(t, tile(t, U), tile(t, B), out)
        u1[t] = v
        return v

    def value_a2(t, out):
        v = maps.step_a(t, tile(t, A), tile(t, Q), out)
        a2[t] = v
        return v

    def main_u1(t, out):
        v = value_u1(t, out)
        if t in (3, 10, 11):
            u1r[t] = roll(v, 127)
        put(xu1.more, t, v)

    def main_a2(t, out):
        put(xz2.more, t, srep[t] * value_a2(t, out))

    def keep_forces(t, f):
        if t >= LEFT:
            fseam[t - LEFT] = f
        elif t == 10:
            f10[...] = f

    for t in ghosts:
        prepare(t, e.at[t], *more[0:4])
        put(xz3.more, t, srep[t] * tile(t, A))
    maps.main(xz3, (0, 1, 2, 10, 11, 12), main_a2, pieces=(3, 9, p3), forces=keep_forces)
    for side in (0, 1):
        for g in range(4):
            ea[side, FOLD * g:FOLD * g + FOLD] = seam_planes(es, e, near, corner, side, g, 0, FOLD)
        prepare(LEFT + side, ea.at[side], *more[0:4])
        put_seam(xs, 2, side, srep[LEFT + side] * tile(LEFT + side, A))
        put_seam(xs, 0, side, tile(LEFT + side, U))
    maps.seam(xs.at[2], lambda t, out: put_seam(xs, 3, t - LEFT, srep[t] * value_a2(t, out)), forces=keep_forces)
    maps.seam(xs.at[0], lambda t, out: put_seam(xs, 1, t - LEFT, value_u1(t, out)))
    u0r.more[11] = roll(tile(11, U), 127)
    for t in (1, 2, 11, 12, 13):
        put(xu0.more, t, tile(t, U))
    maps.main(xu0, (1, 2, 10, 11, 12), main_u1, pieces=(3, 9, p1))

    def seam_a1(t, out):
        v = maps.step_a(t, a2[t], tile(t, A), out)
        a1[t] = v
        put_seam(xs, 4, t - LEFT, srep[t] * v)

    def seam_u2(t, out):
        u2[t] = maps.step_u(t, u1[t], tile(t, U), out)

    def end_a1(t, v):
        v = fixed(t, v, edges, a1)
        a1[t] = v
        put(xz1, t, srep[t] * v)
        if t in OWN:
            second[pl.ds(t - 3, 36, stride=8), :] = v[0:36]

    def end_u2(t, v):
        v = fixed(t, v, edges, u2)
        u2[t] = v
        u2r[t] = roll(v, 127)

    maps.seam(xs.at[3], seam_a1, lambda t: u1[t], None)
    maps.main(
        xz2, (1, 2, 3, 9, 10, 11), lambda t, out: end_a1(t, maps.step_a(t, a2[t], tile(t, A), out)),
        (u1, u1r), fresh, pieces=(4, 8, p4),
    )
    for t in TWICE:
        end_a1(t, a1_in[t])
    maps.seam(xs.at[1], seam_u2)
    maps.main(xu1, (2, 3, 9, 10, 11), lambda t, out: end_u2(t, maps.step_u(t, u1[t], tile(t, U), out)), pieces=(4, 8, p2))
    for t in TWICE:
        end_u2(t, u2_in[t])

    def seam_a0(t, out):
        a0[t] = maps.step_a(t, a1[t], a2[t], out)

    def main_a0(t, out):
        v = fixed(t, maps.step_a(t, a1[t], a2[t], out), edge, a0)
        first[pl.ds(t - 3, 36, stride=8), :] = v[0:36]

    a0 = {}
    maps.seam(xs.at[4], seam_a0, lambda t: tile(t, U), (acc0, acc1))
    for t in seams:
        maps.collect(t, fseam[t - LEFT], maps.seam_corners(u2[t]), (acc0, acc1))
    maps.main(xz1, range(2, 11), main_a0, (Field(tile, U), u0r), so_far)
    for t in OWN:
        maps.collect(t, f3[t - 3] if t < 10 else f10[...], [u2[t], u2r[t], u2[t + 1], u2r[t + 1]], (acc0, acc1))
    copies = [pltpu.make_async_copy(src, dst, out_sem.at[k]) for k, (src, dst) in enumerate(
        ((first, first_out), (second, second_out), (sens, sens_out)))]
    copies[0].start()
    copies[1].start()

    def total(t):
        return sum(acc0[t, c:c + 11] + acc1[t, c + 1:c + 12] for c in (0, 12, 24))

    lane = lanes(11)
    seam = jnp.where(((lane + 1) & 7) >= 4, total(LEFT), total(RIGHT))
    ends = (lane == 0) | (lane >= 126)
    for r in range(ROWS):
        t = r + 3
        d = e[t, D:D + 11]
        sens[pl.ds(r, 11, stride=8), :] = (-3.0 * (1.0 - EMIN)) * (d * d) * jnp.where(ends, roll(seam, 125 - 8 * t), total(t))
    copies[2].start()
    for c in copies:
        c.wait()


def local(u_now, u_prev, adjoint_next, adjoint_later, density, step_factor, fixed_nodes, load_top, load_depth, brick_stiffness):
    vmem = pl.BlockSpec(memory_space=pltpu.VMEM)
    hbm = pl.BlockSpec(memory_space=pltpu.HBM)
    flat = lambda x: x.reshape(-1, 128)
    sources = (
        flat(u_now), flat(u_prev), flat(adjoint_next), flat(adjoint_later), flat(density), flat(step_factor),
        flat(fixed_nodes), load_top, load_depth, brick_stiffness,
    )
    f32 = lambda *shape: jax.ShapeDtypeStruct(shape + (128,), F32)
    bf16 = lambda *shape: jax.ShapeDtypeStruct(shape, BF16)
    passed = (
        [f32(MAIN, PLANES), bf16(OUT, DEPTH), f32(2, FOLD), f32(4, FOLD // 2), f32(2, PLANES)]
        + [f32(TILES, GROUP)] * 12 + [bf16(MAIN, WIDE, 128)] * 4 + [f32(4, GROUP)] * 4 + [f32(7, OUT)]
    )
    gathered = pl.pallas_call(
        exchange_kernel,
        out_shape=passed,
        in_specs=[hbm] * 10,
        out_specs=[vmem] * len(passed),
        scratch_shapes=[pltpu.VMEM(x.shape, x.dtype) for x in sources] + [
            pltpu.VMEM((2, FOLD, 128), F32),
            pltpu.VMEM((4, FOLD // 2, 128), F32),
            pltpu.SemaphoreType.DMA((10,)),
            pltpu.SemaphoreType.DMA((12,)),
            pltpu.SemaphoreType.DMA((12,)),
        ],
        compiler_params=pltpu.CompilerParams(collective_id=0, has_side_effects=True, vmem_limit_bytes=32 * 2**20),
        name="exchange",
    )(*(pltpu.with_memory_space_constraint(x, pltpu.HBM) for x in sources))
    tiles = lambda n, rows, kind: pltpu.VMEM((n, rows, 128), kind)
    results = ((36 * ROWS, 128), (36 * ROWS, 128), (11 * ROWS, 128))
    first, second, sens = pl.pallas_call(
        plate_kernel,
        out_shape=tuple(jax.ShapeDtypeStruct(shape, F32) for shape in results),
        in_specs=[vmem] * len(passed),
        out_specs=(hbm,) * 3,
        scratch_shapes=[tiles(TILES, GROUP, F32)] * 13 + [tiles(MAIN, WIDE, BF16)] * 5
        + [pltpu.VMEM((OUT, 128), F32), tiles(2, OUT, F32), tiles(2, PLANES, F32), pltpu.VMEM((5, DEPTH, 256), BF16)]
        + [pltpu.VMEM(shape, F32) for shape in results]
        + [pltpu.SemaphoreType.DMA((3,))],
        compiler_params=pltpu.CompilerParams(vmem_limit_bytes=40 * 2**20),
        name="plate",
    )(*gathered)
    return (
        first.reshape(u_now.shape),
        second.reshape(u_now.shape),
        sens.reshape(density.shape),
    )


def solution(mesh):
    in_specs = (
        P(None, None, "gx", "gy"),
        P(None, None, "gx", "gy"),
        P(None, None, "gx", "gy"),
        P(None, None, "gx", "gy"),
        P(None, "gx", "gy"),
        P(None, "gx", "gy"),
        P(None, "gx", "gy"),
        P("gx", "gy"),
        P("gx", "gy"),
        P(),
    )
    out_specs = (P(None, None, "gx", "gy"), P(None, None, "gx", "gy"), P(None, "gx", "gy"))
    return jax.shard_map(local, mesh=mesh, in_specs=in_specs, out_specs=out_specs, check_vma=False)
```

time: 16.7 us -> 14.4 us (0.86)
  the two profiles are of different devices: /device:TPU:65 before, /device:TPU:56 now
where the time goes in v6:
time: 14.4 us; the launch traced here: 14.2 us
  Pallas kernels  13.6 us (94%)
  between operations  0.64 us (4%)
    pallas_call x1, Pallas kernels, local(): pl.pallas_call(exchange_kernel, out_shape=passed, in_specs=[hbm] * 10, ou...  9.74 us
    pallas_call x1, Pallas kernels, local(): pl.pallas_call(plate_kernel, out_shape=tuple((jax.ShapeDtypeStruct(shape,...  3.84 us

profile of v6, /device:TPU:56, one launch (start us, length us, event | category | flops | bytes accessed | tf_op | source)
XLA Modules:
  0.0 14.2 jit_solution(8788636813524653728)
XLA Ops:
  0.6 9.7 %exchange.1 = (f32[14,192,128]{2,1,0:T(8,128)S(1)}, bf16[320,480]{1,0:T(8,128)(2,1)S(1)}, f32[2,48,128]{2,1,0:T(8,128)S(1)}, f32[4,24,128]{2,1,0:T(8,128)S(1)}, ...) custom-call(f32[288,128]{1,0:T(8,128)} %bitcast.10, ...), custom_call_target="tpu_custom_call" | custom-call | tf_op jit(solution)/shard_map/exchange/pallas_call | solution.py:571
  10.4 3.8 %plate.1 = (f32[288,128]{1,0:T(8,128)}, f32[288,128]{1,0:T(8,128)}, f32[88,128]{1,0:T(8,128)}) custom-call(f32[14,192,128]{2,1,0:T(8,128)S(1)} %get-tuple-element.32.refs_0_, bf16[320,480]{1,0:T(8,128)(2,1)S(1)} %get-tuple-element.33.refs_1_, f32[2,48,128]{2,1,0:T(8,128)S(1)} %get-tuple-element.34.refs_2_, f32[4,24,128]{2,1,0:T(8,128)S(1)} %get-tuple-element.35.refs_3_, ...), custom_call_target="tpu_custom_call" | custom-call | tf_op jit(solution)/shard_map/plate/pallas_call | solution.py:588

commit v7 on v6

--- a/solution.py
+++ b/solution.py
@@ -100,23 +100,26 @@
             at += 80
 
 
-def prepare(at, tile, fac, fup, srep, load):
-    layer = lax.broadcasted_iota(jnp.int32, (12, 128), 0).astype(F32)
-    d = tile[D:D + 12]
-    f = jnp.where(d > 0.0, EMIN + (1.0 - EMIN) * (d * d * d), 0.0)
+def prepare(at, tile, fac, fup, srep, load, push=True, elements=True):
+    zeros = lambda n: jnp.zeros((n, 128), F32)
     s = tile[S:S + 12]
-    zeros = lambda n: jnp.zeros((n, 128), F32)
-    fac[at, 36:40] = zeros(4)
-    fup[at, 36:40] = zeros(4)
     srep[at, 36:40] = zeros(4)
-    load[at, 0:24] = zeros(24)
-    load[at, 24:36] = jnp.where(tile[LOAD + 1:LOAD + 2] == layer, tile[LOAD:LOAD + 1], 0.0)
-    load[at, 36:40] = zeros(4)
     for c in (0, 12, 24):
-        fac[at, c:c + 12] = f
-        fup[at, c:c + 1] = zeros(1)
-        fup[at, c + 1:c + 12] = f[0:11]
         srep[at, c:c + 12] = s
+    if elements:
+        d = tile[D:D + 12]
+        f = jnp.where(d > 0.0, EMIN + (1.0 - EMIN) * (d * d * d), 0.0)
+        fac[at, 36:40] = zeros(4)
+        fup[at, 36:40] = zeros(4)
+        for c in (0, 12, 24):
+            fac[at, c:c + 12] = f
+            fup[at, c:c + 1] = zeros(1)
+            fup[at, c + 1:c + 12] = f[0:11]
+    if push:
+        layer = lax.broadcasted_iota(jnp.int32, (12, 128), 0).astype(F32)
+        load[at, 0:24] = zeros(24)
+        load[at, 24:36] = jnp.where(tile[LOAD + 1:LOAD + 2] == layer, tile[LOAD:LOAD + 1], 0.0)
+        load[at, 36:40] = zeros(4)
 
 
 def weigh(f, above, below):
@@ -126,44 +129,37 @@
     ]
 
 
-def pairs_of(w, jobs, post):
+def pairs_of(w, jobs):
     pending = []
     for at in range(0, len(jobs), 2):
         two = jobs[at:at + 2]
-        wide = [jnp.concatenate([x, y], 0) for _, x, y in two]
-        wide = wide[0] if len(wide) == 1 else jnp.concatenate(wide, 1)
-        f = jnp.dot(w[...], wide, preferred_element_type=F32)
-        for job in pending:
-            post(*job)
-        pending = [(key, f[:, 128 * k:128 * k + 128]) for k, (key, _, _) in enumerate(two)]
-    for job in pending:
-        post(*job)
-
-
-def seam_planes(es, e, near, corner, side, g, start, stop):
-    lane = lanes(stop - start)
+        wide = [operand() for _, operand, _ in two]
+        f = jnp.dot(w[...], wide[0] if len(wide) == 1 else jnp.concatenate(wide, 1), preferred_element_type=F32)
+        for t, part, post in pending:
+            post(t, part)
+        pending = [(t, f[:, 128 * k:128 * k + 128], post) for k, (t, _, post) in enumerate(two)]
+    for t, part, post in pending:
+        post(t, part)
+
+
+def seam_planes(es, near, corner, edges, side, g):
+    lane = lanes(FOLD)
     row = ((lane + 1) & 127) >> 3
     late = ((lane + 1) & 7) >= 4
-    inner, low, high = (row >= 3) & (row <= 10), row < 3, (row > 10) & (row < 14)
+    inner, outer = (row >= 3) & (row <= 10), (row < 3) | ((row > 10) & (row < 14))
     by = 24 - 64 * (g >> 1) - 4 * (g & 1)
-    planes = slice(FOLD * g + start, FOLD * g + stop)
-    half = FOLD // 2
-
-    def unfold(ref, first, second):
-        parts = []
-        if start < half:
-            parts.append(roll(ref[start:min(stop, half)], by + first))
-        if stop > half:
-            parts.append(roll(ref[max(start, half) - half:stop - half], by + second))
-        return parts[0] if len(parts) == 1 else jnp.concatenate(parts, 0)
-
-    ghost = es[side, planes]
-    for t in (0, 1, 2, 11, 12, 13):
-        ghost = jnp.where(row == t, roll(e[t, planes], 8 * t + 3), ghost)
-    below = unfold(corner.at[2 * side], 64, 96)
-    above = unfold(corner.at[2 * side + 1], 64, 32)
-    far = jnp.where(inner, roll(near[side, start:stop], by), jnp.where(low, below, jnp.where(high, above, 0.0)))
-    return jnp.where(late, ghost, far) if side == 0 else jnp.where(late, far, ghost)
+    planes = slice(FOLD * g, FOLD * g + FOLD)
+
+    def unfold(below, above, last):
+        early = ((lanes(FOLD // 2) - 3 + 4 * last) & 63) < 32
+        return jnp.concatenate(
+            [roll(jnp.where(early, above, below), by + 64), roll(jnp.where(early, below, above), by + 32)], 0
+        )
+
+    here = jnp.where(outer, unfold(edges[0, side], edges[1, side], side), es[side, planes])
+    beyond = unfold(corner[2 * side], corner[2 * side + 1], 1 - side)
+    far = jnp.where(inner, roll(near[side], by), jnp.where(outer, beyond, 0.0))
+    return jnp.where(late, here, far) if side == 0 else jnp.where(late, far, here)
 
 
 class Tiles:
@@ -248,7 +244,10 @@
             if keep is not None and t == elements[-1]:
                 keep[2], keep[3] = g[2], g[3]
 
-        pairs_of(self.w, [(t, x[t], x[t + 1]) for t in elements], post)
+        def operand(t):
+            return lambda: jnp.concatenate([x[t], x[t + 1]], 0)
+
+        return [(t, operand(t), post) for t in elements]
 
     def step_u(self, t, now, before, out):
         s = self.srep[t]
@@ -260,9 +259,9 @@
 
 def exchange_kernel(*refs):
     sources, refs = refs[:10], refs[10:]
-    e, w, near, corner, es, fac, fup, srep, load, u0r, u1, u1r, u2, a2, a1, acc0, acc1 = refs[:17]
-    xu0, xz3, xu1, xz2, p1, p2, p3, p4, f3 = refs[17:26]
-    held, (mine, corner_out, load_sem, send_sem, recv_sem) = refs[26:36], refs[36:]
+    e, w, near, corner, edges, es, fac, fup, srep, load, u0r, u1, u1r, u2, a2, a1, acc0, acc1 = refs[:18]
+    xu0, xz3, xu1, xz2, p1, p2, p3, p4, f3 = refs[18:27]
+    held, (mine, corner_out, load_sem, send_sem, recv_sem) = refs[27:37], refs[37:]
     u, b, a, q, den, step, fix, top, depth, stiff = held
     gx, gy = lax.axis_index("gx"), lax.axis_index("gy")
     nx, ny = lax.axis_size("gx"), lax.axis_size("gy")
@@ -272,7 +271,7 @@
         (-1, -1): down & left, (1, -1): up & left, (-1, 1): down & right, (1, 1): up & right,
     }
     barrier = pltpu.get_barrier_semaphore()
-    for (dx, dy), there in sides.items():
+    for (dx, dy), there in reversed(sides.items()):
         @pl.when(there)
         def _(dx=dx, dy=dy):
             pl.semaphore_signal(barrier, inc=1, device_id=(gx + dx, gy + dy), device_id_type=MESH)
@@ -281,22 +280,23 @@
     for c in loads:
         c.start()
     zeros = lambda n: jnp.zeros((n, 128), F32)
-    e[0, 0:32] = zeros(32)
-    e[0, 96:PLANES] = zeros(PLANES - 96)
-    e[1, 96:128] = zeros(32)
-    for t in (1, 2, 11, 12):
-        e[t, 176:PLANES] = zeros(PLANES - 176)
-    e[13, 88:PLANES] = zeros(PLANES - 88)
+    for t, start in ((1, 96), (2, 176), (11, 176), (12, 88)):
+        e[t, start:PLANES] = zeros(PLANES - start)
 
     @pl.when(jnp.logical_not(down))
     def _():
-        for t in (0, 1, 2):
+        for t in (1, 2):
             e[t] = zeros(PLANES)
+        edges[0] = jnp.zeros((2, FOLD // 2, 128), F32)
+        a2[1] = zeros(GROUP)
 
     @pl.when(jnp.logical_not(up))
     def _():
-        for t in (11, 12, 13):
+        for t in (11, 12):
             e[t] = zeros(PLANES)
+        edges[1] = jnp.zeros((2, FOLD // 2, 128), F32)
+        u1[12] = zeros(GROUP)
+        a2[12] = zeros(GROUP)
 
     for k, dy in enumerate((-1, 1)):
         @pl.when(jnp.logical_not(sides[0, dy]))
@@ -339,43 +339,22 @@
     lane = lanes(half)
     for k, cols in enumerate((first_cols, last_cols)):
         low = ((lane - 3 + 4 * k) & 63) < 32
-        corner_out[2 * k] = jnp.where(low, cols[0:half], roll(cols[half:FOLD], 32))
-        corner_out[2 * k + 1] = jnp.where(low, roll(cols[half:FOLD], -32), cols[0:half])
-
-    pl.semaphore_wait(barrier, sum(there.astype(jnp.int32) for there in sides.values()))
-    plan = [
-        ((-1, -1), corner_out.at[0], corner.at[3]),
-        ((1, -1), corner_out.at[1], corner.at[2]),
-        ((-1, 1), corner_out.at[2], corner.at[1]),
-        ((1, 1), corner_out.at[3], corner.at[0]),
-        ((0, -1), mine.at[0], near.at[1]),
-        ((0, 1), mine.at[1], near.at[0]),
-        ((-1, 0), e.at[3:5, 0:176], e.at[11:13, 0:176]),
-        ((1, 0), e.at[9:11, 0:96], e.at[1:3, 0:96]),
-        ((1, 0), e.at[9:11, 128:176], e.at[1:3, 128:176]),
-        ((-1, 0), e.at[5, 0:88], e.at[13, 0:88]),
-        ((1, 0), e.at[8, 32:96], e.at[0, 32:96]),
-        ((1, 0), e.at[10, 96:128], e.at[2, 96:128]),
-    ]
-    copies = []
-    for k, ((dx, dy), src, dst) in enumerate(plan):
-        copies.append(((dx, dy), pltpu.make_async_remote_copy(
-            src_ref=src, dst_ref=dst, send_sem=send_sem.at[k], recv_sem=recv_sem.at[k],
-            device_id=(gx + dx, gy + dy), device_id_type=MESH,
-        )))
-    for to, c in copies:
-        @pl.when(sides[to])
-        def _(c=c):
-            c.start()
+        corner_out[k] = jnp.where(low, cols[0:half], roll(cols[half:FOLD], 32))
+        corner_out[2 + k] = jnp.where(low, roll(cols[half:FOLD], 32), cols[0:half])
 
     banded_weights(stiff[...], w)
-    for t in OWN:
-        prepare(t, e.at[t], fac, fup, srep, load)
-        now = e[t, U:U + GROUP]
-        u0r[t] = roll(now, 127)
-        put(xu0, t, now)
-        put(xz3, t, srep[t] * e[t, A:A + GROUP])
     maps = Maps(w, fac, fup, srep, load, (acc0, acc1))
+
+    def own_tiles(some):
+        for t in some:
+            prepare(t, e.at[t], fac, fup, srep, load)
+            now = e[t, U:U + GROUP]
+            u0r[t] = roll(now, 127)
+            put(xu0, t, now)
+            put(xz3, t, srep[t] * e[t, A:A + GROUP])
+
+    def value_a2(t, out):
+        return maps.step_a(t, e[t, A:A + GROUP], e[t, Q:Q + GROUP], out)
 
     def main_u1(t, out):
         v = maps.step_u(t, e[t, U:U + GROUP], e[t, B:B + GROUP], out)
@@ -384,9 +363,53 @@
         put(xu1, t, v)
 
     def main_a2(t, out):
-        v = maps.step_a(t, e[t, A:A + GROUP], e[t, Q:Q + GROUP], out)
-        a2[t] = v
+        v = value_a2(t, out)
+        if t < 9:
+            a2[t] = v
         put(xz2, t, srep[t] * v)
+
+    def row_6(t, out):
+        a2[t] = value_a2(t, out)
+
+    def keep_forces(t, f):
+        f3[t - 3] = f
+
+    own_tiles((3, 4, 5, 8, 9, 10))
+    u_jobs = maps.main(xu0, DEEP_1, main_u1, keep=p1)
+    z_jobs = maps.main(xz3, DEEP_1, main_a2, keep=p3, forces=keep_forces)
+    pairs_of(w, z_jobs[0:2] + maps.main(xz3, (8, 9), row_6) + u_jobs[0:2])
+
+    pl.semaphore_wait(barrier, sum(there.astype(jnp.int32) for there in sides.values()))
+    plan = [
+        ((-1, -1), corner_out.at[0], corner.at[3]),
+        ((1, -1), corner_out.at[2], corner.at[2]),
+        ((-1, 1), corner_out.at[1], corner.at[1]),
+        ((1, 1), corner_out.at[3], corner.at[0]),
+        ((0, -1), mine.at[0], near.at[1]),
+        ((0, 1), mine.at[1], near.at[0]),
+        ((-1, 0), corner_out.at[0:2], edges.at[1]),
+        ((-1, 0), e.at[3, 0:176], e.at[11, 0:176]),
+        ((-1, 0), e.at[4, 0:88], e.at[12, 0:88]),
+        ((-1, 0), a2.at[4], a2.at[12]),
+        ((-1, 0), u1.at[4], u1.at[12]),
+        ((1, 0), corner_out.at[2:4], edges.at[0]),
+        ((1, 0), e.at[10, 0:176], e.at[2, 0:176]),
+        ((1, 0), e.at[9, 0:96], e.at[1, 0:96]),
+        ((1, 0), a2.at[9], a2.at[1]),
+    ]
+    copies = {}
+    for k, ((dx, dy), src, dst) in enumerate(plan):
+        copies.setdefault((dx, dy), []).append(pltpu.make_async_remote_copy(
+            src_ref=src, dst_ref=dst, send_sem=send_sem.at[k], recv_sem=recv_sem.at[k],
+            device_id=(gx + dx, gy + dy), device_id_type=MESH,
+        ))
+    for to, group in copies.items():
+        @pl.when(sides[to])
+        def _(group=group):
+            for c in group:
+                c.start()
+
+    own_tiles((6, 7))
 
     def main_u2(t, out):
         u2[t] = maps.step_u(t, u1[t], e[t, U:U + GROUP], out)
@@ -394,13 +417,8 @@
     def main_a1(t, out):
         a1[t] = maps.step_a(t, a2[t], e[t, A:A + GROUP], out)
 
-    def keep_forces(t, f):
-        f3[t - 3] = f
-
-    maps.main(xu0, DEEP_1, main_u1, keep=p1)
-    maps.main(xz3, DEEP_1, main_a2, keep=p3, forces=keep_forces)
-    maps.main(xu1, DEEP_2, main_u2, keep=p2)
-    maps.main(xz2, DEEP_2, main_a1, (u1, u1r), None, keep=p4)
+    pairs_of(w, u_jobs[2:] + z_jobs[2:])
+    pairs_of(w, maps.main(xu1, DEEP_2, main_u2, keep=p2) + maps.main(xz2, DEEP_2, main_a1, (u1, u1r), None, keep=p4))
     lane = lanes(FOLD)
     inner = (((lane + 1) & 127) >> 3 >= 3) & (((lane + 1) & 127) >> 3 <= 10)
     late = ((lane + 1) & 7) >= 4
@@ -409,23 +427,28 @@
         for side in (0, 1):
             es[side, FOLD * g:FOLD * g + FOLD] = jnp.where(inner & (late == (side == 0)), roll(mine[side], by), 0.0)
 
-    for (dx, dy), c in copies:
+    for to, group in copies.items():
+        @pl.when(sides[to])
+        def _(group=group):
+            for c in group:
+                c.wait_send()
+
+    for (dx, dy), group in copies.items():
         @pl.when(sides[-dx, -dy])
-        def _(c=c):
-            c.wait_recv()
-    for to, c in copies:
-        @pl.when(sides[to])
-        def _(c=c):
-            c.wait_send()
+        def _(group=group):
+            for c in group:
+                c.wait_recv()
 
 
 def plate_kernel(*refs):
-    e, w, near, corner, es, fac_in, fup_in, srep_in, load_in, u0r_in, u1_in, u1r_in, u2_in, a2_in, a1_in, acc0_in, acc1_in = refs[:17]
-    xu0_in, xz3_in, xu1_in, xz2_in, p1, p2, p3, p4, f3 = refs[17:26]
-    first_out, second_out, sens_out = refs[26:29]
-    more, (f10, fseam, ea, xs, first, second, sens, out_sem) = refs[29:47], refs[47:]
+    e, w, near, corner, edges, es, fac_in, fup_in, srep_in, load_in, u0r_in, u1_in, u1r_in, u2_in, a2_in, a1_in, acc0_in, acc1_in = refs[:18]
+    xu0_in, xz3_in, xu1_in, xz2_in, p1, p2, p3, p4, f3 = refs[18:27]
+    first_out, second_out, sens_out = refs[27:30]
+    more, (f10, fseam, ends, ea, xs, first, second, sens, out_sem) = refs[30:48], refs[48:]
     fac, fup, srep, load, u0r = (Tiles(OWN, x, y) for x, y in zip((fac_in, fup_in, srep_in, load_in, u0r_in), more))
-    u1, u1r, a2 = (Tiles(ONCE, x, y) for x, y in zip((u1_in, u1r_in, a2_in), more[5:]))
+    u1, u1r, a2 = (
+        Tiles(own, x, y) for own, x, y in zip(((*ONCE, 12), ONCE, (1, *ONCE, 12)), (u1_in, u1r_in, a2_in), more[5:])
+    )
     u2, u2r, acc0, acc1, a1 = more[8:13]
     xu0, xz3 = (Tiles(OWN, x, y) for x, y in zip((xu0_in, xz3_in), more[13:]))
     xu1, xz2 = (Tiles(ONCE, x, y) for x, y in zip((xu1_in, xz2_in), more[15:]))
@@ -436,15 +459,18 @@
     lane = lanes(GROUP)
     from_left = ((lane + 1) & 7) >= 4
     edge = (lane == 0) | (lane == 127)
-    edges = (lane <= 1) | (lane >= 126)
-    ghosts = (0, 1, 2, 11, 12, 13)
+    outermost = (lane <= 1) | (lane >= 126)
+    ghosts = (1, 2, 11, 12)
     seams = (LEFT, RIGHT)
 
     def tile(t, at):
         return ea[t - LEFT, at:at + GROUP] if t >= LEFT else e[t, at:at + GROUP]
 
-    def fixed(t, v, where, ref):
-        return jnp.where(where, roll(jnp.where(from_left, ref[LEFT], ref[RIGHT]), 125 - 8 * t), v)
+    def both(k, ref):
+        ends[k] = jnp.where(from_left, ref[LEFT], ref[RIGHT])
+
+    def fixed(t, v, where, k):
+        return jnp.where(where, roll(ends[k], 125 - 8 * t), v)
 
     def value_u1(t, out):
         v = maps.step_u(t, tile(t, U), tile(t, B), out)
@@ -471,23 +497,6 @@
         elif t == 10:
             f10[...] = f
 
-    for t in ghosts:
-        prepare(t, e.at[t], *more[0:4])
-        put(xz3.more, t, srep[t] * tile(t, A))
-    maps.main(xz3, (0, 1, 2, 10, 11, 12), main_a2, pieces=(3, 9, p3), forces=keep_forces)
-    for side in (0, 1):
-        for g in range(4):
-            ea[side, FOLD * g:FOLD * g + FOLD] = seam_planes(es, e, near, corner, side, g, 0, FOLD)
-        prepare(LEFT + side, ea.at[side], *more[0:4])
-        put_seam(xs, 2, side, srep[LEFT + side] * tile(LEFT + side, A))
-        put_seam(xs, 0, side, tile(LEFT + side, U))
-    maps.seam(xs.at[2], lambda t, out: put_seam(xs, 3, t - LEFT, srep[t] * value_a2(t, out)), forces=keep_forces)
-    maps.seam(xs.at[0], lambda t, out: put_seam(xs, 1, t - LEFT, value_u1(t, out)))
-    u0r.more[11] = roll(tile(11, U), 127)
-    for t in (1, 2, 11, 12, 13):
-        put(xu0.more, t, tile(t, U))
-    maps.main(xu0, (1, 2, 10, 11, 12), main_u1, pieces=(3, 9, p1))
-
     def seam_a1(t, out):
         v = maps.step_a(t, a2[t], tile(t, A), out)
         a1[t] = v
@@ -497,43 +506,105 @@
         u2[t] = maps.step_u(t, u1[t], tile(t, U), out)
 
     def end_a1(t, v):
-        v = fixed(t, v, edges, a1)
+        v = fixed(t, v, outermost, 0)
         a1[t] = v
         put(xz1, t, srep[t] * v)
         if t in OWN:
             second[pl.ds(t - 3, 36, stride=8), :] = v[0:36]
 
     def end_u2(t, v):
-        v = fixed(t, v, edges, u2)
+        v = fixed(t, v, outermost, 1)
         u2[t] = v
         u2r[t] = roll(v, 127)
 
-    maps.seam(xs.at[3], seam_a1, lambda t: u1[t], None)
-    maps.main(
-        xz2, (1, 2, 3, 9, 10, 11), lambda t, out: end_a1(t, maps.step_a(t, a2[t], tile(t, A), out)),
-        (u1, u1r), fresh, pieces=(4, 8, p4),
-    )
-    for t in TWICE:
-        end_a1(t, a1_in[t])
-    maps.seam(xs.at[1], seam_u2)
-    maps.main(xu1, (2, 3, 9, 10, 11), lambda t, out: end_u2(t, maps.step_u(t, u1[t], tile(t, U), out)), pieces=(4, 8, p2))
-    for t in TWICE:
-        end_u2(t, u2_in[t])
+    a0 = {}
 
     def seam_a0(t, out):
         a0[t] = maps.step_a(t, a1[t], a2[t], out)
 
     def main_a0(t, out):
-        v = fixed(t, maps.step_a(t, a1[t], a2[t], out), edge, a0)
+        v = fixed(t, maps.step_a(t, a1[t], a2[t], out), edge, 2)
         first[pl.ds(t - 3, 36, stride=8), :] = v[0:36]
 
-    a0 = {}
-    maps.seam(xs.at[4], seam_a0, lambda t: tile(t, U), (acc0, acc1))
-    for t in seams:
-        maps.collect(t, fseam[t - LEFT], maps.seam_corners(u2[t]), (acc0, acc1))
-    maps.main(xz1, range(2, 11), main_a0, (Field(tile, U), u0r), so_far)
-    for t in OWN:
-        maps.collect(t, f3[t - 3] if t < 10 else f10[...], [u2[t], u2r[t], u2[t + 1], u2r[t + 1]], (acc0, acc1))
+    def ghost_tiles():
+        for t in ghosts:
+            prepare(t, e.at[t], *more[0:4], push=1 < t < 12, elements=t < 12)
+
+    def ghost_z3():
+        for t in ghosts:
+            put(xz3.more, t, srep[t] * tile(t, A))
+        for t in (1, 12):
+            put(xz2.more, t, srep[t] * a2[t])
+
+    def ghost_u0():
+        u0r.more[11] = roll(tile(11, U), 127)
+        for t in ghosts:
+            put(xu0.more, t, tile(t, U))
+        put(xu1.more, 12, u1[12])
+
+    def seam_tiles():
+        for g in (1, 0, 2):
+            for side in (0, 1):
+                ea[side, FOLD * g:FOLD * g + FOLD] = seam_planes(es, near, corner, edges, side, g)
+        for side in (0, 1):
+            prepare(LEFT + side, ea.at[side], *more[0:4])
+            put_seam(xs, 2, side, srep[LEFT + side] * tile(LEFT + side, A))
+        for side in (0, 1):
+            put_seam(xs, 0, side, tile(LEFT + side, U))
+            ea[side, FOLD * 3:FOLD * 4] = seam_planes(es, near, corner, edges, side, 3)
+
+    def z3_rows():
+        pairs_of(w, maps.main(xz3, (1, 2, 10, 11), main_a2, pieces=(3, 9, p3), forces=keep_forces))
+
+    def u0_rows():
+        pairs_of(w, maps.main(xu0, (1, 2, 10, 11), main_u1, pieces=(3, 9, p1)))
+
+    def z3_seam():
+        maps.seam(xs.at[2], lambda t, out: put_seam(xs, 3, t - LEFT, srep[t] * value_a2(t, out)), forces=keep_forces)
+
+    def u0_seam():
+        maps.seam(xs.at[0], lambda t, out: put_seam(xs, 1, t - LEFT, value_u1(t, out)))
+
+    def z2_seam():
+        maps.seam(xs.at[3], seam_a1, lambda t: u1[t], None)
+        both(0, a1)
+
+    def u1_seam():
+        maps.seam(xs.at[1], seam_u2)
+        both(1, u2)
+
+    def z2_rows():
+        for t in TWICE:
+            end_a1(t, a1_in[t])
+        pairs_of(w, maps.main(
+            xz2, (1, 2, 3, 9, 10, 11), lambda t, out: end_a1(t, maps.step_a(t, a2[t], tile(t, A), out)),
+            (u1, u1r), fresh, pieces=(4, 8, p4),
+        ))
+
+    def u1_rows():
+        for t in TWICE:
+            end_u2(t, u2_in[t])
+        pairs_of(w, maps.main(xu1, (2, 3, 9, 10, 11), lambda t, out: end_u2(t, maps.step_u(t, u1[t], tile(t, U), out)), pieces=(4, 8, p2)))
+
+    def z1_seam():
+        maps.seam(xs.at[4], seam_a0, lambda t: tile(t, U), (acc0, acc1))
+        both(2, a0)
+
+    def z1_rows():
+        pairs_of(w, maps.main(xz1, range(2, 11), main_a0, (Field(tile, U), u0r), so_far))
+
+    def seam_sums():
+        for t in seams:
+            maps.collect(t, fseam[t - LEFT], maps.seam_corners(u2[t]), (acc0, acc1))
+
+    def row_sums():
+        for t in OWN:
+            maps.collect(t, f3[t - 3] if t < 10 else f10[...], [u2[t], u2r[t], u2[t + 1], u2r[t + 1]], (acc0, acc1))
+
+    for block in (
+        seam_tiles, ghost_tiles, ghost_z3, ghost_u0, z3_rows, z3_seam, u0_seam, u0_rows, z2_seam, z2_rows, u1_seam, z1_seam, u1_rows, seam_sums, z1_rows, row_sums,
+    ):
+        block()
     copies = [pltpu.make_async_copy(src, dst, out_sem.at[k]) for k, (src, dst) in enumerate(
         ((first, first_out), (second, second_out), (sens, sens_out)))]
     copies[0].start()
@@ -544,11 +615,11 @@
 
     lane = lanes(11)
     seam = jnp.where(((lane + 1) & 7) >= 4, total(LEFT), total(RIGHT))
-    ends = (lane == 0) | (lane >= 126)
+    outer = (lane == 0) | (lane >= 126)
     for r in range(ROWS):
         t = r + 3
         d = e[t, D:D + 11]
-        sens[pl.ds(r, 11, stride=8), :] = (-3.0 * (1.0 - EMIN)) * (d * d) * jnp.where(ends, roll(seam, 125 - 8 * t), total(t))
+        sens[pl.ds(r, 11, stride=8), :] = (-3.0 * (1.0 - EMIN)) * (d * d) * jnp.where(outer, roll(seam, 125 - 8 * t), total(t))
     copies[2].start()
     for c in copies:
         c.wait()
@@ -565,7 +636,7 @@
     f32 = lambda *shape: jax.ShapeDtypeStruct(shape + (128,), F32)
     bf16 = lambda *shape: jax.ShapeDtypeStruct(shape, BF16)
     passed = (
-        [f32(MAIN, PLANES), bf16(OUT, DEPTH), f32(2, FOLD), f32(4, FOLD // 2), f32(2, PLANES)]
+        [f32(MAIN, PLANES), bf16(OUT, DEPTH), f32(2, FOLD), f32(4, FOLD // 2), f32(2, 2, FOLD // 2), f32(2, PLANES)]
         + [f32(TILES, GROUP)] * 12 + [bf16(MAIN, WIDE, 128)] * 4 + [f32(4, GROUP)] * 4 + [f32(7, OUT)]
     )
     gathered = pl.pallas_call(
@@ -577,8 +648,8 @@
             pltpu.VMEM((2, FOLD, 128), F32),
             pltpu.VMEM((4, FOLD // 2, 128), F32),
             pltpu.SemaphoreType.DMA((10,)),
-            pltpu.SemaphoreType.DMA((12,)),
-            pltpu.SemaphoreType.DMA((12,)),
+            pltpu.SemaphoreType.DMA((15,)),
+            pltpu.SemaphoreType.DMA((15,)),
         ],
         compiler_params=pltpu.CompilerParams(collective_id=0, has_side_effects=True, vmem_limit_bytes=32 * 2**20),
         name="exchange",
@@ -591,7 +662,7 @@
         in_specs=[vmem] * len(passed),
         out_specs=(hbm,) * 3,
         scratch_shapes=[tiles(TILES, GROUP, F32)] * 13 + [tiles(MAIN, WIDE, BF16)] * 5
-        + [pltpu.VMEM((OUT, 128), F32), tiles(2, OUT, F32), tiles(2, PLANES, F32), pltpu.VMEM((5, DEPTH, 256), BF16)]
+        + [pltpu.VMEM((OUT, 128), F32), tiles(2, OUT, F32), tiles(3, GROUP, F32), tiles(2, PLANES, F32), pltpu.VMEM((5, DEPTH, 256), BF16)]
         + [pltpu.VMEM(shape, F32) for shape in results]
         + [pltpu.SemaphoreType.DMA((3,))],
         compiler_params=pltpu.CompilerParams(vmem_limit_bytes=40 * 2**20),

time: 14.4 us -> 14 us (0.972)
  Pallas kernels: 13.6 us -> 13.3 us
    pallas_call x1, Pallas kernels: 3.84 us -> 3.64 us  [local(): pl.pallas_call(plate_kernel, out_shape=tuple((jax.ShapeDtypeStruct(shape,...]
where the time goes in v7:
time: 14 us; the launch traced here: 13.9 us
  Pallas kernels  13.3 us (95%)
  between operations  0.64 us (5%)
    pallas_call x1, Pallas kernels, local(): pl.pallas_call(exchange_kernel, out_shape=passed, in_specs=[hbm] * 10, ou...  9.63 us
    pallas_call x1, Pallas kernels, local(): pl.pallas_call(plate_kernel, out_shape=tuple((jax.ShapeDtypeStruct(shape,...  3.64 us

profile of v7, /device:TPU:56, one launch (start us, length us, event | category | flops | bytes accessed | tf_op | source)
XLA Modules:
  0.0 13.9 jit_solution(5585575947063357939)
XLA Ops:
  0.6 9.6 %exchange.1 = (f32[14,192,128]{2,1,0:T(8,128)S(1)}, bf16[320,480]{1,0:T(8,128)(2,1)S(1)}, f32[2,48,128]{2,1,0:T(8,128)S(1)}, f32[4,24,128]{2,1,0:T(8,128)S(1)}, ...) custom-call(f32[288,128]{1,0:T(8,128)} %bitcast.10, ...), custom_call_target="tpu_custom_call" | custom-call | tf_op jit(solution)/shard_map/exchange/pallas_call | solution.py:642
  10.3 3.6 %plate.1 = (f32[288,128]{1,0:T(8,128)}, f32[288,128]{1,0:T(8,128)}, f32[88,128]{1,0:T(8,128)}) custom-call(f32[14,192,128]{2,1,0:T(8,128)S(1)} %get-tuple-element.33.refs_0_, bf16[320,480]{1,0:T(8,128)(2,1)S(1)} %get-tuple-element.34.refs_1_, f32[2,48,128]{2,1,0:T(8,128)S(1)} %get-tuple-element.35.refs_2_, f32[4,24,128]{2,1,0:T(8,128)S(1)} %get-tuple-element.36.refs_3_, ...), custom_call_target="tpu_custom_call" | custom-call | tf_op jit(solution)/shard_map/plate/pallas_call | solution.py:659

commit v8 on v7

--- a/solution.py
+++ b/solution.py
@@ -217,7 +217,7 @@
             g = weigh(part, self.fac[t], self.fup[t])
             finish(t, g[0] + roll(g[1], 1) + roll(g[2], 8) + roll(g[3], 9))
 
-    def main(self, x, elements, finish, state=None, so_far=None, pieces=None, keep=None, forces=None):
+    def main(self, x, elements, finish, state=None, so_far=None, pieces=None, keep=None, forces=None, beyond=None):
         carry = None
         first, last, ends = pieces if pieces is not None else (None, None, None)
 
@@ -241,6 +241,10 @@
             carry = g[2:]
             if ends is not None and t == first - 1:
                 node(first, (ends[0], ends[1]), carry)
+            if beyond is not None and t == first - 1:
+                finish(t, g[0] + roll(g[1], 1) + beyond[0])
+            if beyond is not None and t == last + 1:
+                finish(t + 1, g[2] + roll(g[3], 1) + beyond[1])
             if keep is not None and t == elements[-1]:
                 keep[2], keep[3] = g[2], g[3]
 
@@ -259,9 +263,9 @@
 
 def exchange_kernel(*refs):
     sources, refs = refs[:10], refs[10:]
-    e, w, near, corner, edges, es, fac, fup, srep, load, u0r, u1, u1r, u2, a2, a1, acc0, acc1 = refs[:18]
-    xu0, xz3, xu1, xz2, p1, p2, p3, p4, f3 = refs[18:27]
-    held, (mine, corner_out, load_sem, send_sem, recv_sem) = refs[27:37], refs[37:]
+    e, w, near, corner, edges, zin, pin, es, fac, fup, srep, load, u0r, u1, u1r, u2, a2, a1, acc0, acc1 = refs[:20]
+    xu0, xz3, xu1, xz2, p1, p2, p3, p4, f3 = refs[20:29]
+    held, (mine, corner_out, zout, pout, ends_u, ends_z, load_sem, send_sem, recv_sem) = refs[29:39], refs[39:]
     u, b, a, q, den, step, fix, top, depth, stiff = held
     gx, gy = lax.axis_index("gx"), lax.axis_index("gy")
     nx, ny = lax.axis_size("gx"), lax.axis_size("gy")
@@ -277,26 +281,28 @@
             pl.semaphore_signal(barrier, inc=1, device_id=(gx + dx, gy + dy), device_id_type=MESH)
 
     loads = [pltpu.make_async_copy(src, dst, load_sem.at[k]) for k, (src, dst) in enumerate(zip(sources, held))]
-    for c in loads:
+    loads[-1].start()
+    for c in loads[:-1]:
         c.start()
     zeros = lambda n: jnp.zeros((n, 128), F32)
-    for t, start in ((1, 96), (2, 176), (11, 176), (12, 88)):
-        e[t, start:PLANES] = zeros(PLANES - start)
+    for t, start, stop in ((1, 0, 80), (1, 96, PLANES), (2, 176, PLANES), (11, 176, PLANES)):
+        e[t, start:stop] = zeros(stop - start)
 
     @pl.when(jnp.logical_not(down))
     def _():
         for t in (1, 2):
             e[t] = zeros(PLANES)
         edges[0] = jnp.zeros((2, FOLD // 2, 128), F32)
-        a2[1] = zeros(GROUP)
+        zin[0] = zeros(GROUP)
+        pin[2], pin[3] = zeros(GROUP), zeros(GROUP)
 
     @pl.when(jnp.logical_not(up))
     def _():
-        for t in (11, 12):
-            e[t] = zeros(PLANES)
+        e[11] = zeros(PLANES)
         edges[1] = jnp.zeros((2, FOLD // 2, 128), F32)
         u1[12] = zeros(GROUP)
-        a2[12] = zeros(GROUP)
+        zin[1] = zeros(GROUP)
+        pin[0], pin[1] = zeros(GROUP), zeros(GROUP)
 
     for k, dy in enumerate((-1, 1)):
         @pl.when(jnp.logical_not(sides[0, dy]))
@@ -308,7 +314,9 @@
             def _(k=k, j=j):
                 corner[2 * k + j] = zeros(FOLD // 2)
 
-    for c in loads:
+    loads[-1].wait()
+    banded_weights(stiff[...], w)
+    for c in loads[:-1]:
         c.wait()
     for r in range(ROWS):
         t = r + 3
@@ -342,7 +350,6 @@
         corner_out[k] = jnp.where(low, cols[0:half], roll(cols[half:FOLD], 32))
         corner_out[2 + k] = jnp.where(low, roll(cols[half:FOLD], 32), cols[0:half])
 
-    banded_weights(stiff[...], w)
     maps = Maps(w, fac, fup, srep, load, (acc0, acc1))
 
     def own_tiles(some):
@@ -364,12 +371,14 @@
 
     def main_a2(t, out):
         v = value_a2(t, out)
-        if t < 9:
-            a2[t] = v
-        put(xz2, t, srep[t] * v)
+        a2[t] = v
+        v = srep[t] * v
+        if t == 4:
+            zout[0] = v
+        put(xz2, t, v)
 
     def row_6(t, out):
-        a2[t] = value_a2(t, out)
+        zout[1] = srep[t] * value_a2(t, out)
 
     def keep_forces(t, f):
         f3[t - 3] = f
@@ -377,7 +386,9 @@
     own_tiles((3, 4, 5, 8, 9, 10))
     u_jobs = maps.main(xu0, DEEP_1, main_u1, keep=p1)
     z_jobs = maps.main(xz3, DEEP_1, main_a2, keep=p3, forces=keep_forces)
-    pairs_of(w, z_jobs[0:2] + maps.main(xz3, (8, 9), row_6) + u_jobs[0:2])
+    pairs_of(w, z_jobs[0:2] + maps.main(xz3, (8, 9), row_6, keep=ends_z) + u_jobs[0:2] + maps.main(xu0, (9,), None, keep=ends_u))
+    for k, (p, q) in enumerate(((p1, 0), (p3, 0), (ends_u, 2), (ends_z, 2))):
+        pout[k] = p[q] + roll(p[q + 1], 1)
 
     pl.semaphore_wait(barrier, sum(there.astype(jnp.int32) for there in sides.values()))
     plan = [
@@ -389,13 +400,14 @@
         ((0, 1), mine.at[1], near.at[0]),
         ((-1, 0), corner_out.at[0:2], edges.at[1]),
         ((-1, 0), e.at[3, 0:176], e.at[11, 0:176]),
-        ((-1, 0), e.at[4, 0:88], e.at[12, 0:88]),
-        ((-1, 0), a2.at[4], a2.at[12]),
         ((-1, 0), u1.at[4], u1.at[12]),
+        ((-1, 0), zout.at[0], zin.at[1]),
+        ((-1, 0), pout.at[0:2], pin.at[0:2]),
         ((1, 0), corner_out.at[2:4], edges.at[0]),
         ((1, 0), e.at[10, 0:176], e.at[2, 0:176]),
-        ((1, 0), e.at[9, 0:96], e.at[1, 0:96]),
-        ((1, 0), a2.at[9], a2.at[1]),
+        ((1, 0), e.at[9, 80:96], e.at[1, 80:96]),
+        ((1, 0), zout.at[1], zin.at[0]),
+        ((1, 0), pout.at[2:4], pin.at[2:4]),
     ]
     copies = {}
     for k, ((dx, dy), src, dst) in enumerate(plan):
@@ -441,13 +453,13 @@
 
 
 def plate_kernel(*refs):
-    e, w, near, corner, edges, es, fac_in, fup_in, srep_in, load_in, u0r_in, u1_in, u1r_in, u2_in, a2_in, a1_in, acc0_in, acc1_in = refs[:18]
-    xu0_in, xz3_in, xu1_in, xz2_in, p1, p2, p3, p4, f3 = refs[18:27]
-    first_out, second_out, sens_out = refs[27:30]
-    more, (f10, fseam, ends, ea, xs, first, second, sens, out_sem) = refs[30:48], refs[48:]
+    e, w, near, corner, edges, zin, pin, es, fac_in, fup_in, srep_in, load_in, u0r_in, u1_in, u1r_in, u2_in, a2_in, a1_in, acc0_in, acc1_in = refs[:20]
+    xu0_in, xz3_in, xu1_in, xz2_in, p1, p2, p3, p4, f3 = refs[20:29]
+    first_out, second_out, sens_out = refs[29:32]
+    more, (f10, fseam, ends, ea, xs, first, second, sens, out_sem) = refs[32:50], refs[50:]
     fac, fup, srep, load, u0r = (Tiles(OWN, x, y) for x, y in zip((fac_in, fup_in, srep_in, load_in, u0r_in), more))
     u1, u1r, a2 = (
-        Tiles(own, x, y) for own, x, y in zip(((*ONCE, 12), ONCE, (1, *ONCE, 12)), (u1_in, u1r_in, a2_in), more[5:])
+        Tiles(own, x, y) for own, x, y in zip(((*ONCE, 12), ONCE, ONCE), (u1_in, u1r_in, a2_in), more[5:])
     )
     u2, u2r, acc0, acc1, a1 = more[8:13]
     xu0, xz3 = (Tiles(OWN, x, y) for x, y in zip((xu0_in, xz3_in), more[13:]))
@@ -460,7 +472,7 @@
     from_left = ((lane + 1) & 7) >= 4
     edge = (lane == 0) | (lane == 127)
     outermost = (lane <= 1) | (lane >= 126)
-    ghosts = (1, 2, 11, 12)
+    ghosts = (2, 11)
     seams = (LEFT, RIGHT)
 
     def tile(t, at):
@@ -528,13 +540,14 @@
 
     def ghost_tiles():
         for t in ghosts:
-            prepare(t, e.at[t], *more[0:4], push=1 < t < 12, elements=t < 12)
+            prepare(t, e.at[t], *more[0:4])
+        prepare(1, e.at[1], *more[0:4], push=False)
 
     def ghost_z3():
         for t in ghosts:
             put(xz3.more, t, srep[t] * tile(t, A))
-        for t in (1, 12):
-            put(xz2.more, t, srep[t] * a2[t])
+        put(xz2.more, 1, zin[0])
+        put(xz2.more, 12, zin[1])
 
     def ghost_u0():
         u0r.more[11] = roll(tile(11, U), 127)
@@ -554,10 +567,10 @@
             ea[side, FOLD * 3:FOLD * 4] = seam_planes(es, near, corner, edges, side, 3)
 
     def z3_rows():
-        pairs_of(w, maps.main(xz3, (1, 2, 10, 11), main_a2, pieces=(3, 9, p3), forces=keep_forces))
+        pairs_of(w, maps.main(xz3, (2, 10), main_a2, pieces=(3, 9, p3), forces=keep_forces, beyond=(pin[3], pin[1])))
 
     def u0_rows():
-        pairs_of(w, maps.main(xu0, (1, 2, 10, 11), main_u1, pieces=(3, 9, p1)))
+        pairs_of(w, maps.main(xu0, (2, 10), main_u1, pieces=(3, 9, p1), beyond=(pin[2], pin[0])))
 
     def z3_seam():
         maps.seam(xs.at[2], lambda t, out: put_seam(xs, 3, t - LEFT, srep[t] * value_a2(t, out)), forces=keep_forces)
@@ -602,7 +615,8 @@
             maps.collect(t, f3[t - 3] if t < 10 else f10[...], [u2[t], u2r[t], u2[t + 1], u2r[t + 1]], (acc0, acc1))
 
     for block in (
-        seam_tiles, ghost_tiles, ghost_z3, ghost_u0, z3_rows, z3_seam, u0_seam, u0_rows, z2_seam, z2_rows, u1_seam, z1_seam, u1_rows, seam_sums, z1_rows, row_sums,
+        seam_tiles, ghost_tiles, ghost_z3, z3_seam, ghost_u0, z3_rows, u0_seam, u0_rows,
+        z2_seam, z2_rows, u1_seam, u1_rows, z1_seam, seam_sums, z1_rows, row_sums,
     ):
         block()
     copies = [pltpu.make_async_copy(src, dst, out_sem.at[k]) for k, (src, dst) in enumerate(
@@ -636,9 +650,10 @@
     f32 = lambda *shape: jax.ShapeDtypeStruct(shape + (128,), F32)
     bf16 = lambda *shape: jax.ShapeDtypeStruct(shape, BF16)
     passed = (
-        [f32(MAIN, PLANES), bf16(OUT, DEPTH), f32(2, FOLD), f32(4, FOLD // 2), f32(2, 2, FOLD // 2), f32(2, PLANES)]
+        [f32(MAIN, PLANES), bf16(OUT, DEPTH), f32(2, FOLD), f32(4, FOLD // 2), f32(2, 2, FOLD // 2), f32(2, GROUP), f32(4, GROUP), f32(2, PLANES)]
         + [f32(TILES, GROUP)] * 12 + [bf16(MAIN, WIDE, 128)] * 4 + [f32(4, GROUP)] * 4 + [f32(7, OUT)]
     )
+    tiles = lambda n, rows, kind: pltpu.VMEM((n, rows, 128), kind)
     gathered = pl.pallas_call(
         exchange_kernel,
         out_shape=passed,
@@ -647,14 +662,17 @@
         scratch_shapes=[pltpu.VMEM(x.shape, x.dtype) for x in sources] + [
             pltpu.VMEM((2, FOLD, 128), F32),
             pltpu.VMEM((4, FOLD // 2, 128), F32),
+            tiles(2, GROUP, F32),
+            tiles(4, GROUP, F32),
+            tiles(4, GROUP, F32),
+            tiles(4, GROUP, F32),
             pltpu.SemaphoreType.DMA((10,)),
-            pltpu.SemaphoreType.DMA((15,)),
-            pltpu.SemaphoreType.DMA((15,)),
+            pltpu.SemaphoreType.DMA((16,)),
+            pltpu.SemaphoreType.DMA((16,)),
         ],
         compiler_params=pltpu.CompilerParams(collective_id=0, has_side_effects=True, vmem_limit_bytes=32 * 2**20),
         name="exchange",
     )(*(pltpu.with_memory_space_constraint(x, pltpu.HBM) for x in sources))
-    tiles = lambda n, rows, kind: pltpu.VMEM((n, rows, 128), kind)
     results = ((36 * ROWS, 128), (36 * ROWS, 128), (11 * ROWS, 128))
     first, second, sens = pl.pallas_call(
         plate_kernel,

time: 14 us -> 14 us (level)
  no operation moved by 1% of the time
where the time goes in v8:
time: 14 us; the launch traced here: 13.8 us
  Pallas kernels  13.2 us (94%)
  between operations  0.64 us (5%)
    pallas_call x1, Pallas kernels, local(): pl.pallas_call(exchange_kernel, out_shape=passed, in_specs=[hbm] * 10, ou...  9.65 us
    pallas_call x1, Pallas kernels, local(): pl.pallas_call(plate_kernel, out_shape=tuple((jax.ShapeDtypeStruct(shape,...  3.54 us

profile of v8, /device:TPU:56, one launch (start us, length us, event | category | flops | bytes accessed | tf_op | source)
XLA Modules:
  0.0 13.8 jit_solution(9289066141861198892)
XLA Ops:
  0.6 9.7 %exchange.1 = (f32[14,192,128]{2,1,0:T(8,128)S(1)}, bf16[320,480]{1,0:T(8,128)(2,1)S(1)}, f32[2,48,128]{2,1,0:T(8,128)S(1)}, f32[4,24,128]{2,1,0:T(8,128)S(1)}, ...) custom-call(f32[288,128]{1,0:T(8,128)} %bitcast.10, ...), custom_call_target="tpu_custom_call" | custom-call | tf_op jit(solution)/shard_map/exchange/pallas_call | solution.py:657
  10.3 3.5 %plate.1 = (f32[288,128]{1,0:T(8,128)}, f32[288,128]{1,0:T(8,128)}, f32[88,128]{1,0:T(8,128)}) custom-call(f32[14,192,128]{2,1,0:T(8,128)S(1)} %get-tuple-element.35.refs_0_, bf16[320,480]{1,0:T(8,128)(2,1)S(1)} %get-tuple-element.36.refs_1_, f32[2,48,128]{2,1,0:T(8,128)S(1)} %get-tuple-element.37.refs_2_, f32[4,24,128]{2,1,0:T(8,128)S(1)} %get-tuple-element.38.refs_3_, ...), custom_call_target="tpu_custom_call" | custom-call | tf_op jit(solution)/shard_map/plate/pallas_call | solution.py:677

commit v9 on v8

--- a/solution.py
+++ b/solution.py
@@ -280,7 +280,9 @@
         def _(dx=dx, dy=dy):
             pl.semaphore_signal(barrier, inc=1, device_id=(gx + dx, gy + dy), device_id_type=MESH)
 
-    loads = [pltpu.make_async_copy(src, dst, load_sem.at[k]) for k, (src, dst) in enumerate(zip(sources, held))]
+    loads = [
+        pltpu.make_async_copy(src, dst.at[0:src.shape[0]], load_sem.at[k]) for k, (src, dst) in enumerate(zip(sources, held))
+    ]
     loads[-1].start()
     for c in loads[:-1]:
         c.start()
@@ -619,7 +621,7 @@
         z2_seam, z2_rows, u1_seam, u1_rows, z1_seam, seam_sums, z1_rows, row_sums,
     ):
         block()
-    copies = [pltpu.make_async_copy(src, dst, out_sem.at[k]) for k, (src, dst) in enumerate(
+    copies = [pltpu.make_async_copy(src.at[0:dst.shape[0]], dst, out_sem.at[k]) for k, (src, dst) in enumerate(
         ((first, first_out), (second, second_out), (sens, sens_out)))]
     copies[0].start()
     copies[1].start()
@@ -637,6 +639,11 @@
     copies[2].start()
     for c in copies:
         c.wait()
+
+
+def roomy(shape):
+    rows, cols = shape
+    return (rows, cols) if cols != 128 else (-(-rows // 64) * 64 if rows > 8 else 16, cols)
 
 
 def local(u_now, u_prev, adjoint_next, adjoint_later, density, step_factor, fixed_nodes, load_top, load_depth, brick_stiffness):
@@ -651,7 +658,7 @@
     bf16 = lambda *shape: jax.ShapeDtypeStruct(shape, BF16)
     passed = (
         [f32(MAIN, PLANES), bf16(OUT, DEPTH), f32(2, FOLD), f32(4, FOLD // 2), f32(2, 2, FOLD // 2), f32(2, GROUP), f32(4, GROUP), f32(2, PLANES)]
-        + [f32(TILES, GROUP)] * 12 + [bf16(MAIN, WIDE, 128)] * 4 + [f32(4, GROUP)] * 4 + [f32(7, OUT)]
+        + [f32(TILES + 1, GROUP)] * 12 + [bf16(MAIN, WIDE, 128)] * 4 + [f32(4, GROUP)] * 4 + [f32(7, OUT)]
     )
     tiles = lambda n, rows, kind: pltpu.VMEM((n, rows, 128), kind)
     gathered = pl.pallas_call(
@@ -659,7 +666,7 @@
         out_shape=passed,
         in_specs=[hbm] * 10,
         out_specs=[vmem] * len(passed),
-        scratch_shapes=[pltpu.VMEM(x.shape, x.dtype) for x in sources] + [
+        scratch_shapes=[pltpu.VMEM(roomy(x.shape), x.dtype) for x in sources] + [
             pltpu.VMEM((2, FOLD, 128), F32),
             pltpu.VMEM((4, FOLD // 2, 128), F32),
             tiles(2, GROUP, F32),
@@ -679,9 +686,9 @@
         out_shape=tuple(jax.ShapeDtypeStruct(shape, F32) for shape in results),
         in_specs=[vmem] * len(passed),
         out_specs=(hbm,) * 3,
-        scratch_shapes=[tiles(TILES, GROUP, F32)] * 13 + [tiles(MAIN, WIDE, BF16)] * 5
+        scratch_shapes=[tiles(TILES + 1, GROUP, F32)] * 13 + [tiles(MAIN, WIDE, BF16)] * 5
         + [pltpu.VMEM((OUT, 128), F32), tiles(2, OUT, F32), tiles(3, GROUP, F32), tiles(2, PLANES, F32), pltpu.VMEM((5, DEPTH, 256), BF16)]
-        + [pltpu.VMEM(shape, F32) for shape in results]
+        + [pltpu.VMEM(roomy(shape), F32) for shape in results]
         + [pltpu.SemaphoreType.DMA((3,))],
         compiler_params=pltpu.CompilerParams(vmem_limit_bytes=40 * 2**20),
         name="plate",

time: 14 us -> 14 us (level)
  no operation moved by 1% of the time
where the time goes in v9:
time: 14 us; the launch traced here: 13.8 us
  Pallas kernels  13.2 us (94%)
  between operations  0.64 us (5%)
    pallas_call x1, Pallas kernels, local(): pl.pallas_call(exchange_kernel, out_shape=passed, in_specs=[hbm] * 10, ou...  9.65 us
    pallas_call x1, Pallas kernels, local(): pl.pallas_call(plate_kernel, out_shape=tuple((jax.ShapeDtypeStruct(shape,...  3.55 us

profile of v9, /device:TPU:56, one launch (start us, length us, event | category | flops | bytes accessed | tf_op | source)
XLA Modules:
  0.0 13.8 jit_solution(15559058534880367786)
XLA Ops:
  0.6 9.7 %exchange.1 = (f32[14,192,128]{2,1,0:T(8,128)S(1)}, bf16[320,480]{1,0:T(8,128)(2,1)S(1)}, f32[2,48,128]{2,1,0:T(8,128)S(1)}, f32[4,24,128]{2,1,0:T(8,128)S(1)}, ...) custom-call(f32[288,128]{1,0:T(8,128)} %bitcast.10, ...), custom_call_target="tpu_custom_call" | custom-call | tf_op jit(solution)/shard_map/exchange/pallas_call | solution.py:664
  10.3 3.5 %plate.1 = (f32[288,128]{1,0:T(8,128)}, f32[288,128]{1,0:T(8,128)}, f32[88,128]{1,0:T(8,128)}) custom-call(f32[14,192,128]{2,1,0:T(8,128)S(1)} %get-tuple-element.35.refs_0_, bf16[320,480]{1,0:T(8,128)(2,1)S(1)} %get-tuple-element.36.refs_1_, f32[2,48,128]{2,1,0:T(8,128)S(1)} %get-tuple-element.37.refs_2_, f32[4,24,128]{2,1,0:T(8,128)S(1)} %get-tuple-element.38.refs_3_, ...), custom_call_target="tpu_custom_call" | custom-call | tf_op jit(solution)/shard_map/plate/pallas_call | solution.py:684
